TPU v7x, 32 devices: a whole 2x2x4 slice. The times are simulated.
32 devices in a mesh: section: 2 (over y), dp: 8 (over z, core), tensor: 2 (over x).
Axes of the slice: x: 2, y: 2, z: 4, core: 2. Of those that a mesh axis runs over, the one named last changes fastest.
Arguments:
- inputs: bfloat16 [32, 1280, 768], P('dp', 'tensor'), may hold values from -6 to 6
- cotangent: bfloat16 [32, 1280, 768], P('dp', 'tensor'), may hold values from -6 to 6
- segment_ids: int32 [32, 1280], P('dp'), may hold values from 0 to 4, never falling along the last dimension, each value on 1 to 512 neighbouring positions
- norm_gains: float32 [2, 2, 768], P('section'), may hold values from 0.25 to 1.75
- norm_biases: float32 [2, 2, 768], P('section'), may hold values from -1.25 to 1.25
- qkv_weight: bfloat16 [2, 3, 768, 768], P('section', None, None, 'tensor'), may hold values from -0.21875 to 0.21875
- qv_bias: float32 [2, 2, 768], P('section'), may hold values from -1.25 to 1.25
- out_weight: bfloat16 [2, 768, 768], P('section', 'tensor'), may hold values from -1.25 to 1.25
- up_weight: bfloat16 [2, 768, 3072], P('section', None, 'tensor'), may hold values from -0.21875 to 0.21875
- up_bias: float32 [2, 3072], P('section'), may hold values from -1.25 to 1.25
- down_weight: bfloat16 [2, 3072, 768], P('section', 'tensor'), may hold values from -0.109375 to 0.109375
- out_biases: float32 [2, 2, 768], P('section'), may hold values from -1.25 to 1.25
Outputs:
- hidden_states: bfloat16 [2, 32, 1280, 768], P('section', 'dp', 'tensor')
- hidden_grads: float32 [2, 32, 1280, 768], P('section', 'dp', 'tensor')
- grad_norm_gains: float32 [2, 2, 768], P('section')
- grad_norm_biases: float32 [2, 2, 768], P('section')
- grad_qkv_weight: float32 [2, 3, 768, 768], P('section', None, None, 'tensor')
- grad_qv_bias: float32 [2, 2, 768], P('section')
- grad_out_weight: float32 [2, 768, 768], P('section', 'tensor')
- grad_up_weight: float32 [2, 768, 3072], P('section', None, 'tensor')
- grad_up_bias: float32 [2, 3072], P('section')
- grad_down_weight: float32 [2, 3072, 768], P('section', 'tensor')
- grad_out_biases: float32 [2, 2, 768], P('section')
Inputs may be any that keep to these rules, and one draw needn't show every extreme that they name: `segment_ids`: in each sequence the image numbers never fall, each image holds 1 to 512 tokens, and one image holds exactly 512.
All inputs are finite; a program needn't handle non-finite values.
Results may differ from a plain program's by a relative error of at most 0.03.
Values may be sent and summed in bfloat16 or wider, within the bound.
A program may use at most 448 MiB of HBM per device.

v0:
```python
import jax
import jax.numpy as jnp
from jax import lax
from jax.sharding import PartitionSpec as P

HEAD_DIM = 48


EPSILON = 1e-05
NEGATIVE = -1e30


def passed_along(block, axis, distance):
    devices = range(lax.axis_size(axis))
    route = [(i - distance, i) for i in devices if i - distance in devices]
    return lax.ppermute(block, axis, route)


def norm_parts(token_rows, gain_row, shift_row):
    centre = token_rows - jnp.mean(token_rows, axis=-1, keepdims=True)
    inverse = lax.rsqrt(jnp.mean(centre * centre, axis=-1, keepdims=True) + EPSILON)
    scaled = centre * inverse
    return (scaled * gain_row + shift_row, scaled, inverse)


def norm_back(gradient, scaled, inverse, gain_row):
    upstream = gradient * gain_row
    return inverse * (
        upstream
        - jnp.mean(upstream, axis=-1, keepdims=True)
        - scaled * jnp.mean(upstream * scaled, axis=-1, keepdims=True)
    )


def gelu_exact(values):
    return jax.nn.gelu(values, approximate=False)


def head_view(matrix, heads_local):
    return matrix.reshape(matrix.shape[0], heads_local, HEAD_DIM)


def join_heads(stacked):
    return stacked.transpose(1, 0, 2).reshape(stacked.shape[1], stacked.shape[0] * stacked.shape[2])


def attend_forward(queries, key_rows, value_rows, segment):
    seq_len = queries.shape[0]
    half_rows = seq_len // 2
    heads_local = queries.shape[1] // HEAD_DIM
    scaling = HEAD_DIM ** (-0.5)
    query_heads = head_view(queries, heads_local)
    key_heads = head_view(key_rows, heads_local)
    value_heads = head_view(value_rows, heads_local)

    def one_item(item):
        head_index = item // 2
        row_start = item % 2 * half_rows
        head_keys = lax.dynamic_index_in_dim(key_heads, head_index, 1, keepdims=False)
        head_values = lax.dynamic_index_in_dim(value_heads, head_index, 1, keepdims=False)
        head_queries = lax.dynamic_index_in_dim(query_heads, head_index, 1, keepdims=False)
        block_queries = lax.dynamic_slice_in_dim(head_queries, row_start, half_rows, 0)
        block_segment = lax.dynamic_slice_in_dim(segment, row_start, half_rows, 0)
        scores = (
            jnp.einsum("qd,kd->qk", block_queries, head_keys, preferred_element_type=jnp.float32)
            * scaling
        )
        scores = jnp.where(block_segment[:, None] == segment[None, :], scores, NEGATIVE)
        row_peak = jnp.max(scores, axis=-1, keepdims=True)
        expanded = jnp.exp(scores - row_peak)
        denominator = jnp.sum(expanded, axis=-1, keepdims=True)
        weights = (expanded / denominator).astype(jnp.bfloat16)
        block_out = jnp.dot(weights, head_values, preferred_element_type=jnp.float32).astype(
            jnp.bfloat16
        )
        return (block_out, row_peak[:, 0] + jnp.log(denominator[:, 0]))

    outputs, log_totals = lax.map(one_item, jnp.arange(2 * heads_local, dtype=jnp.int32))
    mixed_rows = join_heads(outputs.reshape(heads_local, seq_len, HEAD_DIM))
    return (mixed_rows, log_totals.reshape(heads_local, seq_len))


def attend_backward(queries, key_rows, value_rows, mixed_grad, log_totals, segment):
    seq_len = queries.shape[0]
    half_rows = seq_len // 2
    heads_local = queries.shape[1] // HEAD_DIM
    scaling = HEAD_DIM ** (-0.5)
    query_heads = head_view(queries, heads_local)
    key_heads = head_view(key_rows, heads_local)
    value_heads = head_view(value_rows, heads_local)
    grad_heads = head_view(mixed_grad, heads_local)

    def one_head(head_index):
        head_queries = lax.dynamic_index_in_dim(query_heads, head_index, 1, keepdims=False)
        head_keys = lax.dynamic_index_in_dim(key_heads, head_index, 1, keepdims=False)
        head_values = lax.dynamic_index_in_dim(value_heads, head_index, 1, keepdims=False)
        head_grads = lax.dynamic_index_in_dim(grad_heads, head_index, 1, keepdims=False)
        head_totals = lax.dynamic_index_in_dim(log_totals, head_index, 0, keepdims=False)

        def one_block(carry, block_index):
            key_grad, value_grad = carry
            row_start = block_index * half_rows
            block_queries = lax.dynamic_slice_in_dim(head_queries, row_start, half_rows, 0)
            block_grads = lax.dynamic_slice_in_dim(head_grads, row_start, half_rows, 0)
            block_totals = lax.dynamic_slice_in_dim(head_totals, row_start, half_rows, 0)
            block_segment = lax.dynamic_slice_in_dim(segment, row_start, half_rows, 0)
            scores = (
                jnp.einsum(
                    "qd,kd->qk", block_queries, head_keys, preferred_element_type=jnp.float32
                )
                * scaling
            )
            scores = jnp.where(block_segment[:, None] == segment[None, :], scores, NEGATIVE)
            weights = jnp.exp(scores - block_totals[:, None])
            low_weights = weights.astype(jnp.bfloat16)
            block_out = jnp.dot(
                low_weights, head_values, preferred_element_type=jnp.float32
            ).astype(jnp.bfloat16)
            weight_grads = jnp.einsum(
                "qd,kd->qk", block_grads, head_values, preferred_element_type=jnp.float32
            )
            row_terms = jnp.sum(weights * weight_grads, axis=-1, keepdims=True)
            score_grads = (weights * (weight_grads - row_terms)).astype(jnp.bfloat16)
            query_grad = (
                jnp.dot(score_grads, head_keys, preferred_element_type=jnp.float32) * scaling
            )
            key_grad = (
                key_grad
                + jnp.einsum(
                    "qk,qd->kd", score_grads, block_queries, preferred_element_type=jnp.float32
                )
                * scaling
            )
            value_grad = value_grad + jnp.einsum(
                "qk,qd->kd", low_weights, block_grads, preferred_element_type=jnp.float32
            )
            return ((key_grad, value_grad), (block_out, query_grad))

        empty = jnp.zeros((seq_len, HEAD_DIM), jnp.float32)
        (key_grad, value_grad), (block_outs, query_grads) = lax.scan(
            one_block, (empty, empty), jnp.arange(2, dtype=jnp.int32)
        )
        return (
            block_outs.reshape(seq_len, HEAD_DIM),
            query_grads.reshape(seq_len, HEAD_DIM),
            key_grad,
            value_grad,
        )

    results = lax.map(one_head, jnp.arange(heads_local, dtype=jnp.int32))
    return tuple((join_heads(item) for item in results))


def store_at(array, value, which, running):
    return array.at[which].set(jnp.where(running, value, array[which]))


def on_device(
    inputs,
    cotangent,
    segment_ids,
    norm_gains,
    norm_biases,
    qkv_weight,
    qv_bias,
    out_weight,
    up_weight,
    up_bias,
    down_weight,
    out_biases,
):
    section_index = lax.axis_index("section")
    section_count = lax.axis_size("section")
    lane_index = lax.axis_index("tensor")
    micro_count, own_rows, model_width = inputs.shape
    seq_len = segment_ids.shape[1]
    cols_local = qkv_weight.shape[3]
    hidden_local = up_weight.shape[2]
    heads_local = cols_local // HEAD_DIM
    gain_rows = norm_gains[0]
    shift_rows = norm_biases[0]
    joined = jnp.concatenate([qkv_weight[0, 0], qkv_weight[0, 1], qkv_weight[0, 2]], axis=1)
    query_shift = lax.dynamic_slice_in_dim(qv_bias[0, 0], lane_index * cols_local, cols_local)
    value_shift = lax.dynamic_slice_in_dim(qv_bias[0, 1], lane_index * cols_local, cols_local)
    up_shift = lax.dynamic_slice_in_dim(up_bias[0], lane_index * hidden_local, hidden_local)
    out_matrix = out_weight[0]
    up_matrix = up_weight[0]
    down_matrix = down_weight[0]
    mixer_shift = out_biases[0, 0]
    feed_shift = out_biases[0, 1]

    def spread_rows(normed_rows, weight):
        return (
            None,
            jnp.dot(
                lax.all_gather(normed_rows, "tensor", axis=0, tiled=True),
                weight,
                preferred_element_type=jnp.float32,
            ),
        )

    def regather(normed_rows):
        return lax.all_gather(normed_rows, "tensor", axis=0, tiled=True)

    def gather_grads(grad_rows):
        return lax.all_gather(grad_rows.astype(jnp.bfloat16), "tensor", axis=0, tiled=True)

    def branch_sum(left_rows, weight):
        return lax.psum_scatter(
            jnp.dot(left_rows, weight, preferred_element_type=jnp.float32).astype(jnp.bfloat16),
            "tensor",
            scatter_dimension=0,
            tiled=True,
        ).astype(jnp.float32)

    def input_sum(grad_rows, weight):
        return lax.psum_scatter(
            jnp.einsum("sc,dc->sd", grad_rows, weight, preferred_element_type=jnp.float32).astype(
                jnp.bfloat16
            ),
            "tensor",
            scatter_dimension=0,
            tiled=True,
        ).astype(jnp.float32)

    def split_projected(projected):
        queries = (projected[:, :cols_local] + query_shift).astype(jnp.bfloat16)
        key_rows = projected[:, cols_local : 2 * cols_local].astype(jnp.bfloat16)
        value_rows = (projected[:, 2 * cols_local :] + value_shift).astype(jnp.bfloat16)
        return (queries, key_rows, value_rows)

    def layer_backward(block_in, middle, log_totals, segment, out_grad):
        residual = block_in.astype(jnp.float32)
        full_grad = gather_grads(out_grad)
        normed_two, scaled_two, inverse_two = norm_parts(middle, gain_rows[1], shift_rows[1])
        normed_two = normed_two.astype(jnp.bfloat16)
        full_two = regather(normed_two)
        hidden = jnp.dot(full_two, up_matrix, preferred_element_type=jnp.float32) + up_shift
        active, gelu_pullback = jax.vjp(gelu_exact, hidden)
        active = active.astype(jnp.bfloat16)
        down_grad = jnp.einsum("sf,sd->fd", active, full_grad, preferred_element_type=jnp.float32)
        active_grad = jnp.einsum(
            "sd,fd->sf", full_grad, down_matrix, preferred_element_type=jnp.float32
        )
        hidden_grad = gelu_pullback(active_grad)[0]
        up_shift_grad = jnp.sum(hidden_grad, axis=0)
        hidden_low = hidden_grad.astype(jnp.bfloat16)
        up_grad = jnp.einsum("sd,sf->df", full_two, hidden_low, preferred_element_type=jnp.float32)
        normed_grad_two = input_sum(hidden_low, up_matrix)
        feed_shift_grad = jnp.sum(out_grad, axis=0)
        middle_grad = out_grad + norm_back(normed_grad_two, scaled_two, inverse_two, gain_rows[1])
        gain_two = jnp.sum(normed_grad_two * scaled_two, axis=0)
        shift_two = jnp.sum(normed_grad_two, axis=0)
        full_mid_grad = gather_grads(middle_grad)
        normed_one, scaled_one, inverse_one = norm_parts(residual, gain_rows[0], shift_rows[0])
        normed_one = normed_one.astype(jnp.bfloat16)
        full_one = regather(normed_one)
        projected = jnp.dot(full_one, joined, preferred_element_type=jnp.float32)
        queries, key_rows, value_rows = split_projected(projected)
        mixed_grad = jnp.einsum(
            "sd,cd->sc", full_mid_grad, out_matrix, preferred_element_type=jnp.float32
        ).astype(jnp.bfloat16)
        mixed_rows, query_grad, key_grad, value_grad = attend_backward(
            queries, key_rows, value_rows, mixed_grad, log_totals, segment
        )
        out_grad_matrix = jnp.einsum(
            "sc,sd->cd", mixed_rows, full_mid_grad, preferred_element_type=jnp.float32
        )
        mixer_shift_grad = jnp.sum(middle_grad, axis=0)
        qkv_low = jnp.concatenate([query_grad, key_grad, value_grad], axis=1).astype(jnp.bfloat16)
        joined_grad = jnp.einsum("sd,sc->dc", full_one, qkv_low, preferred_element_type=jnp.float32)
        normed_grad_one = input_sum(qkv_low, joined)
        in_grad = middle_grad + norm_back(normed_grad_one, scaled_one, inverse_one, gain_rows[0])
        gain_one = jnp.sum(normed_grad_one * scaled_one, axis=0)
        shift_one = jnp.sum(normed_grad_one, axis=0)
        qv_local = jnp.stack([jnp.sum(query_grad, axis=0), jnp.sum(value_grad, axis=0)])
        qv_full = lax.dynamic_update_slice_in_dim(
            jnp.zeros((2, model_width), jnp.float32), qv_local, lane_index * cols_local, 1
        )
        up_full = lax.dynamic_update_slice_in_dim(
            jnp.zeros((up_bias.shape[1],), jnp.float32), up_shift_grad, lane_index * hidden_local, 0
        )
        weight_terms = (joined_grad, out_grad_matrix, up_grad, down_grad)
        small_terms = (
            jnp.stack([gain_one, gain_two]),
            jnp.stack([shift_one, shift_two]),
            qv_full,
            up_full,
            jnp.stack([mixer_shift_grad, feed_shift_grad]),
        )
        return (in_grad, weight_terms, small_terms)

    ticks = micro_count + section_count - 1
    received = jnp.zeros((own_rows, model_width), jnp.bfloat16)
    saved_in = jnp.zeros_like(inputs)
    saved_mid = jnp.zeros((micro_count, own_rows, model_width), jnp.float32)
    saved_totals = jnp.zeros((micro_count, heads_local, seq_len), jnp.float32)
    states = jnp.zeros_like(inputs)
    for tick in range(ticks):
        micro = tick - section_index
        running = (micro >= 0) & (micro < micro_count)
        which = jnp.clip(micro, 0, micro_count - 1)
        own_in = lax.dynamic_index_in_dim(inputs, which, 0, keepdims=False)
        block_in = jnp.where(section_index == 0, own_in, received)
        segment = lax.dynamic_index_in_dim(segment_ids, which, 0, keepdims=False)
        layer_residual = block_in.astype(jnp.float32)
        layer_normed_one = norm_parts(layer_residual, gain_rows[0], shift_rows[0])[0].astype(
            jnp.bfloat16
        )
        layer_full_one, layer_projected = spread_rows(layer_normed_one, joined)
        layer_queries, layer_key_rows, layer_value_rows = split_projected(layer_projected)
        layer_mixed_rows, layer_log_totals = attend_forward(
            layer_queries, layer_key_rows, layer_value_rows, segment
        )
        layer_middle = layer_residual + branch_sum(layer_mixed_rows, out_matrix) + mixer_shift
        layer_normed_two = norm_parts(layer_middle, gain_rows[1], shift_rows[1])[0].astype(
            jnp.bfloat16
        )
        layer_full_two, layer_hidden = spread_rows(layer_normed_two, up_matrix)
        layer_active = gelu_exact(layer_hidden + up_shift).astype(jnp.bfloat16)
        block_out = layer_middle + branch_sum(layer_active, down_matrix) + feed_shift
        block_out, middle, log_totals, full_one, full_two = (
            block_out,
            layer_middle,
            layer_log_totals,
            layer_full_one,
            layer_full_two,
        )
        handed = block_out.astype(jnp.bfloat16)
        saved_in = store_at(saved_in, block_in, which, running)
        saved_mid = store_at(saved_mid, middle, which, running)
        saved_totals = store_at(saved_totals, log_totals, which, running)
        states = store_at(states, handed, which, running)
        if tick + 1 < ticks:
            received = passed_along(handed, "section", 1)
    back_received = jnp.zeros((own_rows, model_width), jnp.bfloat16)
    weight_totals = (
        jnp.zeros(joined.shape, jnp.float32),
        jnp.zeros(out_matrix.shape, jnp.float32),
        jnp.zeros(up_matrix.shape, jnp.float32),
        jnp.zeros(down_matrix.shape, jnp.float32),
    )
    small_totals = (
        jnp.zeros((2, model_width), jnp.float32),
        jnp.zeros((2, model_width), jnp.float32),
        jnp.zeros((2, model_width), jnp.float32),
        jnp.zeros((up_bias.shape[1],), jnp.float32),
        jnp.zeros((2, model_width), jnp.float32),
    )
    grads_store = jnp.zeros((micro_count, own_rows, model_width), jnp.float32)
    for tick in range(ticks):
        micro = tick - (section_count - 1) + section_index
        running = (micro >= 0) & (micro < micro_count)
        which = jnp.clip(micro, 0, micro_count - 1)
        own_grad = lax.dynamic_index_in_dim(cotangent, which, 0, keepdims=False)
        out_grad = jnp.where(section_index == section_count - 1, own_grad, back_received).astype(
            jnp.float32
        )
        in_grad, weight_terms, small_terms = layer_backward(
            lax.dynamic_index_in_dim(saved_in, which, 0, keepdims=False),
            lax.dynamic_index_in_dim(saved_mid, which, 0, keepdims=False),
            lax.dynamic_index_in_dim(saved_totals, which, 0, keepdims=False),
            lax.dynamic_index_in_dim(segment_ids, which, 0, keepdims=False),
            out_grad,
        )
        joined_term, out_term, up_term, down_term = tuple(
            (jnp.where(running, term, 0.0) for term in weight_terms)
        )
        weight_terms = (joined_term, out_term, up_term, down_term)
        weight_totals = tuple((total + term for total, term in zip(weight_totals, weight_terms)))
        small_totals = tuple(
            (
                total + jnp.where(running, term, 0.0)
                for total, term in zip(small_totals, small_terms)
            )
        )
        grads_store = store_at(grads_store, in_grad, which, running)
        if tick + 1 < ticks:
            back_received = passed_along(in_grad.astype(jnp.bfloat16), "section", -1)
    joined_total, out_total, up_total, down_total = weight_totals
    summed = (
        lax.psum(joined_total.astype(jnp.bfloat16), "dp").astype(jnp.float32),
        lax.psum(out_total.astype(jnp.bfloat16), "dp").astype(jnp.float32),
        lax.psum(up_total.astype(jnp.bfloat16), "dp").astype(jnp.float32),
        lax.psum(down_total.astype(jnp.bfloat16), "dp").astype(jnp.float32),
    )
    gain_total, shift_total, qv_total, up_shift_total, out_shift_total = small_totals
    small_summed = lax.psum(
        (gain_total, shift_total, qv_total, up_shift_total, out_shift_total), ("dp", "tensor")
    )
    qkv_grad = summed[0].reshape(model_width, 3, cols_local).transpose(1, 0, 2)
    return (
        states[None],
        grads_store[None],
        small_summed[0][None],
        small_summed[1][None],
        qkv_grad[None],
        small_summed[2][None],
        summed[1][None],
        summed[2][None],
        small_summed[3][None],
        summed[3][None],
        small_summed[4][None],
    )


def solution(mesh):
    placed = (
        P("dp", "tensor", None),
        P("dp", "tensor", None),
        P("dp", None),
        P("section", None, None),
        P("section", None, None),
        P("section", None, None, "tensor"),
        P("section", None, None),
        P("section", "tensor", None),
        P("section", None, "tensor"),
        P("section", None),
        P("section", "tensor", None),
        P("section", None, None),
    )
    return jax.shard_map(
        on_device,
        mesh=mesh,
        in_specs=placed,
        out_specs=(
            P("section", "dp", "tensor", None),
            P("section", "dp", "tensor", None),
            P("section", None, None),
            P("section", None, None),
            P("section", None, None, "tensor"),
            P("section", None, None),
            P("section", "tensor", None),
            P("section", None, "tensor"),
            P("section", None),
            P("section", "tensor", None),
            P("section", None, None),
        ),
        check_vma=False,
    )
```

profile of v0, /device:TPU:3, one launch (start us, length us, event | category | flops | bytes accessed | tf_op | source)
XLA Modules:
  0.0 4471.8 jit_solution(9982630811487577809)
XLA Ops:
  17.6 28.5 all-gather.32.cloned.1.call-done
  53.1 122.5 %while.265 = (s32[]{:T(128)}, bf16[16,640,48]{1,2,0:T(8,128)(2,1)S(1)}, f32[16,640]{1,0:T(8,128)S(1)}, s32[16]{0:T(128)S(1)}, s32[1280]{0:T(1024)S(1)}, /*index=...) while((s32[]{:T(128)}, ...), condition=%wide.region_6.7_spmd, body=%wide.region_3.6_spmd.sunk | while | flops 164689312 | bytes 10246128 | solution.py:78
  182.1 30.4 reduce-scatter.21.cloned.1.call-done
  219.8 31.5 all-gather.34.cloned.1.call-done
  251.3 24.5 convolution_convert_fusion.23
  276.6 29.7 reduce-scatter.23.cloned.1.call-done
  341.5 34.6 all-gather.36.cloned.1.call-done
  384.3 132.2 %while.266 = (s32[]{:T(128)}, bf16[16,640,48]{1,2,0:T(8,128)(2,1)}, f32[16,640]{1,0:T(8,128)S(1)}, s32[16]{0:T(128)S(1)}, s32[1280]{0:T(1024)S(1)}, /*index=5*/b...) while((s32[]{:T(128)}, bf16[16,640,48]{1,2,0:T(8,128)(2,1)}, ...), condition=%wide.region_17.18_spmd, body=%wide.region_14.17_spmd.sunk | while | flops 164689312 | bytes 10243056 | solution.py:78
  526.0 30.5 reduce-scatter.25.cloned.1.call-done
  561.9 31.4 all-gather.38.cloned.1.call-done
  593.3 24.5 convolution_convert_fusion.21
  620.1 28.3 reduce-scatter.27.cloned.1.call-done
  683.1 33.8 all-gather.40.cloned.1.call-done
  725.0 132.1 %while.267 = (s32[]{:T(128)}, bf16[16,640,48]{1,2,0:T(8,128)(2,1)}, f32[16,640]{1,0:T(8,128)S(1)}, s32[16]{0:T(128)S(1)}, s32[1280]{0:T(1024)S(1)}, /*index=5*/b...) while((s32[]{:T(128)}, bf16[16,640,48]{1,2,0:T(8,128)(2,1)}, ...), condition=%wide.region_28.29_spmd, body=%wide.region_25.28_spmd.sunk | while | flops 164689312 | bytes 10243056 | solution.py:78
  866.6 30.5 reduce-scatter.29.cloned.1.call-done
  902.3 31.5 all-gather.42.cloned.1.call-done
  933.9 24.5 convolution_convert_fusion.19
  960.7 28.3 reduce-scatter.31.cloned.1.call-done
  998.3 19.0 collective-permute-done.2
  1023.7 33.7 all-gather.44.cloned.1.call-done
  1065.6 132.1 %while.268 = (s32[]{:T(128)}, bf16[16,640,48]{1,2,0:T(8,128)(2,1)}, f32[16,640]{1,0:T(8,128)S(1)}, s32[16]{0:T(128)S(1)}, s32[1280]{0:T(1024)S(1)}, /*index=5*/b...) while((s32[]{:T(128)}, bf16[16,640,48]{1,2,0:T(8,128)(2,1)}, ...), condition=%wide.region_39.40_spmd, body=%wide.region_36.39_spmd.sunk | while | flops 164689312 | bytes 10243056 | solution.py:78
  1207.2 30.5 reduce-scatter.33.cloned.1.call-done
  1242.9 31.6 all-gather.46.cloned.1.call-done
  1274.5 24.5 convolution_convert_fusion.17
  1301.3 28.3 reduce-scatter.35.cloned.1.call-done
  1371.2 33.3 all-gather.48.cloned.1.call-done
  1412.6 25.5 all-gather.54.cloned.1.call-done
  1447.7 132.1 %while.269 = (s32[]{:T(128)}, bf16[16,640,48]{1,2,0:T(8,128)(2,1)}, f32[16,640]{1,0:T(8,128)S(1)}, s32[16]{0:T(128)S(1)}, s32[1280]{0:T(1024)S(1)}, /*index=5*/b...) while((s32[]{:T(128)}, bf16[16,640,48]{1,2,0:T(8,128)(2,1)}, ...), condition=%wide.region_50.51_spmd, body=%wide.region_47.50_spmd.sunk | while | flops 164689312 | bytes 10243056 | solution.py:78
  1637.4 28.5 all-gather.52.cloned.1.call-done
  1666.0 21.4 fusion.180
  1722.2 26.0 reduce-scatter.41.cloned.1.call-done
  1766.4 25.5 all-gather.56.cloned.1.call-done
  1799.7 268.1 %while.271 = (s32[]{:T(128)}, bf16[8,1280,48]{1,2,0:T(8,128)(2,1)}, f32[8,1280,48]{1,2,0:T(8,128)}, bf16[8,1280,48]{1,2,0:T(8,128)(2,1)}, f32[8,1280,48]{1,2,0:T...) while((s32[]{:T(128)}, bf16[8,1280,48]{1,2,0:T(8,128)(2,1)}, ...), condition=%wide.region_67.68_spmd, body=%wide.region_63.67_spmd.sunk | while | flops 481238400 | bytes 45324236 | solution.py:150
  2081.4 24.4 reduce-scatter.43.cloned.1.call-done
  2116.1 23.5 collective-permute-done.4
  2147.4 21.4 fusion.181
  2215.4 25.1 all-gather.78.cloned.1.call-done
  2247.4 26.5 reduce-scatter.45.cloned.1.call-done
  2282.7 24.3 all-gather.70.cloned.1.call-done
  2313.6 26.6 all-gather.86.cloned.1.call-done
  2354.2 19.2 all-gather.64.cloned.1.call-done
  2380.9 270.5 %while.273 = (s32[]{:T(128)}, bf16[8,1280,48]{1,2,0:T(8,128)(2,1)}, f32[8,1280,48]{1,2,0:T(8,128)}, bf16[8,1280,48]{1,2,0:T(8,128)(2,1)}, f32[8,1280,48]{1,2,0:T...) while((s32[]{:T(128)}, bf16[8,1280,48]{1,2,0:T(8,128)(2,1)}, ...), condition=%wide.region_83.84_spmd, body=%wide.region_79.83_spmd.sunk | while | flops 481238400 | bytes 45324236 | solution.py:150
  2659.6 29.8 reduce-scatter.47.cloned.1.call-done
  2697.9 23.1 collective-permute-done.5
  2724.1 21.4 fusion.182
  2774.3 30.5 reduce-scatter.49.cloned.1.call-done
  2817.3 28.0 all-gather.72.cloned.1.call-done
  2852.9 268.3 %while.275 = (s32[]{:T(128)}, bf16[8,1280,48]{1,2,0:T(8,128)(2,1)}, f32[8,1280,48]{1,2,0:T(8,128)}, bf16[8,1280,48]{1,2,0:T(8,128)(2,1)}, f32[8,1280,48]{1,2,0:T...) while((s32[]{:T(128)}, bf16[8,1280,48]{1,2,0:T(8,128)(2,1)}, ...), condition=%wide.region_99.100_spmd, body=%wide.region_95.99_spmd.sunk | while | flops 481238400 | bytes 45324236 | solution.py:150
  3129.2 29.9 reduce-scatter.51.cloned.1.call-done
  3167.3 23.5 collective-permute-done.6
  3194.2 21.4 fusion.183
  3243.3 30.5 reduce-scatter.53.cloned.1.call-done
  3286.6 27.8 all-gather.80.cloned.1.call-done
  3322.0 269.8 %while.277 = (s32[]{:T(128)}, bf16[8,1280,48]{1,2,0:T(8,128)(2,1)}, f32[8,1280,48]{1,2,0:T(8,128)}, bf16[8,1280,48]{1,2,0:T(8,128)(2,1)}, f32[8,1280,48]{1,2,0:T...) while((s32[]{:T(128)}, bf16[8,1280,48]{1,2,0:T(8,128)(2,1)}, ...), condition=%wide.region_115.116_spmd, body=%wide.region_111.115_spmd.sunk | while | flops 481238400 | bytes 45324236 | solution.py:150
  3600.0 29.7 reduce-scatter.55.cloned.1.call-done
  3637.9 23.5 collective-permute-done.7
  3664.7 21.4 fusion.184
  3714.6 29.9 reduce-scatter.57.cloned.1.call-done
  3753.5 24.0 all-gather.50.cloned.1.call-done
  3777.5 24.5 convolution_convert_fusion.15
  3923.2 272.6 %while.279 = (s32[]{:T(128)}, bf16[8,1280,48]{1,2,0:T(8,128)(2,1)}, f32[8,1280,48]{1,2,0:T(8,128)}, bf16[8,1280,48]{1,2,0:T(8,128)(2,1)}, f32[8,1280,48]{1,2,0:T...) while((s32[]{:T(128)}, bf16[8,1280,48]{1,2,0:T(8,128)(2,1)}, ...), condition=%wide.region_131.132_spmd, body=%wide.region_127.131_spmd.sunk | while | flops 481238400 | bytes 45324236 | solution.py:150
  4278.0 91.6 %all-reduce.4.cloned.1.call-done = (bf16[1,3,768,384]{2,3,1,0:T(8,128)(2,1)}, bf16[1,384,768]{2,1,0:T(8,128)(2,1)}, bf16[1,768,1536]{2,1,0:T(8,128)(2,1)}, bf16[1,1536,768]{2,1,0:T(8,128)(2,1)}) async-done(((bf16[1,3,768,384]{2,3,1,0:T(8,128)(2,1)}, bf16[1,384,768]{2,1,0:T(8,128)(2,1)}, bf16[1,768,1536]{2,1,0:T(8,128)(2,1)}, bf16[1,1536,768]{2,1,0:T(8,128)(2,1)}), (bf16[1,3,768,384]{2,3,1,0:T(8,128)(2,1)}, ...) | async-done | bytes 7077904 | tf_op jit(solution)/shard_map/psum | solution.py:382
  4383.0 18.4 reduce-scatter.59.cloned.1.call-done
  4404.1 55.3 %all-reduce = (f32[1,2,768]{2,1,0:T(2,128)}, f32[1,2,768]{2,1,0:T(2,128)}, f32[1,2,768]{2,1,0:T(2,128)}, f32[1,3072]{1,0:T(1,128)}, f32[1,2,768]{2,1,0:T(2,128)}) all-reduce(f32[1,2,768]{2,1,0:T(2,128)S(1)} %fusion.563, f32[1,2,768]{2,1,0:T(2,128)S(1)} %fusion.562, ...), channel_id=1, replica_groups=mesh['section'=2,'dp'=8,'tensor'=2] {'dp','tensor'}, use_global_device_ids=true, to_apply=%region_145.146 | all-reduce | flops 9216 | bytes 73728 | tf_op jit(solution)/shard_map/psum | solution.py:388
  (5058 shorter events, 3241.3 us)
Async XLA Ops:
  7.2 38.8 all-gather.32.cloned.1.call-start
  11.4 1620.7 %copy-start.195 = (f32[768]{0:T(1024)}, f32[768]{0:T(1024)S(1)}, u32[]{:S(2)}) copy-start(f32[768]{0:T(1024)S(1)} %get-tuple-element.2109) | copy-start | bytes 9220
  11.4 1743.3 %copy-start.137 = (f32[768]{0:T(1024)}, f32[768]{0:T(1024)S(1)}, u32[]{:S(2)}) copy-start(f32[768]{0:T(1024)S(1)} %get-tuple-element.2604) | copy-start | bytes 9220
  14.0 198.5 %reduce-scatter.21.cloned.1.call-start = ((), (), s32[]{:S(2)}) async-start(), calls=%async_computation.21 | async-start | bytes 2949120 | tf_op jit(solution)/shard_map/reduce_scatter | solution.py:209
  14.2 1428.7 %copy-start.230 = (f32[384]{0:T(512)}, f32[384]{0:T(512)S(1)}, u32[]{:S(2)}) copy-start(f32[384]{0:T(512)S(1)} %get-tuple-element.2605) | copy-start | bytes 4612
  182.0 69.3 %all-gather.34.cloned.1.call-start = ((), (), s32[]{:S(2)}) async-start(), calls=%async_computation.22 | async-start | bytes 2949120 | tf_op jit(solution)/shard_map/all_gather | solution.py:196
  182.1 1450.1 %copy-start.125 = (f32[768]{0:T(1024)}, f32[768]{0:T(1024)S(1)}, u32[]{:S(2)}) copy-start(f32[768]{0:T(1024)S(1)} %get-tuple-element.2106) | copy-start | bytes 9220
  219.5 86.9 %reduce-scatter.23.cloned.1.call-start = ((), (), s32[]{:S(2)}) async-start(), calls=%async_computation.23 | async-start | bytes 2949120 | tf_op jit(solution)/shard_map/reduce_scatter | solution.py:209
  219.7 1446.2 %copy-start.299 = (f32[1536]{0:T(1024)}, f32[1536]{0:T(1024)S(1)}, u32[]{:S(2)}) copy-start(f32[1536]{0:T(1024)S(1)} %fusion.548) | copy-start | bytes 18436
  275.8 100.4 %all-gather.36.cloned.1.call-start = ((), (), s32[]{:S(2)}) async-start(), calls=%async_computation.24 | async-start | bytes 2949120 | tf_op jit(solution)/shard_map/all_gather | solution.py:196
  312.5 23.9 collective-permute-start
  341.5 215.0 %reduce-scatter.25.cloned.1.call-start = ((), (), s32[]{:S(2)}) async-start(), calls=%async_computation.25 | async-start | bytes 2949120 | tf_op jit(solution)/shard_map/reduce_scatter | solution.py:209
  526.0 67.3 %all-gather.38.cloned.1.call-start = ((), (), s32[]{:S(2)}) async-start(), calls=%async_computation.26 | async-start | bytes 2949120 | tf_op jit(solution)/shard_map/all_gather | solution.py:196
  561.5 86.9 %reduce-scatter.27.cloned.1.call-start = ((), (), s32[]{:S(2)}) async-start(), calls=%async_computation.27 | async-start | bytes 2949120 | tf_op jit(solution)/shard_map/reduce_scatter | solution.py:209
  617.8 99.0 %all-gather.40.cloned.1.call-start = ((), (), s32[]{:S(2)}) async-start(), calls=%async_computation.28 | async-start | bytes 2949120 | tf_op jit(solution)/shard_map/all_gather | solution.py:196
  652.8 23.8 collective-permute-start.1
  683.0 214.1 %reduce-scatter.29.cloned.1.call-start = ((), (), s32[]{:S(2)}) async-start(), calls=%async_computation.29 | async-start | bytes 2949120 | tf_op jit(solution)/shard_map/reduce_scatter | solution.py:209
  866.5 67.3 %all-gather.42.cloned.1.call-start = ((), (), s32[]{:S(2)}) async-start(), calls=%async_computation.30 | async-start | bytes 2949120 | tf_op jit(solution)/shard_map/all_gather | solution.py:196
  902.1 86.9 %reduce-scatter.31.cloned.1.call-start = ((), (), s32[]{:S(2)}) async-start(), calls=%async_computation.31 | async-start | bytes 2949120 | tf_op jit(solution)/shard_map/reduce_scatter | solution.py:209
  958.4 99.0 %all-gather.44.cloned.1.call-start = ((), (), s32[]{:S(2)}) async-start(), calls=%async_computation.32 | async-start | bytes 2949120 | tf_op jit(solution)/shard_map/all_gather | solution.py:196
  993.5 23.8 collective-permute-start.2
  1023.6 214.0 %reduce-scatter.33.cloned.1.call-start = ((), (), s32[]{:S(2)}) async-start(), calls=%async_computation.33 | async-start | bytes 2949120 | tf_op jit(solution)/shard_map/reduce_scatter | solution.py:209
  1207.1 67.3 %all-gather.46.cloned.1.call-start = ((), (), s32[]{:S(2)}) async-start(), calls=%async_computation.34 | async-start | bytes 2949120 | tf_op jit(solution)/shard_map/all_gather | solution.py:196
  1242.7 86.9 %reduce-scatter.35.cloned.1.call-start = ((), (), s32[]{:S(2)}) async-start(), calls=%async_computation.35 | async-start | bytes 2949120 | tf_op jit(solution)/shard_map/reduce_scatter | solution.py:209
  1299.0 105.5 %all-gather.48.cloned.1.call-start = ((), (), s32[]{:S(2)}) async-start(), calls=%async_computation.36 | async-start | bytes 2949120 | tf_op jit(solution)/shard_map/all_gather | solution.py:196
  1334.1 23.9 collective-permute-start.3
  1370.5 67.6 %all-gather.54.cloned.1.call-start = ((), (), s32[]{:S(2)}) async-start(), calls=%async_computation.42 | async-start | bytes 2949120 | tf_op jit(solution)/shard_map/all_gather | solution.py:203
  1371.1 248.7 %reduce-scatter.37.cloned.1.call-start = ((), (), s32[]{:S(2)}) async-start(), calls=%async_computation.37 | async-start | bytes 2949120 | tf_op jit(solution)/shard_map/reduce_scatter | solution.py:209
  1589.3 76.7 %all-gather.52.cloned.1.call-start = ((), (), s32[]{:S(2)}) async-start(), calls=%async_computation.40 | async-start | bytes 2949120 | tf_op jit(solution)/shard_map/all_gather | solution.py:203
  1634.2 65.7 %all-gather.90.cloned.1.call-start = ((), (), s32[]{:S(2)}) async-start(), calls=%async_computation.69 | async-start | bytes 2949120 | tf_op jit(solution)/shard_map/all_gather | solution.py:206
  1637.2 110.9 %reduce-scatter.41.cloned.1.call-start = ((), (), s32[]{:S(2)}) async-start(), calls=%async_computation.41 | async-start | bytes 2949120 | tf_op jit(solution)/shard_map/reduce_scatter | solution.py:217
  1717.6 74.2 %all-gather.56.cloned.1.call-start = ((), (), s32[]{:S(2)}) async-start(), calls=%async_computation.43 | async-start | bytes 2949120 | tf_op jit(solution)/shard_map/all_gather | solution.py:206
  1760.0 345.8 %reduce-scatter.43.cloned.1.call-start = ((), (), s32[]{:S(2)}) async-start(), calls=%async_computation.44 | async-start | bytes 2949120 | tf_op jit(solution)/shard_map/reduce_scatter | solution.py:217
  2075.3 72.0 %all-gather.58.cloned.1.call-start = ((), (), s32[]{:S(2)}) async-start(), calls=%async_computation.45 | async-start | bytes 2949120 | tf_op jit(solution)/shard_map/all_gather | solution.py:203
  2081.0 93.1 %all-gather.60.cloned.1.call-start = ((), (), s32[]{:S(2)}) async-start(), calls=%async_computation.46 | async-start | bytes 2949120 | tf_op jit(solution)/shard_map/all_gather | solution.py:206
  2114.6 24.9 collective-permute-start.4
  2142.6 64.6 %all-gather.62.cloned.1.call-start = ((), (), s32[]{:S(2)}) async-start(), calls=%async_computation.48 | async-start | bytes 2949120 | tf_op jit(solution)/shard_map/all_gather | solution.py:203
  2147.3 93.2 %all-gather.78.cloned.1.call-start = ((), (), s32[]{:S(2)}) async-start(), calls=%async_computation.60 | async-start | bytes 2949120 | tf_op jit(solution)/shard_map/all_gather | solution.py:203
  2168.8 105.1 %reduce-scatter.45.cloned.1.call-start = ((), (), s32[]{:S(2)}) async-start(), calls=%async_computation.47 | async-start | bytes 2949120 | tf_op jit(solution)/shard_map/reduce_scatter | solution.py:217
  2191.8 115.1 %all-gather.70.cloned.1.call-start = ((), (), s32[]{:S(2)}) async-start(), calls=%async_computation.54 | async-start | bytes 2949120 | tf_op jit(solution)/shard_map/all_gather | solution.py:203
  2192.4 147.8 %all-gather.86.cloned.1.call-start = ((), (), s32[]{:S(2)}) async-start(), calls=%async_computation.66 | async-start | bytes 2949120 | tf_op jit(solution)/shard_map/all_gather | solution.py:203
  2194.0 179.4 %all-gather.64.cloned.1.call-start = ((), (), s32[]{:S(2)}) async-start(), calls=%async_computation.49 | async-start | bytes 2949120 | tf_op jit(solution)/shard_map/all_gather | solution.py:206
  2282.6 406.7 %reduce-scatter.47.cloned.1.call-start = ((), (), s32[]{:S(2)}) async-start(), calls=%async_computation.50 | async-start | bytes 2949120 | tf_op jit(solution)/shard_map/reduce_scatter | solution.py:217
  2658.8 65.3 %all-gather.66.cloned.1.call-start = ((), (), s32[]{:S(2)}) async-start(), calls=%async_computation.51 | async-start | bytes 2949120 | tf_op jit(solution)/shard_map/all_gather | solution.py:203
  2659.5 97.0 %all-gather.68.cloned.1.call-start = ((), (), s32[]{:S(2)}) async-start(), calls=%async_computation.52 | async-start | bytes 2949120 | tf_op jit(solution)/shard_map/all_gather | solution.py:206
  2696.1 24.9 collective-permute-start.5
  2724.0 80.7 %reduce-scatter.49.cloned.1.call-start = ((), (), s32[]{:S(2)}) async-start(), calls=%async_computation.53 | async-start | bytes 2949120 | tf_op jit(solution)/shard_map/reduce_scatter | solution.py:217
  2774.2 71.1 %all-gather.72.cloned.1.call-start = ((), (), s32[]{:S(2)}) async-start(), calls=%async_computation.55 | async-start | bytes 2949120 | tf_op jit(solution)/shard_map/all_gather | solution.py:206
  2813.5 345.6 %reduce-scatter.51.cloned.1.call-start = ((), (), s32[]{:S(2)}) async-start(), calls=%async_computation.56 | async-start | bytes 2949120 | tf_op jit(solution)/shard_map/reduce_scatter | solution.py:217
  3128.6 65.6 %all-gather.74.cloned.1.call-start = ((), (), s32[]{:S(2)}) async-start(), calls=%async_computation.57 | async-start | bytes 2949120 | tf_op jit(solution)/shard_map/all_gather | solution.py:203
  3129.2 96.4 %all-gather.76.cloned.1.call-start = ((), (), s32[]{:S(2)}) async-start(), calls=%async_computation.58 | async-start | bytes 2949120 | tf_op jit(solution)/shard_map/all_gather | solution.py:206
  3165.9 24.9 collective-permute-start.6
  3193.9 80.0 %reduce-scatter.53.cloned.1.call-start = ((), (), s32[]{:S(2)}) async-start(), calls=%async_computation.59 | async-start | bytes 2949120 | tf_op jit(solution)/shard_map/reduce_scatter | solution.py:217
  3243.3 71.1 %all-gather.80.cloned.1.call-start = ((), (), s32[]{:S(2)}) async-start(), calls=%async_computation.61 | async-start | bytes 2949120 | tf_op jit(solution)/shard_map/all_gather | solution.py:206
  3282.6 347.1 %reduce-scatter.55.cloned.1.call-start = ((), (), s32[]{:S(2)}) async-start(), calls=%async_computation.62 | async-start | bytes 2949120 | tf_op jit(solution)/shard_map/reduce_scatter | solution.py:217
  3599.2 65.5 %all-gather.82.cloned.1.call-start = ((), (), s32[]{:S(2)}) async-start(), calls=%async_computation.63 | async-start | bytes 2949120 | tf_op jit(solution)/shard_map/all_gather | solution.py:203
  3599.9 96.3 %all-gather.84.cloned.1.call-start = ((), (), s32[]{:S(2)}) async-start(), calls=%async_computation.64 | async-start | bytes 2949120 | tf_op jit(solution)/shard_map/all_gather | solution.py:206
  3636.5 24.9 collective-permute-start.7
  3664.4 80.0 %reduce-scatter.57.cloned.1.call-start = ((), (), s32[]{:S(2)}) async-start(), calls=%async_computation.65 | async-start | bytes 2949120 | tf_op jit(solution)/shard_map/reduce_scatter | solution.py:217
  3713.9 63.6 %all-gather.50.cloned.1.call-start = ((), (), s32[]{:S(2)}) async-start(), calls=%async_computation.38 | async-start | bytes 2949120 | tf_op jit(solution)/shard_map/all_gather | solution.py:196
  3714.5 201.3 %all-gather.88.cloned.1.call-start = ((), (), s32[]{:S(2)}) async-start(), calls=%async_computation.67 | async-start | bytes 2949120 | tf_op jit(solution)/shard_map/all_gather | solution.py:206
  3753.2 468.3 %reduce-scatter.39.cloned.1.call-start = ((), (), s32[]{:S(2)}) async-start(), calls=%async_computation.39 | async-start | bytes 2949120 | tf_op jit(solution)/shard_map/reduce_scatter | solution.py:209
  3802.0 567.6 %all-reduce.4.cloned.1.call-start = ((), (), s32[]{:S(2)}) async-start(), calls=%async_computation.70 | async-start | bytes 14155776 | tf_op jit(solution)/shard_map/psum | solution.py:382
  4215.4 186.0 %reduce-scatter.59.cloned.1.call-start = ((), (), s32[]{:S(2)}) async-start(), calls=%async_computation.68 | async-start | bytes 2949120 | tf_op jit(solution)/shard_map/reduce_scatter | solution.py:217
  (1081 other events, 10213.6 us)
Sparse Core Ops, SparseCore 0:
  14.1 31.8 all-gather.31
  182.1 30.3 reduce-scatter.20
  219.6 31.6 all-gather.33
  275.9 30.3 reduce-scatter.22
  341.6 34.5 all-gather.35
  526.1 30.3 reduce-scatter.24
  561.6 31.6 all-gather.37
  617.9 30.3 reduce-scatter.26
  683.1 33.6 all-gather.39
  866.7 30.3 reduce-scatter.28
  902.2 31.6 all-gather.41
  958.5 30.3 reduce-scatter.30
  1023.8 33.6 all-gather.43
  1207.3 30.3 reduce-scatter.32
  1242.8 31.6 all-gather.45
  1299.1 30.3 reduce-scatter.34
  1370.7 33.7 all-gather.47
  1406.4 31.6 all-gather.53
  1589.4 30.3 reduce-scatter.36
  1634.3 31.6 all-gather.51
  1668.2 31.6 all-gather.89
  1717.7 30.3 reduce-scatter.40
  1760.2 31.6 all-gather.55
  2075.4 30.3 reduce-scatter.42
  2108.1 31.6 all-gather.57
  2142.7 31.2 all-gather.59
  2175.6 31.6 all-gather.61
  2208.9 31.6 all-gather.77
  2243.4 30.3 reduce-scatter.44
  2275.3 31.6 all-gather.69
  2308.5 31.6 all-gather.85
  2341.7 31.6 all-gather.63
  2658.9 30.3 reduce-scatter.46
  2690.9 31.6 all-gather.65
  2724.8 31.6 all-gather.67
  2774.3 30.3 reduce-scatter.48
  2813.6 31.6 all-gather.71
  3128.7 30.3 reduce-scatter.50
  3160.6 31.6 all-gather.73
  3194.0 31.5 all-gather.75
  3243.4 30.3 reduce-scatter.52
  3282.7 31.6 all-gather.79
  3599.3 30.3 reduce-scatter.54
  3631.3 31.6 all-gather.81
  3664.6 31.5 all-gather.83
  3714.0 30.3 reduce-scatter.56
  3745.8 31.6 all-gather.49
  3778.9 31.6 all-gather.87
  3812.7 30.3 reduce-scatter.38
  4215.5 154.0 all-reduce.3
  4371.8 29.5 reduce-scatter.58
where the time goes:
time: 4520 us; the launch traced here: 4470 us
  waiting for transfers between devices  1390 us (31%)
  matrix products  1260 us (28%)
  local copies, waits for them, and re-layouts  1020 us (23%)
  loops' own time  348 us (8%)
  other arithmetic  346 us (8%)
  blocking collectives  55.3 us (1%)
    all_gather x10, waiting for transfers between devices, spread_rows(): lax.all_gather(normed_rows, 'tensor', axis=0, tiled=True)  314 us
    reduce_scatter x10, waiting for transfers between devices, input_sum(): lax.psum_scatter(jnp.einsum('sc,dc->sd', grad_rows, weight, preferred_ele...  276 us
    reduce_scatter x10, waiting for transfers between devices, branch_sum(): lax.psum_scatter(jnp.dot(left_rows, weight, preferred_element_type=jnp.fl...  252 us
    dynamic_update_slice x200, local copies, waits for them, and re-layouts, attend_backward(): results = lax.map(one_head, jnp.arange(heads_local, dtype=jnp.int32))  229 us
    another operation x5, loops' own time, attend_forward(): lax.map(one_item, jnp.arange(2 * heads_local, dtype=jnp.int32))  213 us
    dot_general x80, matrix products, one_item(): jnp.dot(weights, head_values, preferred_element_type=jnp.float32)  178 us
    ppermute x8, waiting for transfers between devices, passed_along(): return lax.ppermute(block, axis, route)  163 us
    dot_general x80, matrix products, one_item(): jnp.einsum('qd,kd->qk', block_queries, head_keys, preferred_element_type=...  150 us

commit v1 on v0

--- a/solution.py
+++ b/solution.py
@@ -1,13 +1,968 @@
+import functools
+import math
+
 import jax
 import jax.numpy as jnp
 from jax import lax
+from jax.experimental import pallas as pl
+from jax.experimental.pallas import tpu as pltpu
 from jax.sharding import PartitionSpec as P
 
 HEAD_DIM = 48
-
-
+IMAGE_IDS = 5
+IMAGE_MOST = 512
 EPSILON = 1e-05
 NEGATIVE = -1e30
+TILE = 128
+EXTRA = 16
+LOG2E = math.log2(math.e)
+SCALING = HEAD_DIM ** (-0.5)
+AXES = ("section", "dp", "tensor")
+VMEM_LIMIT = 56 * 1024 * 1024
+HALF_ERF = (0.127414796, -0.142248368, 0.7107068705, -0.7265760135, 0.5307027145)
+ERF_RATE = 0.3275911 * math.sqrt(0.5)
+F32 = jnp.float32
+BF16 = jnp.bfloat16
+
+
+def nn(left, right):
+    return lax.dot_general(left, right, (((1,), (0,)), ((), ())), preferred_element_type=F32)
+
+
+def nt(left, right):
+    return lax.dot_general(left, right, (((1,), (1,)), ((), ())), preferred_element_type=F32)
+
+
+def tn(left, right):
+    return lax.dot_general(left, right, (((0,), (0,)), ((), ())), preferred_element_type=F32)
+
+
+def normalise(rows):
+    centre = rows - jnp.mean(rows, axis=-1, keepdims=True)
+    inverse = lax.rsqrt(jnp.mean(centre * centre, axis=-1, keepdims=True) + EPSILON)
+    return centre * inverse, inverse
+
+
+def normalise_back(gradient, scaled, inverse, gain):
+    upstream = gradient * gain
+    return inverse * (
+        upstream
+        - jnp.mean(upstream, axis=-1, keepdims=True)
+        - scaled * jnp.mean(upstream * scaled, axis=-1, keepdims=True)
+    )
+
+
+def gelu_pair(values):
+    bell = jnp.exp2(values * values * (-0.5 * LOG2E))
+    step = 1.0 / (1.0 + ERF_RATE * jnp.abs(values))
+    poly = HALF_ERF[4]
+    for term in HALF_ERF[3::-1]:
+        poly = poly * step + term
+    tail = poly * step * bell
+    share = jnp.where(values >= 0, 1.0 - tail, tail)
+    return values * share, share + values * bell * (1.0 / math.sqrt(2 * math.pi))
+
+
+def extra_rows(rows, width):
+    at = lax.broadcasted_iota(jnp.int32, (EXTRA, width), 0)
+    out = jnp.zeros((EXTRA, width), F32)
+    for index, row in enumerate(rows):
+        out = jnp.where(at == index, row, out)
+    return out.astype(BF16)
+
+
+def three_parts(row):
+    first = row.astype(BF16).astype(F32)
+    second = (row - first).astype(BF16).astype(F32)
+    return [first, second, row - first - second]
+
+
+def each_image(start_ref, tiles_ref, body):
+    most = IMAGE_MOST // TILE + 1
+
+    def image(index, carry):
+        first = start_ref[index]
+        tiles = tiles_ref[index]
+        for count in range(1, most + 1):
+
+            @pl.when(tiles == count)
+            def _():
+                body(index, pl.multiple_of(first * TILE, TILE), count * TILE)
+
+        return carry
+
+    lax.fori_loop(0, IMAGE_IDS, image, 0)
+
+
+def piece_copies(refs, sems, targets):
+    low_ref, high_ref = refs
+    half = low_ref.shape[0]
+    copies = []
+    for slot, (first, count, target) in enumerate(targets):
+        source = low_ref.at[first : first + count] if first < half else high_ref.at[first - half : first - half + count]
+        copies.append(pltpu.make_async_copy(source, target, sems.at[slot]))
+    return copies
+
+
+def start_pieces(sel, own, other, copies_of):
+    for index in range(len(own)):
+
+        @pl.when(sel == 0)
+        def _():
+            for copy in copies_of(index, own[index]):
+                copy.start()
+
+        @pl.when(sel != 0)
+        def _():
+            for copy in copies_of(index, other[index]):
+                copy.start()
+
+
+def attend_forward_image(index, at, width, heads, seg_ref, qkv_ref, store):
+    win = pl.ds(at, width)
+    mine = seg_ref[:, win] == index
+    mask = jnp.where(mine, 0.0, NEGATIVE)
+    one = jnp.ones((1, width), F32)
+    query_extra = extra_rows([mask, one], width)
+    key_extra = extra_rows([one, mask], width)
+    value_extra = extra_rows([one], width)
+    cols = heads * HEAD_DIM
+
+    def head(which, carry):
+        low = pl.multiple_of(which * HEAD_DIM, EXTRA)
+        queries = jnp.concatenate([qkv_ref[0, pl.ds(low, HEAD_DIM), win], query_extra], axis=0)
+        keys = jnp.concatenate([qkv_ref[0, pl.ds(cols + low, HEAD_DIM), win], key_extra], axis=0)
+        values = jnp.concatenate([qkv_ref[0, pl.ds(2 * cols + low, HEAD_DIM), win], value_extra], axis=0)
+        scores = tn(keys, queries)
+        peak = jnp.max(scores, axis=0, keepdims=True)
+        weights = jnp.exp2(scores - peak).astype(BF16)
+        mixed = nn(values, weights)
+        total = mixed[HEAD_DIM : HEAD_DIM + 1]
+        store(which, low, win, mine, mixed[:HEAD_DIM] * (1.0 / total), peak + jnp.log2(total))
+        return carry
+
+    lax.fori_loop(0, heads, head, 0, unroll=True)
+
+
+def mixer_forward_kernel(
+    sel_ref, start_ref, tiles_ref, seg_ref, hidden_ref, norm_ref, qkv_shift_ref, out_shift_ref, *rest, pieces, heads
+):
+    own = [rest[2 * i : 2 * i + 2] for i in range(pieces)]
+    other = [rest[2 * pieces + 2 * i : 2 * pieces + 2 * i + 2] for i in range(pieces)]
+    qkv_ref, mixed_ref, total_ref, middle_ref, weight, out_weight, normed, mixed_all, sems = rest[4 * pieces :]
+    step = pl.program_id(0)
+    sel = sel_ref[0]
+    cols = heads * HEAD_DIM
+    rows_all = hidden_ref.shape[0]
+    block = 256
+    half = own[0][0].shape[0]
+
+    def copies_of(index, refs):
+        return piece_copies(
+            refs,
+            sems.at[index],
+            [
+                (0, half, weight.at[index, 0:half]),
+                (half, 3 * cols - half, weight.at[index, half : 3 * cols]),
+                (3 * cols, cols, out_weight.at[index * cols : (index + 1) * cols]),
+            ],
+        )
+
+    @pl.when(step == 0)
+    def _():
+        start_pieces(sel, own, other, copies_of)
+
+        def norm_block(i, carry):
+            rows = pl.ds(pl.multiple_of(i * block, block), block)
+            scaled, _ = normalise(hidden_ref[rows, :].astype(F32))
+            normed[rows, :] = (scaled * norm_ref[0:1, :] + norm_ref[1:2, :]).astype(BF16)
+            return carry
+
+        lax.fori_loop(0, rows_all // block, norm_block, 0)
+
+    for index in range(pieces):
+
+        @pl.when(step == index)
+        def _():
+            for copy in copies_of(index, own[index]):
+                copy.wait()
+
+    def project(i, carry):
+        win = pl.ds(pl.multiple_of(i * block, block), block)
+        projected = nt(weight[step], normed[win, :]) + qkv_shift_ref[0]
+        qkv_ref[0, 0:cols, win] = (projected[0:cols] * (SCALING * LOG2E)).astype(BF16)
+        qkv_ref[0, cols : 3 * cols, win] = projected[cols : 3 * cols].astype(BF16)
+        return carry
+
+    lax.fori_loop(0, rows_all // block, project, 0)
+
+    def store(which, low, win, mine, mixed, total):
+        rows = pl.ds(low, HEAD_DIM)
+        old = mixed_ref[0, rows, win].astype(F32)
+        mixed_ref[0, rows, win] = jnp.where(mine, mixed, old).astype(BF16)
+        total_ref[which, :, win] = jnp.where(mine, total, total_ref[which, :, win])
+
+    each_image(
+        start_ref,
+        tiles_ref,
+        lambda index, at, width: attend_forward_image(index, at, width, heads, seg_ref, qkv_ref, store),
+    )
+    mixed_all[pl.ds(pl.multiple_of(step * cols, cols), cols), :] = mixed_ref[0]
+
+    @pl.when(step == pieces - 1)
+    def _():
+        def finish(i, carry):
+            rows = pl.ds(pl.multiple_of(i * block, block), block)
+            branch = tn(mixed_all[:, rows], out_weight[...])
+            middle_ref[rows, :] = hidden_ref[rows, :].astype(F32) + branch + out_shift_ref[...]
+            return carry
+
+        lax.fori_loop(0, rows_all // block, finish, 0)
+
+
+def once(shape):
+    zeros = (0,) * len(shape)
+    return pl.BlockSpec(shape, lambda *_: zeros, pipeline_mode=pl.Buffered(1))
+
+
+def anywhere(count):
+    return [pl.BlockSpec(memory_space=pl.ANY)] * count
+
+
+def flat(pieces):
+    return [half for piece in pieces for half in piece]
+
+
+def mixer_forward(sel, images, hidden, norm, qkv_shift, out_shift, own, other):
+    rows, width = hidden.shape
+    pieces = len(own)
+    heads = width // HEAD_DIM // pieces
+    cols = heads * HEAD_DIM
+    start, tiles, segment = images
+    return pl.pallas_call(
+        functools.partial(mixer_forward_kernel, pieces=pieces, heads=heads),
+        grid_spec=pltpu.PrefetchScalarGridSpec(
+            num_scalar_prefetch=3,
+            grid=(pieces,),
+            in_specs=[
+                once((1, rows)),
+                once((rows, width)),
+                once((2, width)),
+                pl.BlockSpec((1, 3 * cols, 1), lambda i, *_: (i, 0, 0)),
+                once((1, width)),
+            ]
+            + anywhere(4 * pieces),
+            out_specs=[
+                pl.BlockSpec((1, 3 * cols, rows), lambda i, *_: (i, 0, 0)),
+                pl.BlockSpec((1, cols, rows), lambda i, *_: (i, 0, 0)),
+                pl.BlockSpec((heads, 1, rows), lambda i, *_: (i, 0, 0)),
+                once((rows, width)),
+            ],
+            scratch_shapes=[
+                pltpu.VMEM((pieces, 3 * cols, width), BF16),
+                pltpu.VMEM((width, width), BF16),
+                pltpu.VMEM((rows, width), BF16),
+                pltpu.VMEM((width, rows), BF16),
+                pltpu.SemaphoreType.DMA((pieces, 3)),
+            ],
+        ),
+        out_shape=[
+            jax.ShapeDtypeStruct((pieces, 3 * cols, rows), BF16),
+            jax.ShapeDtypeStruct((pieces, cols, rows), BF16),
+            jax.ShapeDtypeStruct((pieces * heads, 1, rows), F32),
+            jax.ShapeDtypeStruct((rows, width), F32),
+        ],
+        compiler_params=pltpu.CompilerParams(vmem_limit_bytes=VMEM_LIMIT),
+        cost_estimate=pl.CostEstimate(flops=16_000_000_000, bytes_accessed=20_000_000, transcendentals=0),
+        name="mixer_forward",
+    )(sel, start, tiles, segment, hidden, norm, qkv_shift, out_shift, *flat(own), *flat(other))
+
+
+def feed_forward_kernel(sel_ref, middle_ref, norm_ref, up_shift_ref, out_shift_ref, *rest, pieces):
+    up_own, down_own, up_other, down_other = [
+        [rest[2 * (pieces * k + i) : 2 * (pieces * k + i) + 2] for i in range(pieces)] for k in range(4)
+    ]
+    out_ref, active_ref, slope_ref, up_weight, down_weight, sems = rest[8 * pieces :]
+    step = pl.program_id(0)
+    sel = sel_ref[0]
+    size = up_weight.shape[2]
+    half = up_own[0][0].shape[0]
+
+    def copies_of(index, refs, kind):
+        target = (up_weight, down_weight)[kind]
+        return piece_copies(
+            refs,
+            sems.at[kind, index],
+            [(0, half, target.at[index, 0:half]), (half, half, target.at[index, half : 2 * half])],
+        )
+
+    @pl.when(step == 0)
+    def _():
+        start_pieces(sel, up_own, up_other, functools.partial(copies_of, kind=0))
+        start_pieces(sel, down_own, down_other, functools.partial(copies_of, kind=1))
+
+    scaled, _ = normalise(middle_ref[...])
+    normed = (scaled * norm_ref[0:1, :] + norm_ref[1:2, :]).astype(BF16)
+    total = middle_ref[...] + out_shift_ref[...]
+    for index in range(pieces):
+
+        @pl.when(step == 0)
+        def _():
+            for copy in copies_of(index, up_own[index], 0) + copies_of(index, down_own[index], 1):
+                copy.wait()
+
+        part = pl.ds(index * size, size)
+        raised = nn(normed, up_weight[index]) + up_shift_ref[:, part]
+        active, slope = gelu_pair(raised)
+        active = active.astype(BF16)
+        active_ref[:, part] = active
+        slope_ref[:, part] = slope.astype(BF16)
+        total = total + nn(active, down_weight[index])
+    out_ref[...] = total.astype(BF16)
+
+
+def feed_forward(sel, middle, norm, up_shift, out_shift, up_own, down_own, up_other, down_other):
+    rows, width = middle.shape
+    pieces = len(up_own)
+    hidden = up_shift.shape[1]
+    size = hidden // pieces
+    block = 256
+    return pl.pallas_call(
+        functools.partial(feed_forward_kernel, pieces=pieces),
+        grid_spec=pltpu.PrefetchScalarGridSpec(
+            num_scalar_prefetch=1,
+            grid=(rows // block,),
+            in_specs=[
+                pl.BlockSpec((block, width), lambda i, *_: (i, 0)),
+                once((2, width)),
+                once((1, hidden)),
+                once((1, width)),
+            ]
+            + anywhere(8 * pieces),
+            out_specs=[
+                pl.BlockSpec((block, width), lambda i, *_: (i, 0)),
+                pl.BlockSpec((block, hidden), lambda i, *_: (i, 0)),
+                pl.BlockSpec((block, hidden), lambda i, *_: (i, 0)),
+            ],
+            scratch_shapes=[
+                pltpu.VMEM((pieces, width, size), BF16),
+                pltpu.VMEM((pieces, size, width), BF16),
+                pltpu.SemaphoreType.DMA((2, pieces, 2)),
+            ],
+        ),
+        out_shape=[
+            jax.ShapeDtypeStruct((rows, width), BF16),
+            jax.ShapeDtypeStruct((rows, hidden), BF16),
+            jax.ShapeDtypeStruct((rows, hidden), BF16),
+        ],
+        compiler_params=pltpu.CompilerParams(vmem_limit_bytes=VMEM_LIMIT),
+        cost_estimate=pl.CostEstimate(flops=16_000_000_000, bytes_accessed=20_000_000, transcendentals=0),
+        name="feed_forward",
+    )(sel, middle, norm, up_shift, out_shift, *flat(up_own), *flat(down_own), *flat(up_other), *flat(down_other))
+
+
+def feed_backward_kernel(sel_ref, grad_ref, middle_ref, norm_ref, active_ref, slope_ref, *rest, pieces, parts):
+    up_own, down_own, up_other, down_other = [
+        [rest[2 * (pieces * k + i) : 2 * (pieces * k + i) + 2] for i in range(pieces)] for k in range(4)
+    ]
+    (
+        weight_grad_ref,
+        up_shift_grad_ref,
+        middle_grad_ref,
+        small_ref,
+        up_weight,
+        down_weight,
+        normed_t,
+        grad_t,
+        low_grad,
+        normed_grad,
+        sems,
+    ) = rest[8 * pieces :]
+    step = pl.program_id(0)
+    sel = sel_ref[0]
+    rows_all, width = grad_ref.shape
+    chunk = active_ref.shape[1]
+    block = 256
+    blocks = rows_all // block
+    half = up_own[0][0].shape[0]
+
+    def copies_of(index, refs, kind):
+        target = (up_weight, down_weight)[kind]
+        return piece_copies(
+            refs,
+            sems.at[kind, index],
+            [(0, half, target.at[index, 0:half]), (half, half, target.at[index, half : 2 * half])],
+        )
+
+    @pl.when(step == 0)
+    def _():
+        start_pieces(sel, down_own, down_other, functools.partial(copies_of, kind=1))
+        start_pieces(sel, up_own, up_other, functools.partial(copies_of, kind=0))
+
+        def prepare(i, carry):
+            rows = pl.ds(pl.multiple_of(i * block, block), block)
+            scaled, _ = normalise(middle_ref[rows, :])
+            normed = (scaled * norm_ref[0:1, :] + norm_ref[1:2, :]).astype(BF16)
+            normed_t[:, rows] = normed.T
+            grad_t[:, rows] = grad_ref[rows, :].T
+            return carry
+
+        lax.fori_loop(0, blocks, prepare, 0)
+
+    for index in range(pieces):
+
+        @pl.when(step == index * parts)
+        def _():
+            for copy in copies_of(index, up_own[index], 0) + copies_of(index, down_own[index], 1):
+                copy.wait()
+
+    piece = step // parts
+    for part in range(parts):
+
+        @pl.when(step % parts == part)
+        def _():
+            cols = pl.ds(part * chunk, chunk)
+
+            def back(i, shift_grad):
+                rows = pl.ds(pl.multiple_of(i * block, block), block)
+                active_grad = nt(grad_ref[rows, :], down_weight[piece, cols, :])
+                hidden_grad = active_grad * slope_ref[rows, :].astype(F32)
+                low = hidden_grad.astype(BF16)
+                low_grad[rows, :] = low
+                term = nt(low, up_weight[piece, :, cols])
+
+                @pl.when(step == 0)
+                def _():
+                    normed_grad[rows, :] = term
+
+                @pl.when(step != 0)
+                def _():
+                    normed_grad[rows, :] += term
+
+                return shift_grad + jnp.sum(hidden_grad, axis=0, keepdims=True)
+
+            up_shift_grad_ref[0] = lax.fori_loop(0, blocks, back, jnp.zeros((1, chunk), F32))
+
+    def weigh(i, carry):
+        rows = pl.ds(pl.multiple_of(i * block, block), block)
+        weight_grad_ref[0, rows, :] = nn(normed_t[rows, :], low_grad[...]).astype(BF16)
+        lower = pl.ds(pl.multiple_of(width + i * block, block), block)
+        weight_grad_ref[0, lower, :] = nn(grad_t[rows, :], active_ref[...]).astype(BF16)
+        return carry
+
+    lax.fori_loop(0, width // block, weigh, 0)
+
+    @pl.when(step == pieces * parts - 1)
+    def _():
+        def finish(i, sums):
+            rows = pl.ds(pl.multiple_of(i * block, block), block)
+            scaled, inverse = normalise(middle_ref[rows, :])
+            gradient = normed_grad[rows, :]
+            upper = grad_ref[rows, :].astype(F32)
+            middle_grad = upper + normalise_back(gradient, scaled, inverse, norm_ref[0:1, :])
+            middle_grad_ref[rows, :] = middle_grad
+            terms = (gradient * scaled, gradient, middle_grad, upper)
+            return tuple(old + jnp.sum(term, axis=0, keepdims=True) for old, term in zip(sums, terms))
+
+        zero = jnp.zeros((1, width), F32)
+        sums = lax.fori_loop(0, blocks, finish, (zero, zero, zero, zero))
+        for index, row in enumerate(sums):
+            small_ref[index : index + 1, :] = row
+
+
+def feed_backward(sel, grad, middle, norm, active, slope, up_own, down_own, up_other, down_other):
+    rows, width = middle.shape
+    pieces = len(up_own)
+    hidden = active.shape[1]
+    size = hidden // pieces
+    parts = 2
+    chunk = size // parts
+    return pl.pallas_call(
+        functools.partial(feed_backward_kernel, pieces=pieces, parts=parts),
+        grid_spec=pltpu.PrefetchScalarGridSpec(
+            num_scalar_prefetch=1,
+            grid=(pieces * parts,),
+            in_specs=[
+                once((rows, width)),
+                once((rows, width)),
+                once((2, width)),
+                pl.BlockSpec((rows, chunk), lambda i, *_: (0, i)),
+                pl.BlockSpec((rows, chunk), lambda i, *_: (0, i)),
+            ]
+            + anywhere(8 * pieces),
+            out_specs=[
+                pl.BlockSpec((1, 2 * width, chunk), lambda i, *_: (i // parts, 0, i % parts)),
+                pl.BlockSpec((1, 1, chunk), lambda i, *_: (i, 0, 0)),
+                once((rows, width)),
+                once((4, width)),
+            ],
+            scratch_shapes=[
+                pltpu.VMEM((pieces, width, size), BF16),
+                pltpu.VMEM((pieces, size, width), BF16),
+                pltpu.VMEM((width, rows), BF16),
+                pltpu.VMEM((width, rows), BF16),
+                pltpu.VMEM((rows, chunk), BF16),
+                pltpu.VMEM((rows, width), F32),
+                pltpu.SemaphoreType.DMA((2, pieces, 2)),
+            ],
+        ),
+        out_shape=[
+            jax.ShapeDtypeStruct((pieces, 2 * width, size), BF16),
+            jax.ShapeDtypeStruct((pieces * parts, 1, chunk), F32),
+            jax.ShapeDtypeStruct((rows, width), F32),
+            jax.ShapeDtypeStruct((4, width), F32),
+        ],
+        compiler_params=pltpu.CompilerParams(vmem_limit_bytes=VMEM_LIMIT),
+        cost_estimate=pl.CostEstimate(flops=30_000_000_000, bytes_accessed=50_000_000, transcendentals=0),
+        name="feed_backward",
+    )(sel, grad, middle, norm, active, slope, *flat(up_own), *flat(down_own), *flat(up_other), *flat(down_other))
+
+
+def attend_backward_image(index, at, width, heads, seg_ref, qkv_ref, mixed_ref, total_ref, mixed_grad, sums):
+    win = pl.ds(at, width)
+    mine = seg_ref[:, win] == index
+    mask = jnp.where(mine, 0.0, NEGATIVE)
+    one = jnp.ones((1, width), F32)
+    key_extra = extra_rows([one, mask, one, one, one], width)
+    value_extra = extra_rows([one, one, one], width)
+    cols = heads * HEAD_DIM
+
+    def head(which, carry):
+        low = pl.multiple_of(which * HEAD_DIM, EXTRA)
+        query_rows = pl.ds(low, HEAD_DIM)
+        key_rows = pl.ds(cols + low, HEAD_DIM)
+        value_rows = pl.ds(2 * cols + low, HEAD_DIM)
+        queries = qkv_ref[0, query_rows, win]
+        keys = qkv_ref[0, key_rows, win]
+        values = qkv_ref[0, value_rows, win]
+        grads = mixed_grad[query_rows, win]
+        inner = jnp.sum(
+            grads.astype(F32) * mixed_ref[0, query_rows, win].astype(F32), axis=0, keepdims=True
+        )
+        query_extra = extra_rows([mask, one] + three_parts(-total_ref[which, :, win]), width)
+        grad_extra = extra_rows(three_parts(-inner), width)
+        scores = tn(jnp.concatenate([keys, key_extra], axis=0), jnp.concatenate([queries, query_extra], axis=0))
+        weights = jnp.exp2(scores)
+        terms = tn(jnp.concatenate([values, value_extra], axis=0), jnp.concatenate([grads, grad_extra], axis=0))
+        score_grads = (weights * terms).astype(BF16)
+        sums[query_rows, win] += nn(keys, score_grads) * SCALING
+        sums[key_rows, win] += nt(queries, score_grads) * (1.0 / LOG2E)
+        sums[value_rows, win] += nt(grads, weights.astype(BF16))
+        return carry
+
+    lax.fori_loop(0, heads, head, 0, unroll=2)
+
+
+def mixer_backward_kernel(
+    sel_ref, start_ref, tiles_ref, seg_ref, hidden_ref, middle_grad_ref, norm_ref, qkv_ref, mixed_ref, total_ref, *rest,
+    pieces, heads,
+):
+    own = [rest[2 * i : 2 * i + 2] for i in range(pieces)]
+    other = [rest[2 * pieces + 2 * i : 2 * pieces + 2 * i + 2] for i in range(pieces)]
+    (
+        weight_grad_ref,
+        qkv_shift_grad_ref,
+        in_grad_ref,
+        small_ref,
+        weight,
+        out_weight,
+        normed,
+        low_middle,
+        mixed_grad,
+        sums,
+        projected_grad,
+        sems,
+    ) = rest[4 * pieces :]
+    step = pl.program_id(0)
+    sel = sel_ref[0]
+    cols = heads * HEAD_DIM
+    rows_all, width = hidden_ref.shape
+    block = 256
+    blocks = rows_all // block
+    half = own[0][0].shape[0]
+
+    def copies_of(index, refs):
+        first = index * 3 * cols
+        return piece_copies(
+            refs,
+            sems.at[index],
+            [
+                (3 * cols, cols, out_weight.at[index * cols : (index + 1) * cols]),
+                (0, half, weight.at[first : first + half]),
+                (half, 3 * cols - half, weight.at[first + half : first + 3 * cols]),
+            ],
+        )
+
+    @pl.when(step == 0)
+    def _():
+        start_pieces(sel, own, other, copies_of)
+
+        def prepare(i, carry):
+            rows = pl.ds(pl.multiple_of(i * block, block), block)
+            scaled, _ = normalise(hidden_ref[rows, :].astype(F32))
+            normed[rows, :] = (scaled * norm_ref[0:1, :] + norm_ref[1:2, :]).astype(BF16)
+            low_middle[rows, :] = middle_grad_ref[rows, :].astype(BF16)
+            return carry
+
+        lax.fori_loop(0, blocks, prepare, 0)
+
+    for index in range(pieces):
+
+        @pl.when(step == index)
+        def _():
+            for copy in copies_of(index, own[index]):
+                copy.wait()
+
+    def spread(i, carry):
+        win = pl.ds(pl.multiple_of(i * block, block), block)
+        mine = out_weight[pl.ds(pl.multiple_of(step * cols, cols), cols), :]
+        mixed_grad[:, win] = nt(mine, low_middle[win, :]).astype(BF16)
+        return carry
+
+    lax.fori_loop(0, blocks, spread, 0)
+    weight_grad_ref[0, 3 * cols : 4 * cols, :] = nn(mixed_ref[0], low_middle[...]).astype(BF16)
+    sums[...] = jnp.zeros_like(sums)
+    each_image(
+        start_ref,
+        tiles_ref,
+        lambda index, at, width: attend_backward_image(
+            index, at, width, heads, seg_ref, qkv_ref, mixed_ref, total_ref, mixed_grad, sums
+        ),
+    )
+    for third in range(3):
+        rows = pl.ds(third * cols, cols)
+        gradient = sums[rows, :]
+        low = gradient.astype(BF16)
+        projected_grad[pl.ds(pl.multiple_of(step * (3 * cols) + third * cols, cols), cols), :] = low
+        qkv_shift_grad_ref[0, rows, :] = jnp.sum(gradient, axis=1, keepdims=True)
+        weight_grad_ref[0, rows, :] = nn(low, normed[...]).astype(BF16)
+
+    @pl.when(step == pieces - 1)
+    def _():
+        def finish(i, carry):
+            rows = pl.ds(pl.multiple_of(i * block, block), block)
+            scaled, inverse = normalise(hidden_ref[rows, :].astype(F32))
+            gradient = tn(projected_grad[:, rows], weight[...])
+            in_grad = middle_grad_ref[rows, :] + normalise_back(gradient, scaled, inverse, norm_ref[0:1, :])
+            in_grad_ref[rows, :] = in_grad.astype(BF16)
+            terms = (gradient * scaled, gradient)
+            return tuple(old + jnp.sum(term, axis=0, keepdims=True) for old, term in zip(carry, terms))
+
+        zero = jnp.zeros((1, width), F32)
+        totals = lax.fori_loop(0, blocks, finish, (zero, zero))
+        for index, row in enumerate(totals):
+            small_ref[index : index + 1, :] = row
+
+
+def mixer_backward(sel, images, hidden, middle_grad, norm, qkv, mixed, totals, own, other):
+    rows, width = hidden.shape
+    pieces = len(own)
+    heads = width // HEAD_DIM // pieces
+    cols = heads * HEAD_DIM
+    start, tiles, segment = images
+    return pl.pallas_call(
+        functools.partial(mixer_backward_kernel, pieces=pieces, heads=heads),
+        grid_spec=pltpu.PrefetchScalarGridSpec(
+            num_scalar_prefetch=3,
+            grid=(pieces,),
+            in_specs=[
+                once((1, rows)),
+                once((rows, width)),
+                once((rows, width)),
+                once((2, width)),
+                pl.BlockSpec((1, 3 * cols, rows), lambda i, *_: (i, 0, 0)),
+                pl.BlockSpec((1, cols, rows), lambda i, *_: (i, 0, 0)),
+                pl.BlockSpec((heads, 1, rows), lambda i, *_: (i, 0, 0)),
+            ]
+            + anywhere(4 * pieces),
+            out_specs=[
+                pl.BlockSpec((1, 4 * cols, width), lambda i, *_: (i, 0, 0)),
+                pl.BlockSpec((1, 3 * cols, 1), lambda i, *_: (i, 0, 0)),
+                once((rows, width)),
+                once((2, width)),
+            ],
+            scratch_shapes=[
+                pltpu.VMEM((3 * width, width), BF16),
+                pltpu.VMEM((width, width), BF16),
+                pltpu.VMEM((rows, width), BF16),
+                pltpu.VMEM((rows, width), BF16),
+                pltpu.VMEM((cols, rows), BF16),
+                pltpu.VMEM((3 * cols, rows), F32),
+                pltpu.VMEM((3 * width, rows), BF16),
+                pltpu.SemaphoreType.DMA((pieces, 3)),
+            ],
+        ),
+        out_shape=[
+            jax.ShapeDtypeStruct((pieces, 4 * cols, width), BF16),
+            jax.ShapeDtypeStruct((pieces, 3 * cols, 1), F32),
+            jax.ShapeDtypeStruct((rows, width), BF16),
+            jax.ShapeDtypeStruct((2, width), F32),
+        ],
+        compiler_params=pltpu.CompilerParams(vmem_limit_bytes=VMEM_LIMIT),
+        cost_estimate=pl.CostEstimate(flops=40_000_000_000, bytes_accessed=20_000_000, transcendentals=0),
+        name="mixer_backward",
+    )(sel, start, tiles, segment, hidden, middle_grad, norm, qkv, mixed, totals, *flat(own), *flat(other))
+
+
+def route(change):
+    shape = [lax.axis_size(axis) for axis in AXES]
+    pairs = []
+    for s in range(shape[0]):
+        for d in range(shape[1]):
+            for t in range(shape[2]):
+                to = change(s, d, t)
+                if to is not None:
+                    pairs.append(((s * shape[1] + d) * shape[2] + t, (to[0] * shape[1] + to[1]) * shape[2] + to[2]))
+    return pairs
+
+
+def swap(block, change):
+    return lax.ppermute(block, AXES, route(change))
+
+
+def over_tensor(s, d, t):
+    return (s, d, 1 - t)
+
+
+def over_section(s, d, t):
+    return (1 - s, d, t)
+
+
+def over_core(s, d, t):
+    return (s, d ^ 1, t)
+
+
+def gather_family(own_halves, core):
+    mine = lax.dynamic_index_in_dim(own_halves, core, 0, keepdims=False)
+    twin = lax.dynamic_index_in_dim(own_halves, 1 - core, 0, keepdims=False)
+    half = mine.shape[0] // 2
+    beside = swap(mine, over_tensor)
+    across = swap(mine, over_section)
+    far_low = swap(beside[:half], over_section)
+    far_high = swap(across[half:], over_tensor)
+
+    def halves(piece):
+        return (piece[:half], piece[half:])
+
+    own = [halves(mine), halves(twin), halves(beside), halves(swap(beside, over_core))]
+    other = [
+        halves(across),
+        halves(swap(across, over_core)),
+        (far_low, far_high),
+        (swap(far_low, over_core), swap(far_high, over_core)),
+    ]
+    return own, other
+
+
+def take_half(block, which, axis):
+    half = block.shape[axis] // 2
+    return lax.dynamic_slice_in_dim(block, which * half, half, axis)
+
+
+def added(left, right):
+    return (left.astype(F32) + right.astype(F32)).astype(BF16)
+
+
+def reduce_family(grads, layer, section, core, z_index, z_count):
+    pieces, rows, columns = grads.shape
+    pairs = grads.reshape(2, 2, rows, columns)
+    chip = added(pairs[:, 0], swap(pairs[:, 1], over_core))
+    lane = added(chip[0], swap(chip[1], over_tensor))
+    part = added(take_half(lane, section, 0), swap(take_half(lane, 1 - section, 0), over_section))
+    bits = []
+    distance = 1
+    while distance < z_count:
+        bits.append(distance)
+        distance *= 2
+    for distance in bits:
+        along = lambda s, d, t, distance=distance: (s, ((d // 2) ^ distance) * 2 + d % 2, t)
+        bit = (z_index // distance) % 2
+        part = added(take_half(part, bit, 0), swap(take_half(part, 1 - bit, 0), along))
+    for distance in reversed(bits):
+        along = lambda s, d, t, distance=distance: (s, ((d // 2) ^ distance) * 2 + d % 2, t)
+        bit = (z_index // distance) % 2
+        came = swap(part, along)
+        part = jnp.where(bit == 0, jnp.concatenate([part, came], 0), jnp.concatenate([came, part], 0))
+    back = swap(part, lambda s, d, t: (layer, d, t) if s != layer else None)
+    whole = jnp.concatenate([part, back] if layer == 0 else [back, part], 0)
+    twin = swap(whole, over_core)
+    return jnp.where(core == 0, jnp.stack([whole, twin]), jnp.stack([twin, whole]))
+
+
+def spread_output(block, layer, lane):
+    mine = take_half(block, lane, 0)
+    rest = take_half(block, 1 - lane, 0)
+    return [
+        mine,
+        swap(rest, lambda s, d, t: (s, d, 1 - t) if s == layer else None),
+        swap(mine, lambda s, d, t: (layer, d, t) if s != layer else None),
+        swap(rest, lambda s, d, t: (layer, d, 1 - t) if s != layer else None),
+    ]
+
+
+def reordered(pieces, lane, core):
+    pieces = jnp.where(lane == 0, pieces, pieces[jnp.array([2, 3, 0, 1])])
+    return jnp.where(core == 0, pieces, pieces[jnp.array([1, 0, 3, 2])])
+
+
+def one_sequence_each(
+    inputs,
+    cotangent,
+    segment_ids,
+    norm_gains,
+    norm_biases,
+    qkv_weight,
+    qv_bias,
+    out_weight,
+    up_weight,
+    up_bias,
+    down_weight,
+    out_biases,
+):
+    section = lax.axis_index("section")
+    group = lax.axis_index("dp")
+    lane = lax.axis_index("tensor")
+    core = group % 2
+    z_index = group // 2
+    z_count = lax.axis_size("dp") // 2
+    own_rows, width = inputs.shape[1:]
+    hidden = up_bias.shape[1]
+    cols = qkv_weight.shape[3]
+    part = cols // 2
+    mine = 2 * section + lane
+
+    projections = qkv_weight[0].transpose(0, 2, 1).reshape(3, 2, part, width).transpose(1, 0, 2, 3)
+    mixer_halves = jnp.concatenate(
+        [projections.reshape(2, 3 * part, width), out_weight[0].reshape(2, part, width)], axis=1
+    )
+    up_halves = up_weight[0].reshape(width, 2, -1).transpose(1, 0, 2)
+    down_halves = down_weight[0].reshape(2, -1, width)
+
+    def whole_sequence(array):
+        kept = lax.dynamic_index_in_dim(array, mine, 0, keepdims=False)
+        sent = lax.dynamic_index_in_dim(array, 2 * section + 1 - lane, 0, keepdims=False)
+        came = swap(sent, over_tensor)
+        return jnp.where(lane == 0, jnp.concatenate([kept, came], 0), jnp.concatenate([came, kept], 0))
+
+    small = jnp.concatenate(
+        [
+            norm_gains.reshape(-1),
+            norm_biases.reshape(-1),
+            qv_bias.reshape(-1),
+            up_bias.reshape(-1),
+            out_biases.reshape(-1),
+        ]
+    )
+    small_other = swap(small, over_section)
+    smalls = [jnp.where(section == layer, small, small_other) for layer in range(2)]
+
+    first_in = whole_sequence(inputs)
+    mixer_own, mixer_other = gather_family(mixer_halves, core)
+    up_own, up_other = gather_family(up_halves, core)
+    down_own, down_other = gather_family(down_halves, core)
+    last_grad = whole_sequence(cotangent)
+
+    segment = lax.dynamic_index_in_dim(segment_ids, mine, 0, keepdims=True)
+    ids = jnp.arange(IMAGE_IDS, dtype=jnp.int32)[:, None]
+    begin = jnp.sum((segment < ids).astype(jnp.int32), axis=1)
+    end = jnp.sum((segment <= ids).astype(jnp.int32), axis=1)
+    start = begin // TILE
+    images = (start, (end - 1) // TILE - start + 1, segment)
+
+    def params(layer):
+        vector = smalls[layer]
+        gains = vector[: 2 * width].reshape(2, width)
+        shifts = vector[2 * width : 4 * width].reshape(2, width)
+        qv = vector[4 * width : 6 * width].reshape(2, 4, part)
+        ups = vector[6 * width : 6 * width + hidden].reshape(4, hidden // 4)
+        outs = vector[6 * width + hidden :].reshape(2, 1, width)
+        zero = jnp.zeros((4, part), F32)
+        qkv_shift = jnp.concatenate([reordered(qv[0], lane, core), zero, reordered(qv[1], lane, core)], axis=1)
+        up_shift = reordered(ups, lane, core).reshape(1, hidden)
+        norms = [jnp.stack([gains[i], shifts[i]]) for i in range(2)]
+        return norms, qkv_shift[:, :, None], up_shift, outs
+
+    state = first_in
+    kept = []
+    outputs = []
+    for layer in range(2):
+        sel = (section ^ layer).astype(jnp.int32).reshape(1)
+        norms, qkv_shift, up_shift, outs = params(layer)
+        qkv, mixed, totals, middle = mixer_forward(
+            sel, images, state, norms[0], qkv_shift, outs[0], mixer_own, mixer_other
+        )
+        result, active, slope = feed_forward(
+            sel, middle, norms[1], up_shift, outs[1], up_own, down_own, up_other, down_other
+        )
+        kept.append((sel, norms, state, qkv, mixed, totals, middle, active, slope))
+        state = result
+        outputs.append(spread_output(result, layer, lane))
+
+    grad = last_grad
+    weight_grads = [None, None]
+    small_grads = [None, None]
+    in_grads = [None, None]
+    for layer in (1, 0):
+        sel, norms, state, qkv, mixed, totals, middle, active, slope = kept[layer]
+        feed_grads, up_shift_grad, middle_grad, feed_small = feed_backward(
+            sel, grad, middle, norms[1], active, slope, up_own, down_own, up_other, down_other
+        )
+        feed_sum = reduce_family(feed_grads, layer, section, core, z_index, z_count)
+        mixer_grads, qkv_shift_grad, grad, mixer_small = mixer_backward(
+            sel, images, state, middle_grad, norms[0], qkv, mixed, totals, mixer_own, mixer_other
+        )
+        in_grads[layer] = spread_output(grad, layer, lane)
+        mixer_sum = reduce_family(mixer_grads, layer, section, core, z_index, z_count)
+        weight_grads[layer] = (feed_sum, mixer_sum)
+        qkv_shift_grad = qkv_shift_grad.reshape(4, 3, part)
+        query_grad = reordered(qkv_shift_grad[:, 0], lane, core).reshape(-1)
+        value_grad = reordered(qkv_shift_grad[:, 2], lane, core).reshape(-1)
+        up_grad = reordered(up_shift_grad.reshape(4, hidden // 4), lane, core).reshape(-1)
+        vector = jnp.concatenate(
+            [
+                mixer_small[0],
+                feed_small[0],
+                mixer_small[1],
+                feed_small[1],
+                query_grad,
+                value_grad,
+                up_grad,
+                feed_small[2],
+                feed_small[3],
+            ]
+        )
+        small_grads[layer] = lax.psum(vector, AXES)
+
+    def pick(pair):
+        return jnp.where(section == 0, pair[0], pair[1])
+
+    def gathered(pair):
+        relative = jnp.stack([pick(both) for both in zip(*pair)])
+        relative = jnp.where(lane == 0, relative, relative[jnp.array([1, 0, 3, 2])])
+        return jnp.where(section == 0, relative, relative[jnp.array([2, 3, 0, 1])])
+
+    states = gathered(outputs)
+    grads = gathered(in_grads).astype(F32)
+    feed_sum = pick([pair[0] for pair in weight_grads]).astype(F32)
+    mixer_sum = pick([pair[1] for pair in weight_grads]).astype(F32)
+    vector = pick(small_grads)
+    qkv_grad = mixer_sum[:, : 3 * part].reshape(2, 3, part, width).transpose(1, 3, 0, 2).reshape(3, width, cols)
+    out_grad = mixer_sum[:, 3 * part :].reshape(cols, width)
+    up_grad = feed_sum[:, :width].transpose(1, 0, 2).reshape(width, -1)
+    down_grad = feed_sum[:, width:].transpose(0, 2, 1).reshape(-1, width)
+    return (
+        states[None],
+        grads[None],
+        vector[: 2 * width].reshape(1, 2, width),
+        vector[2 * width : 4 * width].reshape(1, 2, width),
+        qkv_grad[None],
+        vector[4 * width : 6 * width].reshape(1, 2, width),
+        out_grad[None],
+        up_grad[None],
+        vector[6 * width : 6 * width + hidden].reshape(1, hidden),
+        down_grad[None],
+        vector[6 * width + hidden :].reshape(1, 2, width),
+    )
 
 
 def passed_along(block, axis, distance):
@@ -155,7 +1110,7 @@
     return array.at[which].set(jnp.where(running, value, array[which]))
 
 
-def on_device(
+def pipelined(
     inputs,
     cotangent,
     segment_ids,
@@ -419,6 +1374,16 @@
         P("section", "tensor", None),
         P("section", None, None),
     )
+    sizes = dict(mesh.shape)
+
+    def on_device(inputs, *rest):
+        each = inputs.shape[0] == sizes["section"] * sizes["tensor"]
+        paired = sizes["section"] == 2 and sizes["tensor"] == 2 and sizes["dp"] % 2 == 0
+        doubling = (sizes["dp"] // 2) & (sizes["dp"] // 2 - 1) == 0
+        if each and paired and doubling:
+            return one_sequence_each(inputs, *rest)
+        return pipelined(inputs, *rest)
+
     return jax.shard_map(
         on_device,
         mesh=mesh,

time: 4520 us -> 1250 us (0.28)
  matrix products: 1260 us -> 0 us
  waiting for transfers between devices: 1390 us -> 424 us
  local copies, waits for them, and re-layouts: 1020 us -> 146 us
  Pallas kernels: 0 us -> 445 us
  loops' own time: 348 us -> 0 us
  other arithmetic: 346 us -> 119 us
  starting transfers between devices: 27 us -> 86.1 us
  blocking collectives: 55.3 us -> 0 us
    dot_general x705 -> x0, matrix products: 1260 us -> none  [the longest x80 178 us: one_item(): jnp.dot(weights, head_values, preferred_element_type=jnp.float32)]
    all_gather x30 -> x0, waiting for transfers between devices: 606 us -> none  [the longest x10 314 us: spread_rows(): lax.all_gather(normed_rows, 'tensor', axis=0, tiled=True)]
    reduce_scatter x20 -> x0, waiting for transfers between devices: 527 us -> none  [the longest x10 276 us: input_sum(): lax.psum_scatter(jnp.einsum('sc,dc->sd', grad_rows, weight, preferred_ele...]
    pallas_call x0 -> x8, Pallas kernels: none -> 445 us  [the longest x2 159 us: mixer_backward(): pl.pallas_call(functools.partial(mixer_backward_kernel, pieces=pieces, he...]
    dynamic_slice x817 -> x13, local copies, waits for them, and re-layouts: 401 us -> 1.86 us  [the longest x1 1.33 us: one_sequence_each(): segment = lax.dynamic_index_in_dim(segment_ids, mine, 0, keepdims=True)]
    another operation x50 -> x0, loops' own time: 348 us -> none  [the longest x5 213 us: attend_forward(): lax.map(one_item, jnp.arange(2 * heads_local, dtype=jnp.int32))]
    while x1685 -> x0, local copies, waits for them, and re-layouts: 243 us -> none
    dynamic_update_slice x280 -> x0, local copies, waits for them, and re-layouts: 234 us -> none  [the longest x200 229 us: attend_backward(): results = lax.map(one_head, jnp.arange(heads_local, dtype=jnp.int32))]
where the time goes in v1:
time: 1250 us; the launch traced here: 1240 us
  Pallas kernels  445 us (36%)
  waiting for transfers between devices  424 us (34%)
  local copies, waits for them, and re-layouts  146 us (12%)
  other arithmetic  119 us (10%)
  starting transfers between devices  86.1 us (7%)
  between operations  16.2 us (1%)
    ppermute x75, waiting for transfers between devices, swap(): return lax.ppermute(block, AXES, route(change))  335 us
    pallas_call x2, Pallas kernels, mixer_backward(): pl.pallas_call(functools.partial(mixer_backward_kernel, pieces=pieces, he...  159 us
    pallas_call x2, Pallas kernels, feed_backward(): pl.pallas_call(functools.partial(feed_backward_kernel, pieces=pieces, par...  129 us
    pallas_call x2, Pallas kernels, mixer_forward(): pl.pallas_call(functools.partial(mixer_forward_kernel, pieces=pieces, hea...  92.4 us
    psum x1, waiting for transfers between devices, one_sequence_each(): small_grads[layer] = lax.psum(vector, AXES)  89.2 us
    ppermute x75, starting transfers between devices, swap(): return lax.ppermute(block, AXES, route(change))  86 us
    pallas_call x2, Pallas kernels, feed_forward(): pl.pallas_call(functools.partial(feed_forward_kernel, pieces=pieces), gri...  63.7 us
    another operation x11, other arithmetic, gathered(): relative = jnp.stack([pick(both) for both in zip(*pair)])  30 us
  transfers between devices with their start and end apart: 76, of which 24 were waited for; matrix products, arithmetic and copies ran while one was open for 17% of the time, Pallas kernels for 4%

profile of v1, /device:TPU:3, one launch (start us, length us, event | category | flops | bytes accessed | tf_op | source)
XLA Modules:
  0.0 1236.3 jit_solution(870466736293176816)
XLA Ops:
  24.8 5.1 reshape_squeeze.10
  29.9 4.9 constant_dynamic-slice_fusion.19
  69.3 37.4 %collective-permute-done.32 = bf16[640,768]{1,0:T(8,128)(2,1)} collective-permute-done((bf16[640,768]{1,0:T(8,128)(2,1)}, bf16[640,768]{1,0:T(8,128)(2,1)}, u32[]{:S(2)}, u32[]{:S(2)}) %collective-permute-start.32) | collective-permute-done | bytes 983072 | tf_op jit(solution)/shard_map/ppermute | solution.py:720
  108.2 3.3 maximum_select_fusion.6.hidden_ref
  111.5 3.4 maximum_select_fusion.7.grad_ref
  121.6 11.2 collective-permute-done.12
  134.4 3.2 collective-permute-start.15
  140.9 4.9 collective-permute-done.6.rest_12_
  147.9 3.3 collective-permute-start.8
  154.5 3.7 collective-permute-done.16.rest_20_
  160.0 4.5 collective-permute-start.11
  165.4 46.3 %mixer_forward.2 = (bf16[4,576,1280]{2,1,0:T(8,128)(2,1)}, bf16[4,192,1280]{2,1,0:T(8,128)(2,1)}, f32[16,1,1280]{2,1,0:T(1,128)}, f32[1280,768]{1,0:T(8,128)}) custom-call(s32[1]{0:T(128)} %bitcast.sel_ref, s32[5]{0:T(128)} %get-tuple-element.135.start_ref, s32[5]{0:T(128)} %get-tuple-element.134.tiles_ref, s32[1,1280]{1,0:T(1,128)} %get-tuple-element.137.seg_ref, ...), custom_call_target="tpu_custom_call" | custom-call | flops 16000000000 | bytes 20000000 | tf_op jit(solution)/shard_map/mixer_forward/pallas_call | solution.py:242
  219.4 32.0 %feed_forward.2 = (bf16[1280,768]{1,0:T(8,128)(2,1)}, bf16[1280,3072]{1,0:T(8,128)(2,1)}, bf16[1280,3072]{1,0:T(8,128)(2,1)}) custom-call(s32[1]{0:T(128)} %bitcast.sel_ref, f32[1280,768]{1,0:T(8,128)} %get-tuple-element.41.middle_ref, f32[2,768]{1,0:T(2,128)} %pad_maximum_fusion.7.norm_ref, f32[1,3072]{1,0:T(1,128)} %bitcast.263, ...), custom_call_target="tpu_custom_call" | custom-call | flops 16000000000 | bytes 20000000 | tf_op jit(solution)/shard_map/feed_forward/pallas_call | solution.py:330
  251.4 46.1 %mixer_forward.3 = (bf16[4,576,1280]{2,1,0:T(8,128)(2,1)}, bf16[4,192,1280]{2,1,0:T(8,128)(2,1)}, f32[16,1,1280]{2,1,0:T(1,128)}, f32[1280,768]{1,0:T(8,128)}) custom-call(s32[1]{0:T(128)} %bitcast.29.sel_ref, s32[5]{0:T(128)} %get-tuple-element.135.start_ref, s32[5]{0:T(128)} %get-tuple-element.134.tiles_ref, s32[1,1280]{1,0:T(1,128)} %get-tuple-element.137.seg_ref, ...), custom_call_target="tpu_custom_call" | custom-call | flops 16000000000 | bytes 20000000 | tf_op jit(solution)/shard_map/mixer_forward/pallas_call | solution.py:242
  297.5 31.7 %feed_forward.3 = (bf16[1280,768]{1,0:T(8,128)(2,1)}, bf16[1280,3072]{1,0:T(8,128)(2,1)}, bf16[1280,3072]{1,0:T(8,128)(2,1)}) custom-call(s32[1]{0:T(128)} %bitcast.29.sel_ref, f32[1280,768]{1,0:T(8,128)} %get-tuple-element.43.middle_ref, f32[2,768]{1,0:T(2,128)} %pad_maximum_fusion.9.norm_ref, f32[1,3072]{1,0:T(1,128)} %bitcast.264, ...), custom_call_target="tpu_custom_call" | custom-call | flops 16000000000 | bytes 20000000 | tf_op jit(solution)/shard_map/feed_forward/pallas_call | solution.py:330
  329.3 64.7 %feed_backward.2 = (bf16[4,1536,768]{2,1,0:T(8,128)(2,1)}, f32[8,1,384]{2,1,0:T(1,128)}, f32[1280,768]{1,0:T(8,128)}, f32[4,768]{1,0:T(4,128)}) custom-call(s32[1]{0:T(128)} %bitcast.29.sel_ref, bf16[1280,768]{1,0:T(8,128)(2,1)} %maximum_select_fusion.7.grad_ref, f32[1280,768]{1,0:T(8,128)} %get-tuple-element.43.middle_ref, ...), custom_call_target="tpu_custom_call" | custom-call | flops 30000001024 | bytes 50000000 | tf_op jit(solution)/shard_map/feed_backward/pallas_call | solution.py:480
  394.0 79.5 %mixer_backward.2 = (bf16[4,768,768]{2,1,0:T(8,128)(2,1)}, f32[4,576,1]{2,1,0:T(8,128)}, bf16[1280,768]{1,0:T(8,128)(2,1)}, f32[2,768]{1,0:T(2,128)}) custom-call(s32[1]{0:T(128)} %bitcast.29.sel_ref, s32[5]{0:T(128)} %get-tuple-element.135.start_ref, s32[5]{0:T(128)} %get-tuple-element.134.tiles_ref, s32[1,1280]{1,0:T(1,128)} %get-tuple-element.137.seg_ref, ...), custom_call_target="tpu_custom_call" | custom-call | flops 40000000000 | bytes 20000000 | tf_op jit(solution)/shard_map/mixer_backward/pallas_call | solution.py:663
  473.5 64.7 %feed_backward.3 = (bf16[4,1536,768]{2,1,0:T(8,128)(2,1)}, f32[8,1,384]{2,1,0:T(1,128)}, f32[1280,768]{1,0:T(8,128)}, f32[4,768]{1,0:T(4,128)}) custom-call(s32[1]{0:T(128)} %bitcast.sel_ref, bf16[1280,768]{1,0:T(8,128)(2,1)} %get-tuple-element.51.grad_ref, f32[1280,768]{1,0:T(8,128)} %get-tuple-element.41.middle_ref, f32[2,768]{1,0:T(2,128)} %pad_maximum_fusion.7.norm_ref, ...), custom_call_target="tpu_custom_call" | custom-call | flops 30000001024 | bytes 50000000 | tf_op jit(solution)/shard_map/feed_backward/pallas_call | solution.py:480
  538.3 80.0 %mixer_backward.3 = (bf16[4,768,768]{2,1,0:T(8,128)(2,1)}, f32[4,576,1]{2,1,0:T(8,128)}, bf16[1280,768]{1,0:T(8,128)(2,1)}, f32[2,768]{1,0:T(2,128)}) custom-call(s32[1]{0:T(128)} %bitcast.sel_ref, s32[5]{0:T(128)} %get-tuple-element.135.start_ref, s32[5]{0:T(128)} %get-tuple-element.134.tiles_ref, s32[1,1280]{1,0:T(1,128)} %get-tuple-element.137.seg_ref, ...), custom_call_target="tpu_custom_call" | custom-call | flops 40000000000 | bytes 20000000 | tf_op jit(solution)/shard_map/mixer_backward/pallas_call | solution.py:663
  626.4 3.9 fusion.17
  633.8 4.9 slice_bitcast_fusion.2
  648.5 8.3 collective-permute-start.29
  657.0 3.2 slice_bitcast_fusion.10
  663.5 4.3 fusion.25
  667.8 3.1 fusion.18
  670.8 8.5 collective-permute-done.28
  680.7 17.4 %collective-permute-done.29 = bf16[640,768]{1,0:T(8,128)(2,1)} collective-permute-done((bf16[640,768]{1,0:T(8,128)(2,1)S(1)}, bf16[640,768]{1,0:T(8,128)(2,1)}, u32[]{:S(2)}, u32[]{:S(2)}) %collective-permute-start.29) | collective-permute-done | bytes 983072 | tf_op jit(solution)/shard_map/ppermute | solution.py:720
  701.6 3.3 slice_bitcast_fusion.12
  705.0 89.2 %all-reduce.3.cloned.1.call-done = (f32[9216]{0:T(1024)}, f32[9216]{0:T(1024)}) async-done(((f32[9216]{0:T(1024)}, f32[9216]{0:T(1024)}), (f32[9216]{0:T(1024)}, f32[9216]{0:T(1024)})) %all-reduce.3.cloned.1.call-update) | async-done | bytes 73744 | tf_op jit(solution)/shard_map/psum | solution.py:934
  808.3 3.0 fusion.27
  811.3 10.2 collective-permute-done.36
  826.5 7.2 collective-permute-start.38
  840.4 3.6 fusion
  846.7 4.9 fusion.1
  851.8 29.0 %collective-permute-done.49 = bf16[768,768]{1,0:T(8,128)(2,1)} collective-permute-done((bf16[768,768]{1,0:T(8,128)(2,1)}, bf16[768,768]{1,0:T(8,128)(2,1)}, u32[]{:S(2)}, u32[]{:S(2)}) %collective-permute-start.49) | collective-permute-done | bytes 1179680 | tf_op jit(solution)/shard_map/ppermute | solution.py:720
  882.4 23.6 %collective-permute-done.40 = bf16[768,768]{1,0:T(8,128)(2,1)} collective-permute-done((bf16[768,768]{1,0:T(8,128)(2,1)}, bf16[768,768]{1,0:T(8,128)(2,1)}, u32[]{:S(2)}, u32[]{:S(2)}) %collective-permute-start.40) | collective-permute-done | bytes 1179680 | tf_op jit(solution)/shard_map/ppermute | solution.py:720
  911.5 7.2 collective-permute-done.50
  919.0 12.3 collective-permute-done.41
  931.5 25.0 %collective-permute-done.67 = bf16[1536,768]{1,0:T(8,128)(2,1)} collective-permute-done((bf16[1536,768]{1,0:T(8,128)(2,1)}, bf16[1536,768]{1,0:T(8,128)(2,1)}, u32[]{:S(2)}, u32[]{:S(2)}) %collective-permute-start.67) | collective-permute-done | bytes 2359328 | tf_op jit(solution)/shard_map/ppermute | solution.py:720
  959.1 47.9 %collective-permute-done.58 = bf16[1536,768]{1,0:T(8,128)(2,1)S(1)} collective-permute-done((bf16[1536,768]{1,0:T(8,128)(2,1)S(1)}, bf16[1536,768]{1,0:T(8,128)(2,1)S(1)}, u32[]{:S(2)}, u32[]{:S(2)}) %collective-permute-start.58) | collective-permute-done | bytes 2359328 | tf_op jit(solution)/shard_map/ppermute | solution.py:720
  1008.2 10.7 collective-permute-done.42
  1019.6 14.5 %collective-permute-done.59 = bf16[768,768]{1,0:T(8,128)(2,1)S(1)} collective-permute-done((bf16[768,768]{1,0:T(8,128)(2,1)S(1)}, bf16[768,768]{1,0:T(8,128)(2,1)S(1)}, u32[]{:S(2)}, u32[]{:S(2)}) %collective-permute-start.59) | collective-permute-done | bytes 1179680 | tf_op jit(solution)/shard_map/ppermute | solution.py:720
  1037.2 22.1 %collective-permute-done.60 = bf16[384,768]{1,0:T(8,128)(2,1)S(1)} collective-permute-done((bf16[384,768]{1,0:T(8,128)(2,1)S(1)}, bf16[384,768]{1,0:T(8,128)(2,1)S(1)}, u32[]{:S(2)}, u32[]{:S(2)}) %collective-permute-start.60) | collective-permute-done | bytes 589856 | tf_op jit(solution)/shard_map/ppermute | solution.py:720
  1062.3 21.9 %collective-permute-done.61 = bf16[192,768]{1,0:T(8,128)(2,1)S(1)} collective-permute-done((bf16[192,768]{1,0:T(8,128)(2,1)S(1)}, bf16[192,768]{1,0:T(8,128)(2,1)S(1)}, u32[]{:S(2)}, u32[]{:S(2)}) %collective-permute-start.61) | collective-permute-done | bytes 294944 | tf_op jit(solution)/shard_map/ppermute | solution.py:720
  1084.5 9.1 collective-permute-done.44
  1093.7 6.3 collective-permute-done.71
  1101.0 5.3 collective-permute-done.62
  1109.6 4.8 gather_fusion.12
  1114.4 4.9 gather_fusion.14
  1130.3 5.9 collective-permute-start.73
  1142.8 7.1 broadcast_select_fusion
  1149.9 4.8 gather_fusion.15
  1161.6 4.3 fusion.35
  1169.0 4.0 fusion.36
  1173.0 3.1 collective-permute-start.65
  1176.1 3.7 fusion.10
  1179.8 4.9 gather_fusion.13
  1184.7 6.3 fusion.8
  1191.0 3.1 fusion.12
  1198.6 8.6 fusion.3
  1207.2 3.1 slice_bitcast_fusion
  1210.3 5.8 copy.125
  1216.2 7.0 broadcast_in_dim_reshape.14
  1223.2 6.0 copy.126
  (514 shorter events, 192.6 us)
Async XLA Ops:
  7.2 786.9 %all-reduce.3.cloned.1.call-start = ((), (), s32[]{:S(2)}) async-start(), calls=%async_computation | async-start | bytes 147456 | tf_op jit(solution)/shard_map/psum | solution.py:934
  12.3 94.7 %collective-permute-start.2 = (bf16[768,768]{1,0:T(8,128)(2,1)S(1)}, bf16[768,768]{1,0:T(8,128)(2,1)}, u32[]{:S(2)}, u32[]{:S(2)}) collective-permute-start(bf16[768,768]{1,0:T(8,128)(2,1)S(1)} %bitcast.249), channel_id=1, source_target_pairs={{0,1},{1,0},{2,3},{3,2},{4,5},{5,4},{6,7},{7,6},{8,9},{9,8},{10,11... | collective-permute-start | bytes 3538952 | tf_op jit(solution)/shard_map/ppermute | solution.py:720
  12.3 102.6 %collective-permute-start.4 = (bf16[768,768]{1,0:T(8,128)(2,1)S(1)}, bf16[768,768]{1,0:T(8,128)(2,1)}, u32[]{:S(2)}, u32[]{:S(2)}) collective-permute-start(bf16[768,768]{1,0:T(8,128)(2,1)S(1)} %bitcast.250), channel_id=1, source_target_pairs={{0,16},{1,17},{2,18},{3,19},{4,20},{5,21},{6,22},{7,23},{8,24},{9,... | collective-permute-start | bytes 3538952 | tf_op jit(solution)/shard_map/ppermute | solution.py:720
  20.5 29.1 %collective-permute-start.1 = (f32[9216]{0:T(1024)}, f32[9216]{0:T(1024)}, u32[]{:S(2)}, u32[]{:S(2)}) collective-permute-start(f32[9216]{0:T(1024)} %constant_dynamic-update-slice_fusion), channel_id=1, source_target_pairs={{0,16},{1,17},{2,18},{3,19},{4,20},{5,21},{6,22},{7,23},{8,24},{9,... | collective-permute-start | bytes 110600 | tf_op jit(solution)/shard_map/ppermute | solution.py:720
  23.4 44.7 %collective-permute-start = (bf16[640,768]{1,0:T(8,128)(2,1)}, bf16[640,768]{1,0:T(8,128)(2,1)}, u32[]{:S(2)}, u32[]{:S(2)}) collective-permute-start(bf16[640,768]{1,0:T(8,128)(2,1)} %get-tuple-element.143), channel_id=1, source_target_pairs={{0,1},{1,0},{2,3},{3,2},{4,5},{5,4},{6,7},{7,6},{8,9},{9,8},{10,11... | collective-permute-start | bytes 2949128 | tf_op jit(solution)/shard_map/ppermute | solution.py:720
  36.0 81.0 %collective-permute-start.10 = (bf16[768,768]{1,0:T(8,128)(2,1)}, bf16[768,768]{1,0:T(8,128)(2,1)}, u32[]{:S(2)}, u32[]{:S(2)}) collective-permute-start(bf16[768,768]{1,0:T(8,128)(2,1)} %bitcast.222), channel_id=1, source_target_pairs={{0,1},{1,0},{2,3},{3,2},{4,5},{5,4},{6,7},{7,6},{8,9},{9,8},{10,11... | collective-permute-start | bytes 3538952 | tf_op jit(solution)/shard_map/ppermute | solution.py:720
  49.5 57.1 %collective-permute-start.32 = (bf16[640,768]{1,0:T(8,128)(2,1)}, bf16[640,768]{1,0:T(8,128)(2,1)}, u32[]{:S(2)}, u32[]{:S(2)}) collective-permute-start(bf16[640,768]{1,0:T(8,128)(2,1)} %get-tuple-element.141), channel_id=1, source_target_pairs={{0,1},{1,0},{2,3},{3,2},{4,5},{5,4},{6,7},{7,6},{8,9},{9,8},{10,11... | collective-permute-start | bytes 2949128 | tf_op jit(solution)/shard_map/ppermute | solution.py:720
  68.0 53.5 %collective-permute-start.14 = (bf16[768,768]{1,0:T(8,128)(2,1)}, bf16[768,768]{1,0:T(8,128)(2,1)S(1)}, u32[]{:S(2)}, u32[]{:S(2)}) collective-permute-start(bf16[768,768]{1,0:T(8,128)(2,1)} %bitcast.222), channel_id=1, source_target_pairs={{0,16},{1,17},{2,18},{3,19},{4,20},{5,21},{6,22},{7,23},{8,24},{9,... | collective-permute-start | bytes 3538952 | tf_op jit(solution)/shard_map/ppermute | solution.py:720
  106.7 26.1 %collective-permute-start.12 = (bf16[768,768]{1,0:T(8,128)(2,1)}, bf16[768,768]{1,0:T(8,128)(2,1)S(1)}, u32[]{:S(2)}, u32[]{:S(2)}) collective-permute-start(bf16[768,768]{1,0:T(8,128)(2,1)} %dynamic-slice_bitcast_fusion), channel_id=1, source_target_pairs={{0,1},{1,0},{2,3},{3,2},{4,5},{5,4},{6,7},{7,6},{8,9},{9,8},{10,11... | collective-permute-start | bytes 3538952 | tf_op jit(solution)/shard_map/ppermute | solution.py:720
  107.0 27.4 %collective-permute-start.20 = (bf16[768,768]{1,0:T(8,128)(2,1)}, bf16[768,768]{1,0:T(8,128)(2,1)S(1)}, u32[]{:S(2)}, u32[]{:S(2)}) collective-permute-start(bf16[768,768]{1,0:T(8,128)(2,1)} %dynamic-slice_bitcast_fusion), channel_id=1, source_target_pairs={{0,16},{1,17},{2,18},{3,19},{4,20},{5,21},{6,22},{7,23},{8,24},{9,... | collective-permute-start | bytes 3538952 | tf_op jit(solution)/shard_map/ppermute | solution.py:720
  114.9 33.0 %collective-permute-start.5 = (bf16[768,768]{1,0:T(8,128)(2,1)}, bf16[768,768]{1,0:T(8,128)(2,1)S(1)}, u32[]{:S(2)}, u32[]{:S(2)}) collective-permute-start(bf16[768,768]{1,0:T(8,128)(2,1)} %collective-permute-done.4), channel_id=1, source_target_pairs={{0,2},{1,3},{2,0},{3,1},{4,6},{5,7},{6,4},{7,5},{8,10},{9,11},{10,... | collective-permute-start | bytes 3538952 | tf_op jit(solution)/shard_map/ppermute | solution.py:720
  117.0 34.2 %collective-permute-start.3 = (bf16[768,768]{1,0:T(8,128)(2,1)}, bf16[768,768]{1,0:T(8,128)(2,1)S(1)}, u32[]{:S(2)}, u32[]{:S(2)}) collective-permute-start(bf16[768,768]{1,0:T(8,128)(2,1)} %collective-permute-done.2), channel_id=1, source_target_pairs={{0,2},{1,3},{2,0},{3,1},{4,6},{5,7},{6,4},{7,5},{8,10},{9,11},{10,... | collective-permute-start | bytes 3538952 | tf_op jit(solution)/shard_map/ppermute | solution.py:720
  121.6 24.2 %collective-permute-start.6 = (bf16[384,768]{1,0:T(8,128)(2,1)S(1)}, bf16[384,768]{1,0:T(8,128)(2,1)S(1)}, u32[]{:S(2)}, u32[]{:S(2)}) collective-permute-start(bf16[384,768]{1,0:T(8,128)(2,1)S(1)} %get-tuple-element.205.rest_4_), channel_id=1, source_target_pairs={{0,16},{1,17},{2,18},{3,19},{4,20},{5,21},{6,22},{7,23},{8,24},{9,... | collective-permute-start | bytes 1769480 | tf_op jit(solution)/shard_map/ppermute | solution.py:720
  134.4 30.2 %collective-permute-start.15 = (bf16[768,768]{1,0:T(8,128)(2,1)S(1)}, bf16[768,768]{1,0:T(8,128)(2,1)S(1)}, u32[]{:S(2)}, u32[]{:S(2)}) collective-permute-start(bf16[768,768]{1,0:T(8,128)(2,1)S(1)} %collective-permute-done.14), channel_id=1, source_target_pairs={{0,2},{1,3},{2,0},{3,1},{4,6},{5,7},{6,4},{7,5},{8,10},{9,11},{10,... | collective-permute-start | bytes 3538952 | tf_op jit(solution)/shard_map/ppermute | solution.py:720
  158.2 54.7 %collective-permute-start.22 = (bf16[384,768]{1,0:T(8,128)(2,1)}, bf16[384,768]{1,0:T(8,128)(2,1)}, u32[]{:S(2)}, u32[]{:S(2)}) collective-permute-start(bf16[384,768]{1,0:T(8,128)(2,1)} %get-tuple-element.189.rest_12_), channel_id=1, source_target_pairs={{0,16},{1,17},{2,18},{3,19},{4,20},{5,21},{6,22},{7,23},{8,24},{9,... | collective-permute-start | bytes 1769480 | tf_op jit(solution)/shard_map/ppermute | solution.py:720
  158.7 55.0 %collective-permute-start.23 = (bf16[384,768]{1,0:T(8,128)(2,1)S(1)}, bf16[384,768]{1,0:T(8,128)(2,1)}, u32[]{:S(2)}, u32[]{:S(2)}) collective-permute-start(bf16[384,768]{1,0:T(8,128)(2,1)S(1)} %get-tuple-element.180.rest_25_), channel_id=1, source_target_pairs={{0,1},{1,0},{2,3},{3,2},{4,5},{5,4},{6,7},{7,6},{8,9},{9,8},{10,11... | collective-permute-start | bytes 1769480 | tf_op jit(solution)/shard_map/ppermute | solution.py:720
  160.0 54.1 %collective-permute-start.11 = (bf16[768,768]{1,0:T(8,128)(2,1)}, bf16[768,768]{1,0:T(8,128)(2,1)S(1)}, u32[]{:S(2)}, u32[]{:S(2)}) collective-permute-start(bf16[768,768]{1,0:T(8,128)(2,1)} %collective-permute-done.10), channel_id=1, source_target_pairs={{0,2},{1,3},{2,0},{3,1},{4,6},{5,7},{6,4},{7,5},{8,10},{9,11},{10,... | collective-permute-start | bytes 3538952 | tf_op jit(solution)/shard_map/ppermute | solution.py:720
  164.5 49.7 %collective-permute-start.21 = (bf16[768,768]{1,0:T(8,128)(2,1)S(1)}, bf16[768,768]{1,0:T(8,128)(2,1)S(1)}, u32[]{:S(2)}, u32[]{:S(2)}) collective-permute-start(bf16[768,768]{1,0:T(8,128)(2,1)S(1)} %collective-permute-done.20), channel_id=1, source_target_pairs={{0,2},{1,3},{2,0},{3,1},{4,6},{5,7},{6,4},{7,5},{8,10},{9,11},{10,... | collective-permute-start | bytes 3538952 | tf_op jit(solution)/shard_map/ppermute | solution.py:720
  164.6 52.3 %collective-permute-start.13 = (bf16[768,768]{1,0:T(8,128)(2,1)S(1)}, bf16[768,768]{1,0:T(8,128)(2,1)S(1)}, u32[]{:S(2)}, u32[]{:S(2)}) collective-permute-start(bf16[768,768]{1,0:T(8,128)(2,1)S(1)} %collective-permute-done.12), channel_id=1, source_target_pairs={{0,2},{1,3},{2,0},{3,1},{4,6},{5,7},{6,4},{7,5},{8,10},{9,11},{10,... | collective-permute-start | bytes 3538952 | tf_op jit(solution)/shard_map/ppermute | solution.py:720
  630.4 29.9 %collective-permute-start.26 = (bf16[640,768]{1,0:T(8,128)(2,1)}, bf16[640,768]{1,0:T(8,128)(2,1)}, u32[]{:S(2)}, u32[]{:S(2)}) collective-permute-start(bf16[640,768]{1,0:T(8,128)(2,1)} %get-tuple-element.172), channel_id=1, source_target_pairs={{0,1},{1,0},{2,3},{3,2},{4,5},{5,4},{6,7},{7,6},{8,9},{9,8},{10,11... | collective-permute-start | bytes 2949128 | tf_op jit(solution)/shard_map/ppermute | solution.py:720
  632.5 67.5 %collective-permute-start.30 = (bf16[640,768]{1,0:T(8,128)(2,1)}, bf16[640,768]{1,0:T(8,128)(2,1)}, u32[]{:S(2)}, u32[]{:S(2)}) collective-permute-start(bf16[640,768]{1,0:T(8,128)(2,1)} %get-tuple-element.172), channel_id=1, source_target_pairs={{16,1},{17,0},{18,3},{19,2},{20,5},{21,4},{22,7},{23,6},{24,9},{25... | collective-permute-start | bytes 2949128 | tf_op jit(solution)/shard_map/ppermute | solution.py:720
  645.5 17.9 %collective-permute-start.27 = (bf16[640,768]{1,0:T(8,128)(2,1)}, bf16[640,768]{1,0:T(8,128)(2,1)}, u32[]{:S(2)}, u32[]{:S(2)}) collective-permute-start(bf16[640,768]{1,0:T(8,128)(2,1)} %get-tuple-element.173), channel_id=1, source_target_pairs={{16,17},{17,16},{18,19},{19,18},{20,21},{21,20},{22,23},{23,22},{2... | collective-permute-start | bytes 2949128 | tf_op jit(solution)/shard_map/ppermute | solution.py:720
  647.2 32.2 %collective-permute-start.28 = (bf16[640,768]{1,0:T(8,128)(2,1)S(1)}, bf16[640,768]{1,0:T(8,128)(2,1)}, u32[]{:S(2)}, u32[]{:S(2)}) collective-permute-start(bf16[640,768]{1,0:T(8,128)(2,1)S(1)} %get-tuple-element.133), channel_id=1, source_target_pairs={{16,0},{17,1},{18,2},{19,3},{20,4},{21,5},{22,6},{23,7},{24,8},{25... | collective-permute-start | bytes 2949128 | tf_op jit(solution)/shard_map/ppermute | solution.py:720
  648.5 49.6 %collective-permute-start.29 = (bf16[640,768]{1,0:T(8,128)(2,1)S(1)}, bf16[640,768]{1,0:T(8,128)(2,1)}, u32[]{:S(2)}, u32[]{:S(2)}) collective-permute-start(bf16[640,768]{1,0:T(8,128)(2,1)S(1)} %get-tuple-element.132), channel_id=1, source_target_pairs={{0,16},{1,17},{2,18},{3,19},{4,20},{5,21},{6,22},{7,23},{8,24},{9,... | collective-permute-start | bytes 2949128 | tf_op jit(solution)/shard_map/ppermute | solution.py:720
  660.3 44.7 %collective-permute-start.31 = (bf16[640,768]{1,0:T(8,128)(2,1)}, bf16[640,768]{1,0:T(8,128)(2,1)}, u32[]{:S(2)}, u32[]{:S(2)}) collective-permute-start(bf16[640,768]{1,0:T(8,128)(2,1)} %get-tuple-element.173), channel_id=1, source_target_pairs={{0,17},{1,16},{2,19},{3,18},{4,21},{5,20},{6,23},{7,22},{8,25},{9,... | collective-permute-start | bytes 2949128 | tf_op jit(solution)/shard_map/ppermute | solution.py:720
  663.4 176.6 %collective-permute-start.66 = (bf16[2,1536,768]{2,1,0:T(8,128)(2,1)}, bf16[2,1536,768]{2,1,0:T(8,128)(2,1)}, u32[]{:S(2)}, u32[]{:S(2)}) collective-permute-start(bf16[2,1536,768]{2,1,0:T(8,128)(2,1)} %slice_bitcast_fusion.2), channel_id=1, source_target_pairs={{0,2},{1,3},{2,0},{3,1},{4,6},{5,7},{6,4},{7,5},{8,10},{9,11},{10,... | collective-permute-start | bytes 14155784 | tf_op jit(solution)/shard_map/ppermute | solution.py:720
  679.4 120.9 %collective-permute-start.35 = (bf16[640,768]{1,0:T(8,128)(2,1)}, bf16[640,768]{1,0:T(8,128)(2,1)S(1)}, u32[]{:S(2)}, u32[]{:S(2)}) collective-permute-start(bf16[640,768]{1,0:T(8,128)(2,1)} %get-tuple-element.130), channel_id=1, source_target_pairs={{16,0},{17,1},{18,2},{19,3},{20,4},{21,5},{22,6},{23,7},{24,8},{25... | collective-permute-start | bytes 2949128 | tf_op jit(solution)/shard_map/ppermute | solution.py:720
  698.1 99.8 %collective-permute-start.33 = (bf16[640,768]{1,0:T(8,128)(2,1)}, bf16[640,768]{1,0:T(8,128)(2,1)}, u32[]{:S(2)}, u32[]{:S(2)}) collective-permute-start(bf16[640,768]{1,0:T(8,128)(2,1)} %get-tuple-element.164), channel_id=1, source_target_pairs={{0,1},{1,0},{2,3},{3,2},{4,5},{5,4},{6,7},{7,6},{8,9},{9,8},{10,11... | collective-permute-start | bytes 2949128 | tf_op jit(solution)/shard_map/ppermute | solution.py:720
  700.0 100.1 %collective-permute-start.34 = (bf16[640,768]{1,0:T(8,128)(2,1)}, bf16[640,768]{1,0:T(8,128)(2,1)}, u32[]{:S(2)}, u32[]{:S(2)}) collective-permute-start(bf16[640,768]{1,0:T(8,128)(2,1)} %get-tuple-element.165), channel_id=1, source_target_pairs={{16,17},{17,16},{18,19},{19,18},{20,21},{21,20},{22,23},{23,22},{2... | collective-permute-start | bytes 2949128 | tf_op jit(solution)/shard_map/ppermute | solution.py:720
  705.0 121.6 %collective-permute-start.48 = (bf16[2,768,768]{2,1,0:T(8,128)(2,1)}, bf16[2,768,768]{2,1,0:T(8,128)(2,1)}, u32[]{:S(2)}, u32[]{:S(2)}) collective-permute-start(bf16[2,768,768]{2,1,0:T(8,128)(2,1)} %slice_bitcast_fusion.10), channel_id=1, source_target_pairs={{0,2},{1,3},{2,0},{3,1},{4,6},{5,7},{6,4},{7,5},{8,10},{9,11},{10,... | collective-permute-start | bytes 7077896 | tf_op jit(solution)/shard_map/ppermute | solution.py:720
  797.9 23.6 %collective-permute-start.36 = (bf16[640,768]{1,0:T(8,128)(2,1)S(1)}, bf16[640,768]{1,0:T(8,128)(2,1)S(1)}, u32[]{:S(2)}, u32[]{:S(2)}) collective-permute-start(bf16[640,768]{1,0:T(8,128)(2,1)S(1)} %copy-done.20), channel_id=1, source_target_pairs={{0,16},{1,17},{2,18},{3,19},{4,20},{5,21},{6,22},{7,23},{8,24},{9,... | collective-permute-start | bytes 2949128 | tf_op jit(solution)/shard_map/ppermute | solution.py:720
  800.1 45.4 %collective-permute-start.57 = (bf16[2,1536,768]{2,1,0:T(8,128)(2,1)}, bf16[2,1536,768]{2,1,0:T(8,128)(2,1)}, u32[]{:S(2)}, u32[]{:S(2)}) collective-permute-start(bf16[2,1536,768]{2,1,0:T(8,128)(2,1)} %slice_bitcast_fusion.4), channel_id=1, source_target_pairs={{0,2},{1,3},{2,0},{3,1},{4,6},{5,7},{6,4},{7,5},{8,10},{9,11},{10,... | collective-permute-start | bytes 14155784 | tf_op jit(solution)/shard_map/ppermute | solution.py:720
  800.2 37.0 %collective-permute-start.39 = (bf16[2,768,768]{2,1,0:T(8,128)(2,1)}, bf16[2,768,768]{2,1,0:T(8,128)(2,1)S(1)}, u32[]{:S(2)}, u32[]{:S(2)}) collective-permute-start(bf16[2,768,768]{2,1,0:T(8,128)(2,1)} %slice_bitcast_fusion.12), channel_id=1, source_target_pairs={{0,2},{1,3},{2,0},{3,1},{4,6},{5,7},{6,4},{7,5},{8,10},{9,11},{10,... | collective-permute-start | bytes 7077896 | tf_op jit(solution)/shard_map/ppermute | solution.py:720
  821.5 86.2 %collective-permute-start.37 = (bf16[640,768]{1,0:T(8,128)(2,1)}, bf16[640,768]{1,0:T(8,128)(2,1)}, u32[]{:S(2)}, u32[]{:S(2)}) collective-permute-start(bf16[640,768]{1,0:T(8,128)(2,1)} %get-tuple-element.164), channel_id=1, source_target_pairs={{16,1},{17,0},{18,3},{19,2},{20,5},{21,4},{22,7},{23,6},{24,9},{25... | collective-permute-start | bytes 2949128 | tf_op jit(solution)/shard_map/ppermute | solution.py:720
  826.5 82.7 %collective-permute-start.38 = (bf16[640,768]{1,0:T(8,128)(2,1)}, bf16[640,768]{1,0:T(8,128)(2,1)}, u32[]{:S(2)}, u32[]{:S(2)}) collective-permute-start(bf16[640,768]{1,0:T(8,128)(2,1)} %get-tuple-element.165), channel_id=1, source_target_pairs={{0,17},{1,16},{2,19},{3,18},{4,21},{5,20},{6,23},{7,22},{8,25},{9,... | collective-permute-start | bytes 2949128 | tf_op jit(solution)/shard_map/ppermute | solution.py:720
  837.3 43.4 %collective-permute-start.49 = (bf16[768,768]{1,0:T(8,128)(2,1)}, bf16[768,768]{1,0:T(8,128)(2,1)}, u32[]{:S(2)}, u32[]{:S(2)}) collective-permute-start(bf16[768,768]{1,0:T(8,128)(2,1)} %slice_bitcast_fusion.14), channel_id=1, source_target_pairs={{0,1},{1,0},{2,3},{3,2},{4,5},{5,4},{6,7},{7,6},{8,9},{9,8},{10,11... | collective-permute-start | bytes 3538952 | tf_op jit(solution)/shard_map/ppermute | solution.py:720
  840.0 65.9 %collective-permute-start.40 = (bf16[768,768]{1,0:T(8,128)(2,1)}, bf16[768,768]{1,0:T(8,128)(2,1)}, u32[]{:S(2)}, u32[]{:S(2)}) collective-permute-start(bf16[768,768]{1,0:T(8,128)(2,1)} %slice_bitcast_fusion.16), channel_id=1, source_target_pairs={{0,1},{1,0},{2,3},{3,2},{4,5},{5,4},{6,7},{7,6},{8,9},{9,8},{10,11... | collective-permute-start | bytes 3538952 | tf_op jit(solution)/shard_map/ppermute | solution.py:720
  845.6 111.0 %collective-permute-start.67 = (bf16[1536,768]{1,0:T(8,128)(2,1)}, bf16[1536,768]{1,0:T(8,128)(2,1)}, u32[]{:S(2)}, u32[]{:S(2)}) collective-permute-start(bf16[1536,768]{1,0:T(8,128)(2,1)} %slice_bitcast_fusion.6), channel_id=1, source_target_pairs={{0,1},{1,0},{2,3},{3,2},{4,5},{5,4},{6,7},{7,6},{8,9},{9,8},{10,11... | collective-permute-start | bytes 7077896 | tf_op jit(solution)/shard_map/ppermute | solution.py:720
  880.7 126.3 %collective-permute-start.58 = (bf16[1536,768]{1,0:T(8,128)(2,1)S(1)}, bf16[1536,768]{1,0:T(8,128)(2,1)S(1)}, u32[]{:S(2)}, u32[]{:S(2)}) collective-permute-start(bf16[1536,768]{1,0:T(8,128)(2,1)S(1)} %slice_bitcast_fusion.8), channel_id=1, source_target_pairs={{0,1},{1,0},{2,3},{3,2},{4,5},{5,4},{6,7},{7,6},{8,9},{9,8},{10,11... | collective-permute-start | bytes 7077896 | tf_op jit(solution)/shard_map/ppermute | solution.py:720
  907.7 23.7 %collective-permute-start.41 = (bf16[384,768]{1,0:T(8,128)(2,1)S(1)}, bf16[384,768]{1,0:T(8,128)(2,1)S(1)}, u32[]{:S(2)}, u32[]{:S(2)}) collective-permute-start(bf16[384,768]{1,0:T(8,128)(2,1)S(1)} %constant_dynamic-slice_fusion.10), channel_id=1, source_target_pairs={{0,16},{1,17},{2,18},{3,19},{4,20},{5,21},{6,22},{7,23},{8,24},{9,... | collective-permute-start | bytes 1769480 | tf_op jit(solution)/shard_map/ppermute | solution.py:720
  918.9 89.1 %collective-permute-start.51 = (bf16[192,768]{1,0:T(8,128)(2,1)S(1)}, bf16[192,768]{1,0:T(8,128)(2,1)S(1)}, u32[]{:S(2)}, u32[]{:S(2)}) collective-permute-start(bf16[192,768]{1,0:T(8,128)(2,1)S(1)} %constant_dynamic-slice_fusion.6), channel_id=1, source_target_pairs={{0,4},{1,5},{2,6},{3,7},{4,0},{5,1},{6,2},{7,3},{8,12},{9,13},{10,... | collective-permute-start | bytes 884744 | tf_op jit(solution)/shard_map/ppermute | solution.py:720
  959.0 60.1 %collective-permute-start.68 = (bf16[768,768]{1,0:T(8,128)(2,1)S(1)}, bf16[768,768]{1,0:T(8,128)(2,1)S(1)}, u32[]{:S(2)}, u32[]{:S(2)}) collective-permute-start(bf16[768,768]{1,0:T(8,128)(2,1)S(1)} %constant_dynamic-slice_fusion.1), channel_id=1, source_target_pairs={{0,16},{1,17},{2,18},{3,19},{4,20},{5,21},{6,22},{7,23},{8,24},{9,... | collective-permute-start | bytes 3538952 | tf_op jit(solution)/shard_map/ppermute | solution.py:720
  1007.8 26.2 %collective-permute-start.59 = (bf16[768,768]{1,0:T(8,128)(2,1)S(1)}, bf16[768,768]{1,0:T(8,128)(2,1)S(1)}, u32[]{:S(2)}, u32[]{:S(2)}) collective-permute-start(bf16[768,768]{1,0:T(8,128)(2,1)S(1)} %constant_dynamic-slice_fusion.4), channel_id=1, source_target_pairs={{0,16},{1,17},{2,18},{3,19},{4,20},{5,21},{6,22},{7,23},{8,24},{9,... | collective-permute-start | bytes 3538952 | tf_op jit(solution)/shard_map/ppermute | solution.py:720
  1008.1 26.3 %collective-permute-start.52 = (bf16[96,768]{1,0:T(8,128)(2,1)S(1)}, bf16[96,768]{1,0:T(8,128)(2,1)S(1)}, u32[]{:S(2)}, u32[]{:S(2)}) collective-permute-start(bf16[96,768]{1,0:T(8,128)(2,1)S(1)} %constant_dynamic-slice_fusion.5), channel_id=1, source_target_pairs={{0,8},{1,9},{2,10},{3,11},{4,12},{5,13},{6,14},{7,15},{8,0},{9,1},... | collective-permute-start | bytes 442376 | tf_op jit(solution)/shard_map/ppermute | solution.py:720
  1019.0 40.6 %collective-permute-start.43 = (bf16[96,768]{1,0:T(8,128)(2,1)S(1)}, bf16[96,768]{1,0:T(8,128)(2,1)S(1)}, u32[]{:S(2)}, u32[]{:S(2)}) collective-permute-start(bf16[96,768]{1,0:T(8,128)(2,1)S(1)} %constant_dynamic-slice_fusion.8), channel_id=1, source_target_pairs={{0,8},{1,9},{2,10},{3,11},{4,12},{5,13},{6,14},{7,15},{8,0},{9,1},... | collective-permute-start | bytes 442376 | tf_op jit(solution)/shard_map/ppermute | solution.py:720
  1034.4 25.0 %collective-permute-start.60 = (bf16[384,768]{1,0:T(8,128)(2,1)S(1)}, bf16[384,768]{1,0:T(8,128)(2,1)S(1)}, u32[]{:S(2)}, u32[]{:S(2)}) collective-permute-start(bf16[384,768]{1,0:T(8,128)(2,1)S(1)} %constant_dynamic-slice_fusion.3), channel_id=1, source_target_pairs={{0,4},{1,5},{2,6},{3,7},{4,0},{5,1},{6,2},{7,3},{8,12},{9,13},{10,... | collective-permute-start | bytes 1769480 | tf_op jit(solution)/shard_map/ppermute | solution.py:720
  1034.5 49.9 %collective-permute-start.53 = (bf16[96,768]{1,0:T(8,128)(2,1)S(1)}, bf16[96,768]{1,0:T(8,128)(2,1)S(1)}, u32[]{:S(2)}, u32[]{:S(2)}) collective-permute-start(bf16[96,768]{1,0:T(8,128)(2,1)S(1)} %add_convert_fusion.10), channel_id=1, source_target_pairs={{0,8},{1,9},{2,10},{3,11},{4,12},{5,13},{6,14},{7,15},{8,0},{9,1},... | collective-permute-start | bytes 442376 | tf_op jit(solution)/shard_map/ppermute | solution.py:720
  1036.7 25.4 %collective-permute-start.70 = (bf16[192,768]{1,0:T(8,128)(2,1)S(1)}, bf16[192,768]{1,0:T(8,128)(2,1)S(1)}, u32[]{:S(2)}, u32[]{:S(2)}) collective-permute-start(bf16[192,768]{1,0:T(8,128)(2,1)S(1)} %constant_dynamic-slice_fusion.21), channel_id=1, source_target_pairs={{0,8},{1,9},{2,10},{3,11},{4,12},{5,13},{6,14},{7,15},{8,0},{9,1},... | collective-permute-start | bytes 884744 | tf_op jit(solution)/shard_map/ppermute | solution.py:720
  1059.5 24.7 %collective-permute-start.61 = (bf16[192,768]{1,0:T(8,128)(2,1)S(1)}, bf16[192,768]{1,0:T(8,128)(2,1)S(1)}, u32[]{:S(2)}, u32[]{:S(2)}) collective-permute-start(bf16[192,768]{1,0:T(8,128)(2,1)S(1)} %constant_dynamic-slice_fusion.2), channel_id=1, source_target_pairs={{0,8},{1,9},{2,10},{3,11},{4,12},{5,13},{6,14},{7,15},{8,0},{9,1},... | collective-permute-start | bytes 884744 | tf_op jit(solution)/shard_map/ppermute | solution.py:720
  1059.7 33.9 %collective-permute-start.44 = (bf16[96,768]{1,0:T(8,128)(2,1)S(1)}, bf16[96,768]{1,0:T(8,128)(2,1)S(1)}, u32[]{:S(2)}, u32[]{:S(2)}) collective-permute-start(bf16[96,768]{1,0:T(8,128)(2,1)S(1)} %add_convert_fusion.11), channel_id=1, source_target_pairs={{0,8},{1,9},{2,10},{3,11},{4,12},{5,13},{6,14},{7,15},{8,0},{9,1},... | collective-permute-start | bytes 442376 | tf_op jit(solution)/shard_map/ppermute | solution.py:720
  1062.2 37.8 %collective-permute-start.71 = (bf16[192,768]{1,0:T(8,128)(2,1)S(1)}, bf16[192,768]{1,0:T(8,128)(2,1)S(1)}, u32[]{:S(2)}, u32[]{:S(2)}) collective-permute-start(bf16[192,768]{1,0:T(8,128)(2,1)S(1)} %add_convert_fusion.6), channel_id=1, source_target_pairs={{0,8},{1,9},{2,10},{3,11},{4,12},{5,13},{6,14},{7,15},{8,0},{9,1},... | collective-permute-start | bytes 884744 | tf_op jit(solution)/shard_map/ppermute | solution.py:720
  1084.3 22.0 %collective-permute-start.62 = (bf16[192,768]{1,0:T(8,128)(2,1)S(1)}, bf16[192,768]{1,0:T(8,128)(2,1)S(1)}, u32[]{:S(2)}, u32[]{:S(2)}) collective-permute-start(bf16[192,768]{1,0:T(8,128)(2,1)S(1)} %add_convert_fusion.7), channel_id=1, source_target_pairs={{0,8},{1,9},{2,10},{3,11},{4,12},{5,13},{6,14},{7,15},{8,0},{9,1},... | collective-permute-start | bytes 884744 | tf_op jit(solution)/shard_map/ppermute | solution.py:720
  1084.5 34.9 %collective-permute-start.54 = (bf16[192,768]{1,0:T(8,128)(2,1)S(1)}, bf16[192,768]{1,0:T(8,128)(2,1)}, u32[]{:S(2)}, u32[]{:S(2)}) collective-permute-start(bf16[192,768]{1,0:T(8,128)(2,1)S(1)} %maximum_select_fusion.15), channel_id=1, source_target_pairs={{0,4},{1,5},{2,6},{3,7},{4,0},{5,1},{6,2},{7,3},{8,12},{9,13},{10,... | collective-permute-start | bytes 884744 | tf_op jit(solution)/shard_map/ppermute | solution.py:720
  1093.7 30.5 %collective-permute-start.45 = (bf16[192,768]{1,0:T(8,128)(2,1)S(1)}, bf16[192,768]{1,0:T(8,128)(2,1)}, u32[]{:S(2)}, u32[]{:S(2)}) collective-permute-start(bf16[192,768]{1,0:T(8,128)(2,1)S(1)} %maximum_select_fusion.14), channel_id=1, source_target_pairs={{0,4},{1,5},{2,6},{3,7},{4,0},{5,1},{6,2},{7,3},{8,12},{9,13},{10,... | collective-permute-start | bytes 884744 | tf_op jit(solution)/shard_map/ppermute | solution.py:720
  1101.0 26.2 %collective-permute-start.72 = (bf16[384,768]{1,0:T(8,128)(2,1)}, bf16[384,768]{1,0:T(8,128)(2,1)}, u32[]{:S(2)}, u32[]{:S(2)}) collective-permute-start(bf16[384,768]{1,0:T(8,128)(2,1)} %maximum_select_fusion.13), channel_id=1, source_target_pairs={{0,4},{1,5},{2,6},{3,7},{4,0},{5,1},{6,2},{7,3},{8,12},{9,13},{10,... | collective-permute-start | bytes 1769480 | tf_op jit(solution)/shard_map/ppermute | solution.py:720
  1107.3 31.2 %collective-permute-start.63 = (bf16[384,768]{1,0:T(8,128)(2,1)}, bf16[384,768]{1,0:T(8,128)(2,1)}, u32[]{:S(2)}, u32[]{:S(2)}) collective-permute-start(bf16[384,768]{1,0:T(8,128)(2,1)} %maximum_select_fusion.12), channel_id=1, source_target_pairs={{0,4},{1,5},{2,6},{3,7},{4,0},{5,1},{6,2},{7,3},{8,12},{9,13},{10,... | collective-permute-start | bytes 1769480 | tf_op jit(solution)/shard_map/ppermute | solution.py:720
  1121.5 33.2 %collective-permute-start.55 = (bf16[384,768]{1,0:T(8,128)(2,1)}, bf16[384,768]{1,0:T(8,128)(2,1)}, u32[]{:S(2)}, u32[]{:S(2)}) collective-permute-start(bf16[384,768]{1,0:T(8,128)(2,1)} %maximum_select_fusion.11), channel_id=1, source_target_pairs={{0,16},{1,17},{2,18},{3,19},{4,20},{5,21},{6,22},{7,23},{8,24},{9,... | collective-permute-start | bytes 1769480 | tf_op jit(solution)/shard_map/ppermute | solution.py:720
  1125.7 33.6 %collective-permute-start.46 = (bf16[384,768]{1,0:T(8,128)(2,1)S(1)}, bf16[384,768]{1,0:T(8,128)(2,1)}, u32[]{:S(2)}, u32[]{:S(2)}) collective-permute-start(bf16[384,768]{1,0:T(8,128)(2,1)S(1)} %maximum_select_fusion.10), channel_id=1, source_target_pairs={{16,0},{17,1},{18,2},{19,3},{20,4},{21,5},{22,6},{23,7},{24,8},{25... | collective-permute-start | bytes 1769480 | tf_op jit(solution)/shard_map/ppermute | solution.py:720
  1130.3 31.3 %collective-permute-start.73 = (bf16[768,768]{1,0:T(8,128)(2,1)}, bf16[768,768]{1,0:T(8,128)(2,1)}, u32[]{:S(2)}, u32[]{:S(2)}) collective-permute-start(bf16[768,768]{1,0:T(8,128)(2,1)} %maximum_select_fusion.9), channel_id=1, source_target_pairs={{0,16},{1,17},{2,18},{3,19},{4,20},{5,21},{6,22},{7,23},{8,24},{9,... | collective-permute-start | bytes 3538952 | tf_op jit(solution)/shard_map/ppermute | solution.py:720
  1141.5 27.5 %collective-permute-start.64 = (bf16[768,768]{1,0:T(8,128)(2,1)}, bf16[768,768]{1,0:T(8,128)(2,1)}, u32[]{:S(2)}, u32[]{:S(2)}) collective-permute-start(bf16[768,768]{1,0:T(8,128)(2,1)} %maximum_select_fusion.8), channel_id=1, source_target_pairs={{16,0},{17,1},{18,2},{19,3},{20,4},{21,5},{22,6},{23,7},{24,8},{25... | collective-permute-start | bytes 3538952 | tf_op jit(solution)/shard_map/ppermute | solution.py:720
  1157.2 33.9 %collective-permute-start.56 = (bf16[768,768]{1,0:T(8,128)(2,1)}, bf16[768,768]{1,0:T(8,128)(2,1)}, u32[]{:S(2)}, u32[]{:S(2)}) collective-permute-start(bf16[768,768]{1,0:T(8,128)(2,1)} %get-tuple-element.175), channel_id=1, source_target_pairs={{0,2},{1,3},{2,0},{3,1},{4,6},{5,7},{6,4},{7,5},{8,10},{9,11},{10,... | collective-permute-start | bytes 3538952 | tf_op jit(solution)/shard_map/ppermute | solution.py:720
  1161.6 29.5 %collective-permute-start.47 = (bf16[768,768]{1,0:T(8,128)(2,1)}, bf16[768,768]{1,0:T(8,128)(2,1)}, u32[]{:S(2)}, u32[]{:S(2)}) collective-permute-start(bf16[768,768]{1,0:T(8,128)(2,1)} %get-tuple-element.177), channel_id=1, source_target_pairs={{0,2},{1,3},{2,0},{3,1},{4,6},{5,7},{6,4},{7,5},{8,10},{9,11},{10,... | collective-permute-start | bytes 3538952 | tf_op jit(solution)/shard_map/ppermute | solution.py:720
  1165.9 32.7 %collective-permute-start.74 = (bf16[1536,768]{1,0:T(8,128)(2,1)}, bf16[1536,768]{1,0:T(8,128)(2,1)}, u32[]{:S(2)}, u32[]{:S(2)}) collective-permute-start(bf16[1536,768]{1,0:T(8,128)(2,1)} %get-tuple-element.145), channel_id=1, source_target_pairs={{0,2},{1,3},{2,0},{3,1},{4,6},{5,7},{6,4},{7,5},{8,10},{9,11},{10,... | collective-permute-start | bytes 7077896 | tf_op jit(solution)/shard_map/ppermute | solution.py:720
  1173.0 25.6 %collective-permute-start.65 = (bf16[1536,768]{1,0:T(8,128)(2,1)}, bf16[1536,768]{1,0:T(8,128)(2,1)}, u32[]{:S(2)}, u32[]{:S(2)}) collective-permute-start(bf16[1536,768]{1,0:T(8,128)(2,1)} %get-tuple-element.147), channel_id=1, source_target_pairs={{0,2},{1,3},{2,0},{3,1},{4,6},{5,7},{6,4},{7,5},{8,10},{9,11},{10,... | collective-permute-start | bytes 7077896 | tf_op jit(solution)/shard_map/ppermute | solution.py:720
  (88 other events, 1620.2 us)
Sparse Core Ops, SparseCore 0:
  663.5 130.5 all-reduce.2

commit v2 on v0

--- a/solution.py
+++ b/solution.py
@@ -1,13 +1,1228 @@
+import functools
+import math
+
 import jax
 import jax.numpy as jnp
 from jax import lax
+from jax.experimental import pallas as pl
+from jax.experimental.pallas import tpu as pltpu
 from jax.sharding import PartitionSpec as P
 
 HEAD_DIM = 48
-
-
+IMAGE_IDS = 5
+IMAGE_MOST = 512
 EPSILON = 1e-05
 NEGATIVE = -1e30
+TILE = 128
+BLOCK = 256
+EXTRA = 16
+LOG2E = math.log2(math.e)
+SCALING = HEAD_DIM ** (-0.5)
+AXES = ("section", "dp", "tensor")
+VMEM_LIMIT = 60 * 1024 * 1024
+MESH = pl.DeviceIdType.MESH
+F32 = jnp.float32
+BF16 = jnp.bfloat16
+
+
+def nn(left, right):
+    return lax.dot_general(left, right, (((1,), (0,)), ((), ())), preferred_element_type=F32)
+
+
+def nt(left, right):
+    return lax.dot_general(left, right, (((1,), (1,)), ((), ())), preferred_element_type=F32)
+
+
+def tn(left, right):
+    return lax.dot_general(left, right, (((0,), (0,)), ((), ())), preferred_element_type=F32)
+
+
+def normalise(rows):
+    centre = rows - jnp.mean(rows, axis=-1, keepdims=True)
+    inverse = lax.rsqrt(jnp.mean(centre * centre, axis=-1, keepdims=True) + EPSILON)
+    return centre * inverse, inverse
+
+
+def normalise_back(gradient, scaled, inverse, gain):
+    upstream = gradient * gain
+    return inverse * (
+        upstream
+        - jnp.mean(upstream, axis=-1, keepdims=True)
+        - scaled * jnp.mean(upstream * scaled, axis=-1, keepdims=True)
+    )
+
+
+def gelu_pair(values):
+    share = 0.5 + 0.5 * lax.erf(values * math.sqrt(0.5))
+    bell = jnp.exp2(values * values * (-0.5 * LOG2E))
+    return values * share, share + values * bell * (1.0 / math.sqrt(2 * math.pi))
+
+
+def extra_rows(rows, width):
+    at = lax.broadcasted_iota(jnp.int32, (EXTRA, width), 0)
+    out = jnp.zeros((EXTRA, width), F32)
+    for index, row in enumerate(rows):
+        out = jnp.where(at == index, row, out)
+    return out.astype(BF16)
+
+
+def three_parts(row):
+    first = row.astype(BF16).astype(F32)
+    second = (row - first).astype(BF16).astype(F32)
+    return [first, second, row - first - second]
+
+
+def each_image(start_ref, tiles_ref, body):
+    most = IMAGE_MOST // TILE + 1
+
+    def image(index, carry):
+        first = start_ref[index]
+        tiles = tiles_ref[index]
+        for count in range(1, most + 1):
+
+            @pl.when(tiles == count)
+            def _():
+                body(index, pl.multiple_of(first * TILE, TILE), count * TILE)
+
+        return carry
+
+    lax.fori_loop(0, IMAGE_IDS, image, 0)
+
+
+def run_copies(copies):
+    for copy in copies:
+        copy.start()
+
+
+def wait_copies(copies):
+    for copy in copies:
+        copy.wait()
+
+
+def slot_of(place_ref, index):
+    return 2 * (place_ref[0] ^ (index // 2)) + (place_ref[1] ^ (index % 2))
+
+
+def once(shape):
+    zeros = (0,) * len(shape)
+    return pl.BlockSpec(shape, lambda *_: zeros, pipeline_mode=pl.Buffered(1))
+
+
+def anywhere(count):
+    return [pl.BlockSpec(memory_space=pl.ANY)] * count
+
+
+def settings(flops, collective=None):
+    remote = {} if collective is None else dict(collective_id=collective, has_side_effects=True)
+    return dict(
+        compiler_params=pltpu.CompilerParams(vmem_limit_bytes=VMEM_LIMIT, **remote),
+        cost_estimate=pl.CostEstimate(flops=flops, bytes_accessed=1_000_000, transcendentals=0),
+    )
+
+
+def blocks_of(ref, axis=0):
+    return ref.shape[axis] // BLOCK
+
+
+def block_at(index):
+    return pl.ds(pl.multiple_of(index * BLOCK, BLOCK), BLOCK)
+
+
+def big_blocks(rows):
+    size = rows // 2
+    return [slice(i * size, (i + 1) * size) for i in range(2)]
+
+
+def attend_forward_image(index, at, width, heads, seg_ref, qkv_ref, store):
+    win = pl.ds(at, width)
+    mine = seg_ref[:, win] == index
+    mask = jnp.where(mine, 0.0, NEGATIVE)
+    one = jnp.ones((1, width), F32)
+    query_extra = extra_rows([mask, one], width)
+    key_extra = extra_rows([one, mask], width)
+    value_extra = extra_rows([one], width)
+    cols = heads * HEAD_DIM
+
+    def rows_of(third, head):
+        low = third * cols + head * HEAD_DIM
+        return qkv_ref[low : low + HEAD_DIM, win]
+
+    def scores(head):
+        queries = jnp.concatenate([rows_of(0, head), query_extra], axis=0)
+        keys = jnp.concatenate([rows_of(1, head), key_extra], axis=0)
+        return tn(keys, queries)
+
+    following = scores(0)
+    for head in range(heads):
+        current = following
+        if head + 1 < heads:
+            following = scores(head + 1)
+        peak = jnp.max(current, axis=0, keepdims=True)
+        weights = jnp.exp2(current - peak).astype(BF16)
+        mixed = nn(jnp.concatenate([rows_of(2, head), value_extra], axis=0), weights)
+        total = mixed[HEAD_DIM : HEAD_DIM + 1]
+        store(head, win, mine, mixed[:HEAD_DIM] * (1.0 / total), peak + jnp.log2(total))
+
+
+def attend_backward_image(index, at, width, heads, seg_ref, qkv_ref, mixed_ref, total_ref, mixed_grad, sums):
+    win = pl.ds(at, width)
+    mine = seg_ref[:, win] == index
+    mask = jnp.where(mine, 0.0, NEGATIVE)
+    one = jnp.ones((1, width), F32)
+    key_extra = extra_rows([one, mask, one, one, one], width)
+    value_extra = extra_rows([one, one, one], width)
+    cols = heads * HEAD_DIM
+
+    def span(third, head):
+        low = third * cols + head * HEAD_DIM
+        return slice(low, low + HEAD_DIM)
+
+    def products(head):
+        own = span(0, head)
+        grads = mixed_grad[own, win]
+        inner = jnp.sum(grads.astype(F32) * mixed_ref[own, win].astype(F32), axis=0, keepdims=True)
+        query_extra = extra_rows([mask, one] + three_parts(-total_ref[head, :, win]), width)
+        grad_extra = extra_rows(three_parts(-inner), width)
+        keys = jnp.concatenate([qkv_ref[span(1, head), win], key_extra], axis=0)
+        queries = jnp.concatenate([qkv_ref[own, win], query_extra], axis=0)
+        values = jnp.concatenate([qkv_ref[span(2, head), win], value_extra], axis=0)
+        return tn(keys, queries), tn(values, jnp.concatenate([grads, grad_extra], axis=0))
+
+    following = products(0)
+    for head in range(heads):
+        scores, terms = following
+        if head + 1 < heads:
+            following = products(head + 1)
+        weights = jnp.exp2(scores)
+        score_grads = (weights * terms).astype(BF16)
+        sums[span(0, head), win] += nn(qkv_ref[span(1, head), win], score_grads) * SCALING
+        sums[span(1, head), win] += nt(qkv_ref[span(0, head), win], score_grads) * (1.0 / LOG2E)
+        sums[span(2, head), win] += nt(mixed_grad[span(0, head), win], weights.astype(BF16))
+
+
+def mixer_forward_kernel(
+    place_ref, start_ref, tiles_ref, seg_ref, hidden_ref, norm_ref, qkv_shift_ref, *rest, pieces, out_pieces, heads
+):
+    first = out_pieces in (0, pieces)
+    last = out_pieces > 0
+    rest = list(rest)
+    weights = [rest.pop(0) for _ in range(pieces)]
+    if not first:
+        normed_in = rest.pop(0)
+        mixed_before = rest.pop(0)
+    if last:
+        out_weights = [rest.pop(0) for _ in range(out_pieces)]
+        out_shift_ref = rest.pop(0)
+    qkv_ref, mixed_ref, total_ref = rest.pop(0), rest.pop(0), rest.pop(0)
+    if first:
+        normed_out = rest.pop(0)
+    if last:
+        middle_ref = rest.pop(0)
+    weight, normed, sems = rest.pop(0), rest.pop(0), rest.pop(0)
+    if last:
+        out_weight, mixed_all, out_sems = rest
+    step = pl.program_id(0)
+    cols = heads * HEAD_DIM
+    before = out_pieces - pieces if last else 0
+    copies = [
+        pltpu.make_async_copy(
+            weights[i].at[0 : 3 * cols], weight.at[i], sems.at[i]
+        )
+        for i in range(pieces)
+    ]
+    if not first:
+        norm_copy = pltpu.make_async_copy(normed_in, normed, sems.at[pieces])
+    out_copies = []
+    if last:
+        for i in range(out_pieces):
+            out_copies.append(
+                pltpu.make_async_copy(
+                    out_weights[i].at[3 * cols : 4 * cols],
+                    out_weight.at[i * cols : (i + 1) * cols],
+                    out_sems.at[i],
+                )
+            )
+        for i in range(before):
+            out_copies.append(
+                pltpu.make_async_copy(
+                    mixed_before.at[i], mixed_all.at[i * cols : (i + 1) * cols], out_sems.at[out_pieces + i]
+                )
+            )
+
+    @pl.when(step == 0)
+    def _():
+        if not first:
+            norm_copy.start()
+        run_copies(copies + out_copies)
+        if first:
+
+            def norm_block(i, carry):
+                rows = block_at(i)
+                scaled, _ = normalise(hidden_ref[rows, :].astype(F32))
+                result = (scaled * norm_ref[0:1, :] + norm_ref[1:2, :]).astype(BF16)
+                normed[rows, :] = result
+                normed_out[rows, :] = result
+                return carry
+
+            lax.fori_loop(0, blocks_of(hidden_ref), norm_block, 0)
+        else:
+            norm_copy.wait()
+
+    for index in range(pieces):
+
+        @pl.when(step == index)
+        def _():
+            copies[index].wait()
+
+    projected = nt(weight[step], normed[...]) + qkv_shift_ref[0]
+    qkv_ref[0, 0:cols, :] = (projected[0:cols] * (SCALING * LOG2E)).astype(BF16)
+    qkv_ref[0, cols : 3 * cols, :] = projected[cols : 3 * cols].astype(BF16)
+
+    def store(head, win, mine, mixed, total):
+        rows = slice(head * HEAD_DIM, (head + 1) * HEAD_DIM)
+        old = mixed_ref[0, rows, win].astype(F32)
+        mixed_ref[0, rows, win] = jnp.where(mine, mixed, old).astype(BF16)
+        total_ref[head, :, win] = jnp.where(mine, total, total_ref[head, :, win])
+
+    each_image(
+        start_ref,
+        tiles_ref,
+        lambda index, at, width: attend_forward_image(
+            index, at, width, heads, seg_ref, qkv_ref.at[0], store
+        ),
+    )
+    if last:
+        mixed_all[pl.ds(pl.multiple_of((before + step) * cols, cols), cols), :] = mixed_ref[0]
+
+        @pl.when(step == pieces - 1)
+        def _():
+            wait_copies(out_copies)
+
+            for rows in big_blocks(hidden_ref.shape[0]):
+                branch = tn(mixed_all[:, rows], out_weight[...])
+                middle_ref[rows, :] = hidden_ref[rows, :].astype(F32) + branch + out_shift_ref[...]
+
+
+def mixer_forward(images, hidden, norm, qkv_shift, pieces, offset=0, before=None, out_pieces=(), out_shift=None):
+    rows, width = hidden.shape
+    count = len(pieces)
+    cols = width // 4
+    heads = cols // HEAD_DIM
+    place, start, tiles, segment = images
+    operands = list(pieces)
+    outs = [
+        jax.ShapeDtypeStruct((count, 3 * cols, rows), BF16),
+        jax.ShapeDtypeStruct((count, cols, rows), BF16),
+        jax.ShapeDtypeStruct((count * heads, 1, rows), F32),
+    ]
+    scratch = [
+        pltpu.VMEM((count, 3 * cols, width), BF16),
+        pltpu.VMEM((rows, width), BF16),
+        pltpu.SemaphoreType.DMA((count + 1,)),
+    ]
+    if before is None:
+        outs.append(jax.ShapeDtypeStruct((rows, width), BF16))
+    else:
+        operands += list(before)
+    specs = anywhere(len(operands) + len(out_pieces))
+    operands += list(out_pieces)
+    if out_pieces:
+        operands.append(out_shift)
+        specs.append(once((1, width)))
+        outs.append(jax.ShapeDtypeStruct((rows, width), F32))
+        scratch += [
+            pltpu.VMEM((width, width), BF16),
+            pltpu.VMEM((width, rows), BF16),
+            pltpu.SemaphoreType.DMA((2 * len(out_pieces),)),
+        ]
+    return pl.pallas_call(
+        functools.partial(
+            mixer_forward_kernel,
+            pieces=count,
+            out_pieces=len(out_pieces),
+            heads=heads,
+        ),
+        grid_spec=pltpu.PrefetchScalarGridSpec(
+            num_scalar_prefetch=3,
+            grid=(count,),
+            in_specs=[
+                once((1, rows)),
+                once((rows, width)),
+                once((2, width)),
+                pl.BlockSpec((1, 3 * cols, 1), lambda i, place, *_: (slot_of(place, i + offset), 0, 0)),
+            ]
+            + specs,
+            out_specs=[
+                pl.BlockSpec((1, 3 * cols, rows), lambda i, *_: (i, 0, 0)),
+                pl.BlockSpec((1, cols, rows), lambda i, *_: (i, 0, 0)),
+                pl.BlockSpec((heads, 1, rows), lambda i, *_: (i, 0, 0)),
+            ]
+            + [once((rows, width))] * (len(outs) - 3),
+            scratch_shapes=scratch,
+        ),
+        out_shape=outs,
+        name="mixer_forward",
+        **settings(4_000_000_000),
+    )(place, start, tiles, segment, hidden, norm, qkv_shift, *operands)
+
+
+def feed_forward_kernel(place_ref, middle_ref, norm_ref, up_shift_ref, start_ref, *rest, pieces, offset, last):
+    ups, downs = rest[:pieces], rest[pieces : 2 * pieces]
+    out_ref, active_ref, slope_ref, up_weight, down_weight, sems = rest[2 * pieces :]
+    step = pl.program_id(0)
+    size = up_weight.shape[2]
+    copies = []
+    for i in range(pieces):
+        copies.append(
+            pltpu.make_async_copy(ups[i], up_weight.at[i], sems.at[0, i])
+        )
+        copies.append(
+            pltpu.make_async_copy(downs[i], down_weight.at[i], sems.at[1, i])
+        )
+
+    @pl.when(step == 0)
+    def _():
+        run_copies(copies)
+
+    scaled, _ = normalise(middle_ref[...])
+    normed = (scaled * norm_ref[0:1, :] + norm_ref[1:2, :]).astype(BF16)
+    total = start_ref[...] if offset else middle_ref[...] + start_ref[...]
+
+    @pl.when(step == 0)
+    def _():
+        wait_copies(copies)
+
+    def raise_by(index):
+        return nn(normed, up_weight[index]) + up_shift_ref[slot_of(place_ref, offset + index)]
+
+    following = raise_by(0)
+    for index in range(pieces):
+        raised = following
+        if index + 1 < pieces:
+            following = raise_by(index + 1)
+        part = pl.ds(index * size, size)
+        active, slope = gelu_pair(raised)
+        active = active.astype(BF16)
+        active_ref[:, part] = active
+        slope_ref[:, part] = slope.astype(BF16)
+        total = total + nn(active, down_weight[index])
+    out_ref[...] = total.astype(out_ref.dtype)
+
+
+def feed_forward(place, middle, norm, up_shift, begin, ups, downs, offset, last):
+    rows, width = middle.shape
+    pieces = len(ups)
+    size = up_shift.shape[2]
+    hidden = size * pieces
+    return pl.pallas_call(
+        functools.partial(
+            feed_forward_kernel,
+            pieces=pieces,
+            offset=offset,
+            last=last,
+        ),
+        grid_spec=pltpu.PrefetchScalarGridSpec(
+            num_scalar_prefetch=1,
+            grid=(rows // BLOCK,),
+            in_specs=[
+                pl.BlockSpec((BLOCK, width), lambda i, *_: (i, 0)),
+                once((2, width)),
+                once(up_shift.shape),
+                pl.BlockSpec((BLOCK, width), lambda i, *_: (i, 0)) if offset else once((1, width)),
+            ]
+            + anywhere(2 * pieces),
+            out_specs=[
+                pl.BlockSpec((BLOCK, width), lambda i, *_: (i, 0)),
+                pl.BlockSpec((BLOCK, hidden), lambda i, *_: (i, 0)),
+                pl.BlockSpec((BLOCK, hidden), lambda i, *_: (i, 0)),
+            ],
+            scratch_shapes=[
+                pltpu.VMEM((pieces, width, size), BF16),
+                pltpu.VMEM((pieces, size, width), BF16),
+                pltpu.SemaphoreType.DMA((2, pieces)),
+            ],
+        ),
+        out_shape=[
+            jax.ShapeDtypeStruct((rows, width), BF16 if last else F32),
+            jax.ShapeDtypeStruct((rows, hidden), BF16),
+            jax.ShapeDtypeStruct((rows, hidden), BF16),
+        ],
+        name="feed_forward",
+        **settings(4_000_000_000),
+    )(place, middle, norm, up_shift, begin, *ups, *downs)
+
+
+ORDER = (1, 3, 0, 2)
+
+
+def greet_core(step):
+    group = lax.axis_index("dp")
+    other = group + 1 - 2 * lax.rem(group, 2)
+
+    @pl.when(step == 0)
+    def _():
+        barrier = pltpu.get_barrier_semaphore()
+        pl.semaphore_signal(barrier, inc=1, device_id={"dp": other}, device_id_type=MESH)
+        pl.semaphore_wait(barrier, 1)
+
+    return other
+
+
+def sum_with_core(step, other, index, grad_of, sent, came, out_ref, send_sems, recv_sems):
+    def copy_of(slot):
+        return pltpu.make_async_remote_copy(
+            src_ref=sent.at[slot],
+            dst_ref=came.at[slot],
+            send_sem=send_sems.at[slot],
+            recv_sem=recv_sems.at[slot],
+            device_id={"dp": other},
+            device_id_type=MESH,
+        )
+
+    slot = index % 2
+    if index < 2:
+        grad_of(lambda where, value: sent.__setitem__((slot,) + where, value.astype(BF16)))
+        copy_of(slot).start()
+    else:
+        copy_of(slot).wait_recv()
+        grad_of(
+            lambda where, value: out_ref.__setitem__(
+                (0,) + where, (value + came[(slot,) + where].astype(F32)).astype(BF16)
+            )
+        )
+        copy_of(slot).wait_send()
+
+
+def feed_backward_kernel(grad_ref, middle_ref, norm_ref, *rest, columns):
+    pieces = 4
+    rest = list(rest)
+    actives = [rest.pop(0) for _ in range(pieces)]
+    slopes = [rest.pop(0) for _ in range(pieces)]
+    ups = [rest.pop(0) for _ in range(pieces)]
+    downs = [rest.pop(0) for _ in range(pieces)]
+    weight_grad_ref, up_shift_grad_ref, middle_grad_ref, small_ref = rest[:4]
+    (
+        normed_t,
+        grad_t,
+        normed_grad,
+        up_weight,
+        down_weight,
+        active,
+        slope,
+        low_grad,
+        sent,
+        came,
+        sems,
+        send_sems,
+        recv_sems,
+    ) = rest[4:]
+    step = pl.program_id(0)
+    rows_all, width = grad_ref.shape
+    size = up_weight.shape[2]
+    blocks = blocks_of(grad_ref)
+    other = greet_core(step)
+    copies = []
+    for slot, i in enumerate(ORDER):
+        own = pl.ds(columns[i] * size, size)
+        at = slot % 2
+        copies.append(
+            [
+                pltpu.make_async_copy(downs[i], down_weight.at[at], sems.at[0, at]),
+                pltpu.make_async_copy(slopes[i].at[:, own], slope.at[at], sems.at[1, at]),
+                pltpu.make_async_copy(ups[i], up_weight.at[at], sems.at[2, at]),
+                pltpu.make_async_copy(actives[i].at[:, own], active.at[at], sems.at[3, at]),
+            ]
+        )
+
+    @pl.when(step == 0)
+    def _():
+        run_copies(copies[0])
+
+        def prepare(i, carry):
+            rows = block_at(i)
+            scaled, _ = normalise(middle_ref[rows, :])
+            normed = (scaled * norm_ref[0:1, :] + norm_ref[1:2, :]).astype(BF16)
+            normed_t[:, rows] = normed.T
+            grad_t[:, rows] = grad_ref[rows, :].T
+            return carry
+
+        lax.fori_loop(0, blocks, prepare, 0)
+
+    for index in range(pieces):
+
+        @pl.when(step == index)
+        def _():
+            at = index % 2
+            wait_copies(copies[index])
+            if index + 1 < pieces:
+                run_copies(copies[index + 1])
+            shift_grad = jnp.zeros((1, size), F32)
+            for rows in big_blocks(rows_all):
+                hidden_grad = nt(grad_ref[rows, :], down_weight[at]) * slope[at, rows, :].astype(F32)
+                low = hidden_grad.astype(BF16)
+                low_grad[rows, :] = low
+                shift_grad = shift_grad + jnp.sum(hidden_grad, axis=0, keepdims=True)
+                term = nt(low, up_weight[at])
+                normed_grad[rows, :] = term if index == 0 else normed_grad[rows, :] + term
+            up_shift_grad_ref[0] = shift_grad
+
+            def grad_of(put):
+                for rows in big_blocks(width):
+                    put((0, rows, slice(None)), nn(normed_t[rows, :], low_grad[...]))
+                    put((1, rows, slice(None)), nn(grad_t[rows, :], active[at]))
+
+            sum_with_core(step, other, index, grad_of, sent, came, weight_grad_ref, send_sems, recv_sems)
+
+    @pl.when(step == pieces - 1)
+    def _():
+        def finish(i, sums):
+            rows = block_at(i)
+            scaled, inverse = normalise(middle_ref[rows, :])
+            gradient = normed_grad[rows, :]
+            upper = grad_ref[rows, :].astype(F32)
+            middle_grad = upper + normalise_back(gradient, scaled, inverse, norm_ref[0:1, :])
+            middle_grad_ref[rows, :] = middle_grad
+            terms = (gradient * scaled, gradient, middle_grad, upper)
+            return tuple(old + jnp.sum(term, axis=0, keepdims=True) for old, term in zip(sums, terms))
+
+        zero = jnp.zeros((1, width), F32)
+        sums = lax.fori_loop(0, blocks, finish, (zero, zero, zero, zero))
+        for index, row in enumerate(sums):
+            small_ref[index : index + 1, :] = row
+
+
+def tensor_slot(step):
+    return lax.max(step - 2, 0)
+
+
+def feed_backward(grad, middle, norm, actives, slopes, columns, ups, downs, collective):
+    rows, width = middle.shape
+    pieces = len(ups)
+    size = ups[0].shape[1]
+    operands = [*actives, *slopes, *ups, *downs]
+    return pl.pallas_call(
+        functools.partial(feed_backward_kernel, columns=columns),
+        grid=(pieces,),
+        in_specs=[once((rows, width)), once((rows, width)), once((2, width))] + anywhere(len(operands)),
+        out_specs=[
+            pl.BlockSpec((1, 2, width, size), lambda i: (tensor_slot(i), 0, 0, 0)),
+            pl.BlockSpec((1, 1, size), lambda i: (i, 0, 0)),
+            once((rows, width)),
+            once((4, width)),
+        ],
+        scratch_shapes=[
+            pltpu.VMEM((width, rows), BF16),
+            pltpu.VMEM((width, rows), BF16),
+            pltpu.VMEM((rows, width), F32),
+            pltpu.VMEM((2, width, size), BF16),
+            pltpu.VMEM((2, size, width), BF16),
+            pltpu.VMEM((2, rows, size), BF16),
+            pltpu.VMEM((2, rows, size), BF16),
+            pltpu.VMEM((rows, size), BF16),
+            pltpu.VMEM((2, 2, width, size), BF16),
+            pltpu.VMEM((2, 2, width, size), BF16),
+            pltpu.SemaphoreType.DMA((4, 2)),
+            pltpu.SemaphoreType.DMA((2,)),
+            pltpu.SemaphoreType.DMA((2,)),
+        ],
+        out_shape=[
+            jax.ShapeDtypeStruct((2, 2, width, size), BF16),
+            jax.ShapeDtypeStruct((pieces, 1, size), F32),
+            jax.ShapeDtypeStruct((rows, width), F32),
+            jax.ShapeDtypeStruct((4, width), F32),
+        ],
+        name="feed_backward",
+        **settings(16_000_000_000, collective),
+    )(grad, middle, norm, *operands)
+
+
+def mixer_backward_kernel(
+    start_ref, tiles_ref, seg_ref, middle_grad_ref, qkv_ref_all, *rest, saved, heads
+):
+    pieces = len(saved)
+    rest = [qkv_ref_all] + list(rest)
+    qkvs = [rest.pop(0) for _ in range(pieces)]
+    mixeds = [rest.pop(0) for _ in range(pieces)]
+    log_totals = [rest.pop(0) for _ in range(pieces)]
+    weights = [rest.pop(0) for _ in range(pieces)]
+    projected_ref, qkv_shift_grad_ref = rest[:2]
+    qkv, mixed, totals, out_weight, low_middle, mixed_grad, sums, sems = rest[2:]
+    step = pl.program_id(0)
+    cols = heads * HEAD_DIM
+    copies = []
+    for i in range(pieces):
+        at = saved[i]
+        copies.append(
+            [
+                pltpu.make_async_copy(weights[i].at[3 * cols : 4 * cols], out_weight.at[i], sems.at[0, i]),
+                pltpu.make_async_copy(qkvs[i].at[at], qkv.at[i], sems.at[1, i]),
+                pltpu.make_async_copy(mixeds[i].at[at], mixed.at[i], sems.at[2, i]),
+                pltpu.make_async_copy(
+                    log_totals[i].at[at * heads : (at + 1) * heads], totals.at[i], sems.at[3, i]
+                ),
+            ]
+        )
+
+    @pl.when(step == 0)
+    def _():
+        for group in copies:
+            run_copies(group)
+        low_middle[...] = middle_grad_ref[...].astype(BF16)
+
+    for index in range(pieces):
+
+        @pl.when(step == index)
+        def _():
+            wait_copies(copies[index])
+
+    mixed_grad[...] = nt(out_weight[step], low_middle[...]).astype(BF16)
+    sums[...] = jnp.zeros_like(sums)
+    each_image(
+        start_ref,
+        tiles_ref,
+        lambda index, at, span: attend_backward_image(
+            index, at, span, heads, seg_ref, qkv.at[step], mixed.at[step], totals.at[step], mixed_grad, sums
+        ),
+    )
+    gradient = sums[...]
+    projected_ref[0] = gradient.astype(BF16)
+    qkv_shift_grad_ref[0] = jnp.sum(gradient, axis=1, keepdims=True)
+
+
+def mixer_backward(images, middle_grad, qkvs, mixeds, log_totals, saved, weights):
+    rows, width = middle_grad.shape
+    count = len(weights)
+    cols = width // 4
+    heads = cols // HEAD_DIM
+    place, start, tiles, segment = images
+    operands = [*qkvs, *mixeds, *log_totals, *weights]
+    return pl.pallas_call(
+        functools.partial(mixer_backward_kernel, saved=saved, heads=heads),
+        grid_spec=pltpu.PrefetchScalarGridSpec(
+            num_scalar_prefetch=2,
+            grid=(count,),
+            in_specs=[once((1, rows)), once((rows, width))] + anywhere(len(operands)),
+            out_specs=[
+                pl.BlockSpec((1, 3 * cols, rows), lambda i, *_: (i, 0, 0)),
+                pl.BlockSpec((1, 3 * cols, 1), lambda i, *_: (i, 0, 0)),
+            ],
+            scratch_shapes=[
+                pltpu.VMEM((count, 3 * cols, rows), BF16),
+                pltpu.VMEM((count, cols, rows), BF16),
+                pltpu.VMEM((count, heads, 1, rows), F32),
+                pltpu.VMEM((count, cols, width), BF16),
+                pltpu.VMEM((rows, width), BF16),
+                pltpu.VMEM((cols, rows), BF16),
+                pltpu.VMEM((3 * cols, rows), F32),
+                pltpu.SemaphoreType.DMA((4, count)),
+            ],
+        ),
+        out_shape=[
+            jax.ShapeDtypeStruct((count, 3 * cols, rows), BF16),
+            jax.ShapeDtypeStruct((count, 3 * cols, 1), F32),
+        ],
+        name="mixer_backward",
+        **settings(16_000_000_000),
+    )(start, tiles, segment, middle_grad, *operands)
+
+
+def input_backward_kernel(hidden_ref, middle_grad_ref, norm_ref, projected, normed_in, *rest, saved):
+    pieces = len(saved)
+    rest = list(rest)
+    mixeds = [rest.pop(0) for _ in range(pieces)]
+    weights = [rest.pop(0) for _ in range(pieces)]
+    weight_grad_ref, in_grad_ref, small_ref = rest[:3]
+    projected_grad, mixed, normed, low_middle, weight, sent, came, sems, send_sems, recv_sems = rest[3:]
+    step = pl.program_id(0)
+    rows_all, width = hidden_ref.shape
+    count = projected.shape[1]
+    other = greet_core(step)
+    copies = []
+    for i in range(pieces):
+        copies.append(
+            [
+                pltpu.make_async_copy(
+                    projected.at[i], projected_grad.at[i * count : (i + 1) * count], sems.at[0, i]
+                ),
+                pltpu.make_async_copy(mixeds[i].at[saved[i]], mixed.at[i], sems.at[1, i]),
+                pltpu.make_async_copy(
+                    weights[i].at[0:count], weight.at[i * count : (i + 1) * count], sems.at[2, i]
+                ),
+            ]
+        )
+    norm_copy = pltpu.make_async_copy(normed_in, normed, sems.at[3, 0])
+
+    @pl.when(step == 0)
+    def _():
+        norm_copy.start()
+        for i in ORDER:
+            run_copies(copies[i])
+        low_middle[...] = middle_grad_ref[...].astype(BF16)
+        norm_copy.wait()
+
+    for index, piece in enumerate(ORDER):
+
+        @pl.when(step == index)
+        def _():
+            wait_copies(copies[piece])
+
+            def grad_of(put):
+                own = slice(piece * count, (piece + 1) * count)
+                put((slice(0, count), slice(None)), nn(projected_grad[own, :], normed[...]))
+                put((slice(count, width), slice(None)), nn(mixed[piece], low_middle[...]))
+
+            sum_with_core(step, other, index, grad_of, sent, came, weight_grad_ref, send_sems, recv_sems)
+
+    @pl.when(step == pieces - 1)
+    def _():
+        total = jnp.zeros((1, width), F32)
+        shift = jnp.zeros((1, width), F32)
+        for rows in big_blocks(rows_all):
+            scaled, inverse = normalise(hidden_ref[rows, :].astype(F32))
+            gradient = tn(projected_grad[:, rows], weight[...])
+            in_grad = middle_grad_ref[rows, :] + normalise_back(gradient, scaled, inverse, norm_ref[0:1, :])
+            in_grad_ref[rows, :] = in_grad.astype(BF16)
+            total = total + jnp.sum(gradient * scaled, axis=0, keepdims=True)
+            shift = shift + jnp.sum(gradient, axis=0, keepdims=True)
+        small_ref[0:1, :] = total
+        small_ref[1:2, :] = shift
+
+
+def input_backward(hidden, middle_grad, norm, projected, normed, mixeds, saved, weights, collective):
+    rows, width = hidden.shape
+    number, count, _ = projected.shape
+    operands = [projected, normed, *mixeds, *weights]
+    return pl.pallas_call(
+        functools.partial(input_backward_kernel, saved=saved),
+        grid=(number,),
+        in_specs=[once((rows, width)), once((rows, width)), once((2, width))] + anywhere(len(operands)),
+        out_specs=[
+            pl.BlockSpec((1, width, width), lambda i: (tensor_slot(i), 0, 0)),
+            once((rows, width)),
+            once((2, width)),
+        ],
+        scratch_shapes=[
+            pltpu.VMEM((number * count, rows), BF16),
+            pltpu.VMEM((number, width - count, rows), BF16),
+            pltpu.VMEM((rows, width), BF16),
+            pltpu.VMEM((rows, width), BF16),
+            pltpu.VMEM((number * count, width), BF16),
+            pltpu.VMEM((2, width, width), BF16),
+            pltpu.VMEM((2, width, width), BF16),
+            pltpu.SemaphoreType.DMA((4, number)),
+            pltpu.SemaphoreType.DMA((2,)),
+            pltpu.SemaphoreType.DMA((2,)),
+        ],
+        out_shape=[
+            jax.ShapeDtypeStruct((2, width, width), BF16),
+            jax.ShapeDtypeStruct((rows, width), BF16),
+            jax.ShapeDtypeStruct((2, width), F32),
+        ],
+        name="input_backward",
+        **settings(8_000_000_000, collective),
+    )(hidden, middle_grad, norm, *operands)
+
+
+def unpack_kernel(feed_ref, mixer_ref, qkv_ref, out_ref, up_ref, down_ref):
+    width = feed_ref.shape[2]
+    part = width // 4
+    for core in range(2):
+        up_ref[:, core * width : (core + 1) * width] = feed_ref[core, 0].astype(F32)
+        down_ref[core * width : (core + 1) * width, :] = feed_ref[core, 1].astype(F32).T
+        out_ref[core * part : (core + 1) * part, :] = mixer_ref[core, 3 * part :, :].astype(F32)
+    for third in range(3):
+        rows = slice(third * part, (third + 1) * part)
+        both = jnp.concatenate([mixer_ref[0, rows, :], mixer_ref[1, rows, :]], axis=0)
+        qkv_ref[third] = both.astype(F32).T
+
+
+def unpack(feed, mixer):
+    width = feed.shape[2]
+    half = width // 2
+    return pl.pallas_call(
+        unpack_kernel,
+        out_shape=[
+            jax.ShapeDtypeStruct((3, width, half), F32),
+            jax.ShapeDtypeStruct((half, width), F32),
+            jax.ShapeDtypeStruct((width, 2 * width), F32),
+            jax.ShapeDtypeStruct((2 * width, width), F32),
+        ],
+        name="unpack",
+        compiler_params=pltpu.CompilerParams(vmem_limit_bytes=VMEM_LIMIT),
+    )(feed, mixer)
+
+
+def route(change):
+    shape = [lax.axis_size(axis) for axis in AXES]
+    pairs = []
+    for s in range(shape[0]):
+        for d in range(shape[1]):
+            for t in range(shape[2]):
+                to = change(s, d, t)
+                if to is not None:
+                    pairs.append(((s * shape[1] + d) * shape[2] + t, (to[0] * shape[1] + to[1]) * shape[2] + to[2]))
+    return pairs
+
+
+def moved(block, change):
+    return lax.ppermute(block, AXES, route(change))
+
+
+def over_tensor(s, d, t):
+    return (s, d, 1 - t)
+
+
+def over_section(s, d, t):
+    return (1 - s, d, t)
+
+
+def over_both(s, d, t):
+    return (1 - s, d, 1 - t)
+
+
+def over_core(s, d, t):
+    return (s, d ^ 1, t)
+
+
+def along_z(distance):
+    count = lax.axis_size("dp") // 2
+    return lambda s, d, t: (s, (d // 2 + distance) % count * 2 + d % 2, t)
+
+
+def tie(*values):
+    return lax.optimization_barrier(values)
+
+
+def take_part(block, which, count, axis=0):
+    size = block.shape[axis] // count
+    return lax.dynamic_slice_in_dim(block, which * size, size, axis)
+
+
+def added(*terms):
+    total = terms[0].astype(F32)
+    for term in terms[1:]:
+        total = total + term.astype(F32)
+    return total.astype(terms[0].dtype)
+
+
+def send_plane(sums, section):
+    return [
+        moved(take_part(sums[1], section, 2), over_tensor),
+        moved(take_part(sums[0], 1 - section, 2), over_section),
+        moved(take_part(sums[1], 1 - section, 2), over_both),
+    ]
+
+
+def send_line(part, z_index):
+    count = lax.axis_size("dp") // 2
+    return [moved(take_part(part, (z_index + step) % count, count), along_z(step)) for step in range(1, count)]
+
+
+def reordered(pieces, lane, core):
+    pieces = jnp.where(lane == 0, pieces, pieces[jnp.array([2, 3, 0, 1])])
+    return jnp.where(core == 0, pieces, pieces[jnp.array([1, 0, 3, 2])])
+
+
+def one_sequence_each(
+    inputs,
+    cotangent,
+    segment_ids,
+    norm_gains,
+    norm_biases,
+    qkv_weight,
+    qv_bias,
+    out_weight,
+    up_weight,
+    up_bias,
+    down_weight,
+    out_biases,
+):
+    section = lax.axis_index("section")
+    group = lax.axis_index("dp")
+    lane = lax.axis_index("tensor")
+    core = group % 2
+    z_index = group // 2
+    z_count = lax.axis_size("dp") // 2
+    width = inputs.shape[2]
+    hidden = up_bias.shape[1]
+    cols = qkv_weight.shape[3]
+    part = cols // 2
+    mine = 2 * section + lane
+
+    def own_half(array, axis):
+        return take_part(array, core, 2, axis)
+
+    mixer_own = jnp.concatenate(
+        [
+            own_half(qkv_weight[0], 2).transpose(0, 2, 1).reshape(3 * part, width),
+            own_half(out_weight[0], 0),
+        ],
+        axis=0,
+    )
+    up_own = own_half(up_weight[0], 1)
+    down_own = own_half(down_weight[0], 0)
+    small = jnp.concatenate(
+        [item.reshape(-1) for item in (norm_gains, norm_biases, qv_bias, up_bias, out_biases)]
+    )
+
+    def sequence_halves(array):
+        kept = lax.dynamic_index_in_dim(array, mine, 0, keepdims=False)
+        sent = lax.dynamic_index_in_dim(array, 2 * section + 1 - lane, 0, keepdims=False)
+        return kept, sent
+
+    def joined(kept, came):
+        return jnp.where(lane == 0, jnp.concatenate([kept, came], 0), jnp.concatenate([came, kept], 0))
+
+    segment = lax.dynamic_index_in_dim(segment_ids, mine, 0, keepdims=True)
+    ids = jnp.arange(IMAGE_IDS, dtype=jnp.int32)[:, None]
+    begin = jnp.sum((segment < ids).astype(jnp.int32), axis=1)
+    end = jnp.sum((segment <= ids).astype(jnp.int32), axis=1)
+    start = begin // TILE
+    place = jnp.stack([lane, core]).astype(jnp.int32)
+    images = (place, start, (end - 1) // TILE - start + 1, segment)
+
+    def params(vector):
+        gains = vector[: 2 * width].reshape(2, width)
+        shifts = vector[2 * width : 4 * width].reshape(2, width)
+        qv = vector[4 * width : 6 * width].reshape(2, 4, part)
+        up_shift = vector[6 * width : 6 * width + hidden].reshape(4, 1, hidden // 4)
+        outs = vector[6 * width + hidden :].reshape(2, 1, width)
+        zero = jnp.zeros((4, part), F32)
+        qkv_shift = jnp.concatenate([qv[0], zero, qv[1]], axis=1)
+        norms = [jnp.stack([gains[i], shifts[i]]) for i in range(2)]
+        return norms, qkv_shift[:, :, None], up_shift, outs
+
+    def by_layer(own, came):
+        return jnp.where(section == 0, own, came), jnp.where(section == 1, own, came)
+
+    kept, sent = sequence_halves(inputs)
+    came, mixer_came, small_came = tie(
+        moved(sent, over_tensor), moved(mixer_own, over_section), moved(small, over_section)
+    )
+    state = joined(kept, came)
+    mixers = by_layer(mixer_own, mixer_came)
+    layer_params = [params(vector) for vector in by_layer(small, small_came)]
+    mixer_pieces = [[mixers[0], moved(mixers[0], over_core)], None]
+    norms, qkv_shift, up_shift, outs = layer_params[0]
+    mixer_a, beside, up_came = tie(
+        mixer_forward(images, state, norms[0], qkv_shift, mixer_pieces[0]),
+        moved(mixers[0], over_tensor),
+        moved(up_own, over_section),
+    )
+    ups = by_layer(up_own, up_came)
+    mixer_pieces[0] = mixer_pieces[0] + [beside, moved(beside, over_core)]
+    mixer_b, up_beside, up_twin, down_came = tie(
+        mixer_forward(
+            images,
+            state,
+            norms[0],
+            qkv_shift,
+            mixer_pieces[0][2:],
+            2,
+            (mixer_a[3], mixer_a[1]),
+            mixer_pieces[0],
+            outs[0],
+        ),
+        moved(ups[0], over_tensor),
+        moved(ups[0], over_core),
+        moved(down_own, over_section),
+    )
+    downs = by_layer(down_own, down_came)
+    down_twin = moved(downs[0], over_core)
+    feed_a, down_beside, up_corner = tie(
+        feed_forward(
+            place, mixer_b[3], norms[1], up_shift, outs[1], [ups[0], up_twin], [downs[0], down_twin], 0, False
+        ),
+        moved(downs[0], over_tensor),
+        moved(up_beside, over_core),
+    )
+    up_pieces = [[ups[0], up_twin, up_beside, up_corner], None]
+    down_pieces = [[downs[0], down_twin, down_beside, moved(down_beside, over_core)], None]
+    feed_b, beside, twin = tie(
+        feed_forward(
+            place, mixer_b[3], norms[1], up_shift, feed_a[0], up_pieces[0][2:], down_pieces[0][2:], 2, True
+        ),
+        moved(mixers[1], over_tensor),
+        moved(mixers[1], over_core),
+    )
+    first_out = feed_b[0]
+    saved = [
+        dict(
+            state=state,
+            normed=mixer_a[3],
+            qkv=[mixer_a[0], mixer_a[0], mixer_b[0], mixer_b[0]],
+            mixed=[mixer_a[1], mixer_a[1], mixer_b[1], mixer_b[1]],
+            totals=[mixer_a[2], mixer_a[2], mixer_b[2], mixer_b[2]],
+            at=[0, 1, 0, 1],
+            middle=mixer_b[3],
+            active=[feed_a[1], feed_a[1], feed_b[1], feed_b[1]],
+            slope=[feed_a[2], feed_a[2], feed_b[2], feed_b[2]],
+        )
+    ]
+    norms, qkv_shift, up_shift, outs = layer_params[1]
+    mixer_pieces[1] = [mixers[1], twin, beside, moved(beside, over_core)]
+    mixer_a, up_beside, up_twin, down_beside, down_twin = tie(
+        mixer_forward(images, first_out, norms[0], qkv_shift, mixer_pieces[1], 0, None, mixer_pieces[1], outs[0]),
+        moved(ups[1], over_tensor),
+        moved(ups[1], over_core),
+        moved(downs[1], over_tensor),
+        moved(downs[1], over_core),
+    )
+    up_pieces[1] = [ups[1], up_twin, up_beside, moved(up_beside, over_core)]
+    down_pieces[1] = [downs[1], down_twin, down_beside, moved(down_beside, over_core)]
+    grad_kept, grad_sent = sequence_halves(cotangent)
+    feed_a, grad_came = tie(
+        feed_forward(place, mixer_a[4], norms[1], up_shift, outs[1], up_pieces[1], down_pieces[1], 0, True),
+        moved(grad_sent, over_tensor),
+    )
+    second_out = feed_a[0]
+    saved.append(
+        dict(
+            state=first_out,
+            normed=mixer_a[3],
+            qkv=[mixer_a[0]] * 4,
+            mixed=[mixer_a[1]] * 4,
+            totals=[mixer_a[2]] * 4,
+            at=[0, 1, 2, 3],
+            middle=mixer_a[4],
+            active=[feed_a[1]] * 4,
+            slope=[feed_a[2]] * 4,
+        )
+    )
+    grad = joined(grad_kept, grad_came)
+
+    def exchange(own, other):
+        return [
+            take_part(own, lane, 2),
+            moved(take_part(own, 1 - lane, 2), over_tensor),
+            moved(take_part(other, lane, 2), over_section),
+            moved(take_part(other, 1 - lane, 2), over_both),
+        ]
+
+    def ordered(relative):
+        relative = jnp.stack(relative)
+        relative = jnp.where(lane == 0, relative, relative[jnp.array([1, 0, 3, 2])])
+        return jnp.where(section == 0, relative, relative[jnp.array([2, 3, 0, 1])])
+
+    out_parts = exchange(
+        jnp.where(section == 0, first_out, second_out), jnp.where(section == 0, second_out, first_out)
+    )
+
+    def feed_back(layer, grad):
+        kept = saved[layer]
+        return feed_backward(
+            grad,
+            kept["middle"],
+            layer_params[layer][0][1],
+            kept["active"],
+            kept["slope"],
+            kept["at"],
+            up_pieces[layer],
+            down_pieces[layer],
+            layer,
+        )
+
+    def mixer_back(layer, middle_grad):
+        kept = saved[layer]
+        return mixer_backward(
+            images, middle_grad, kept["qkv"], kept["mixed"], kept["totals"], kept["at"], mixer_pieces[layer]
+        )
+
+    def input_back(layer, middle_grad, projected):
+        kept = saved[layer]
+        return input_backward(
+            kept["state"],
+            middle_grad,
+            layer_params[layer][0][0],
+            projected,
+            kept["normed"],
+            kept["mixed"],
+            kept["at"],
+            mixer_pieces[layer],
+            2 + layer,
+        )
+
+    def small_vector(feed, mixer, in_small):
+        shifts = reordered(mixer[1].reshape(4, 3, part), lane, core)
+        ups = reordered(feed[1].reshape(4, -1)[jnp.array([2, 0, 3, 1])], lane, core)
+        return jnp.concatenate(
+            [
+                in_small[0],
+                feed[3][0],
+                in_small[1],
+                feed[3][1],
+                shifts[:, 0].reshape(-1),
+                shifts[:, 2].reshape(-1),
+                ups.reshape(-1),
+                feed[3][2],
+                feed[3][3],
+            ]
+        ).reshape(-1, TILE)
+
+    def plane_sum(sums, came):
+        return added(take_part(sums[0], section, 2), *came)
+
+    def line_sum(block, came):
+        return added(take_part(block, z_index, z_count), *came)
+
+    feed1, out_parts = tie(feed_back(1, grad), out_parts)
+    feed_sums1 = feed1[0].reshape(2, -1, width)
+    mixer1, came = tie(mixer_back(1, feed1[2]), send_plane(feed_sums1, section))
+    feed_part1 = plane_sum(feed_sums1, came)
+    input1 = input_back(1, feed1[2], mixer1[0])
+    in_grad1 = input1[1]
+    feed0, came, came_line = tie(
+        feed_back(0, in_grad1), send_plane(input1[0], section), send_line(feed_part1, z_index)
+    )
+    mixer_part1 = plane_sum(input1[0], came)
+    feed_total1 = line_sum(feed_part1, came_line)
+    feed_sums0 = feed0[0].reshape(2, -1, width)
+    mixer0, came, came_line = tie(
+        mixer_back(0, feed0[2]), send_plane(feed_sums0, section), send_line(mixer_part1, z_index)
+    )
+    feed_part0 = plane_sum(feed_sums0, came)
+    mixer_total1 = line_sum(mixer_part1, came_line)
+    input0, came_line = tie(input_back(0, feed0[2], mixer0[0]), send_line(feed_part0, z_index))
+    feed_total0 = line_sum(feed_part0, came_line)
+    mixer_part0 = plane_sum(input0[0], send_plane(input0[0], section))
+    mixer_total0 = line_sum(mixer_part0, send_line(mixer_part0, z_index))
+    in_parts = exchange(
+        jnp.where(section == 0, input0[1], in_grad1), jnp.where(section == 0, in_grad1, input0[1])
+    )
+    vector = jnp.stack([small_vector(feed0, mixer0, input0[2]), small_vector(feed1, mixer1, input1[2])])
+    vector = vector + moved(vector, over_core)
+    vector = added(vector, *[moved(vector, along_z(step)) for step in range(1, z_count)])
+    vector = added(vector, *[moved(vector, change) for change in (over_tensor, over_section, over_both)])
+    vector = jnp.where(section == 0, vector[0], vector[1]).reshape(-1)
+
+    def whole(total0, total1):
+        own = jnp.where(section == 0, total0, total1)
+        came = moved(jnp.where(section == 0, total1, total0), over_section)
+        both = jnp.where(section == 0, jnp.stack([own, came]), jnp.stack([came, own]))
+        parts = [both] + [moved(both, along_z(step)) for step in range(1, z_count)]
+        order = (z_index - jnp.arange(z_count)) % z_count
+        line = jnp.stack(parts)[order].transpose(1, 0, 2, 3).reshape(2, -1, width)
+        twin = moved(line, over_core)
+        return jnp.where(core == 0, jnp.stack([line, twin]), jnp.stack([twin, line]))
+
+    feed_sum = whole(feed_total0, feed_total1)
+    mixer_sum = whole(mixer_total0, mixer_total1).reshape(2, 4 * part, width)
+    qkv_grad, out_grad, up_grad, down_grad = unpack(feed_sum, mixer_sum)
+    states = ordered(out_parts)
+    grads = ordered(in_parts).astype(F32)
+    return (
+        states[None],
+        grads[None],
+        vector[: 2 * width].reshape(1, 2, width),
+        vector[2 * width : 4 * width].reshape(1, 2, width),
+        qkv_grad[None],
+        vector[4 * width : 6 * width].reshape(1, 2, width),
+        out_grad[None],
+        up_grad[None],
+        vector[6 * width : 6 * width + hidden].reshape(1, hidden),
+        down_grad[None],
+        vector[6 * width + hidden :].reshape(1, 2, width),
+    )
 
 
 def passed_along(block, axis, distance):
@@ -155,7 +1370,7 @@
     return array.at[which].set(jnp.where(running, value, array[which]))
 
 
-def on_device(
+def pipelined(
     inputs,
     cotangent,
     segment_ids,
@@ -419,6 +1634,16 @@
         P("section", "tensor", None),
         P("section", None, None),
     )
+    sizes = dict(mesh.shape)
+
+    def on_device(inputs, *rest):
+        each = inputs.shape[0] == sizes["section"] * sizes["tensor"]
+        paired = sizes["section"] == 2 and sizes["tensor"] == 2 and sizes["dp"] % 2 == 0
+        doubling = (sizes["dp"] // 2) & (sizes["dp"] // 2 - 1) == 0
+        if each and paired and doubling:
+            return one_sequence_each(inputs, *rest)
+        return pipelined(inputs, *rest)
+
     return jax.shard_map(
         on_device,
         mesh=mesh,

time: 4520 us -> 826 us (0.18)
  matrix products: 1260 us -> 0 us
  waiting for transfers between devices: 1390 us -> 181 us
  local copies, waits for them, and re-layouts: 1020 us -> 112 us
  loops' own time: 348 us -> 0 us
  Pallas kernels: 0 us -> 347 us
  other arithmetic: 346 us -> 90.1 us
  starting transfers between devices: 27 us -> 84 us
  blocking collectives: 55.3 us -> 0 us
    dot_general x705 -> x0, matrix products: 1260 us -> none  [the longest x80 178 us: one_item(): jnp.dot(weights, head_values, preferred_element_type=jnp.float32)]
    all_gather x30 -> x0, waiting for transfers between devices: 606 us -> none  [the longest x10 314 us: spread_rows(): lax.all_gather(normed_rows, 'tensor', axis=0, tiled=True)]
    reduce_scatter x20 -> x0, waiting for transfers between devices: 527 us -> none  [the longest x10 276 us: input_sum(): lax.psum_scatter(jnp.einsum('sc,dc->sd', grad_rows, weight, preferred_ele...]
    dynamic_slice x817 -> x20, local copies, waits for them, and re-layouts: 401 us -> 19 us  [the longest x19 17.6 us: take_part(): return lax.dynamic_slice_in_dim(block, which * size, size, axis)]
    another operation x50 -> x0, loops' own time: 348 us -> none  [the longest x5 213 us: attend_forward(): lax.map(one_item, jnp.arange(2 * heads_local, dtype=jnp.int32))]
    pallas_call x0 -> x13, Pallas kernels: none -> 347 us  [the longest x2 85.7 us: mixer_backward(): pl.pallas_call(functools.partial(mixer_backward_kernel, saved=saved, head...]
    while x1685 -> x0, local copies, waits for them, and re-layouts: 243 us -> none
    dynamic_update_slice x280 -> x0, local copies, waits for them, and re-layouts: 234 us -> none  [the longest x200 229 us: attend_backward(): results = lax.map(one_head, jnp.arange(heads_local, dtype=jnp.int32))]
where the time goes in v2:
time: 826 us; the launch traced here: 816 us
  Pallas kernels  347 us (42%)
  waiting for transfers between devices  181 us (22%)
  local copies, waits for them, and re-layouts  112 us (14%)
  other arithmetic  90.1 us (11%)
  starting transfers between devices  84 us (10%)
    ppermute x71, waiting for transfers between devices, moved(): return lax.ppermute(block, AXES, route(change))  181 us
    pallas_call x2, Pallas kernels, mixer_backward(): pl.pallas_call(functools.partial(mixer_backward_kernel, saved=saved, head...  85.7 us
    ppermute x71, starting transfers between devices, moved(): return lax.ppermute(block, AXES, route(change))  84 us
    pallas_call x2, Pallas kernels, feed_backward(): pl.pallas_call(functools.partial(feed_backward_kernel, columns=columns),...  79.2 us
    pallas_call x3, Pallas kernels, mixer_forward(): pl.pallas_call(functools.partial(mixer_forward_kernel, pieces=count, out_...  78.3 us
    pallas_call x3, Pallas kernels, feed_forward(): pl.pallas_call(functools.partial(feed_forward_kernel, pieces=pieces, offs...  51.6 us
    pallas_call x2, Pallas kernels, input_backward(): pl.pallas_call(functools.partial(input_backward_kernel, saved=saved), gri...  42.9 us
    dynamic_slice x19, local copies, waits for them, and re-layouts, take_part(): return lax.dynamic_slice_in_dim(block, which * size, size, axis)  17.6 us
  transfers between devices with their start and end apart: 71, of which 17 were waited for; matrix products, arithmetic and copies ran while one was open for 18% of the time, Pallas kernels for 39%

profile of v2, /device:TPU:3, one launch (start us, length us, event | category | flops | bytes accessed | tf_op | source)
XLA Modules:
  0.0 816.2 jit_solution(14189785655691000227)
XLA Ops:
  0.7 3.0 dynamic-slice_bitcast_fusion.4
  7.9 2.4 dynamic-slice_bitcast_fusion.1
  14.4 19.7 %collective-permute-done.2 = f32[9216]{0:T(1024)S(1)} collective-permute-done((f32[9216]{0:T(1024)S(1)}, f32[9216]{0:T(1024)S(1)}, u32[]{:S(2)}, u32[]{:S(2)}) %collective-permute-start.2) | collective-permute-done | bytes 36896 | tf_op jit(solution)/shard_map/ppermute | solution.py:868
  34.1 3.2 broadcast_select_fusion.8
  37.3 2.6 collective-permute-start.3
  44.0 3.4 maximum_select_fusion.4.hidden_ref
  48.4 19.4 %mixer_forward.3 = (bf16[2,576,1280]{2,1,0:T(8,128)(2,1)}, bf16[2,192,1280]{2,1,0:T(8,128)(2,1)}, f32[8,1,1280]{2,1,0:T(1,128)}, bf16[1280,768]{1,0:T(8,128)(2,1)}) custom-call(s32[2]{0:T(128)} %pad_add_fusion.place_ref, s32[5]{0:T(128)} %get-tuple-element.276.start_ref, s32[5]{0:T(128)} %get-tuple-element.275.tiles_ref, ...), custom_call_target="tpu_custom_call" | custom-call | flops 4000000000 | bytes 1000000 | tf_op jit(solution)/shard_map/mixer_forward/pallas_call | solution.py:338
  75.6 22.5 %mixer_forward.4 = (bf16[2,576,1280]{2,1,0:T(8,128)(2,1)}, bf16[2,192,1280]{2,1,0:T(8,128)(2,1)}, f32[8,1,1280]{2,1,0:T(1,128)}, f32[1280,768]{1,0:T(8,128)}) custom-call(s32[2]{0:T(128)} %pad_add_fusion.place_ref, s32[5]{0:T(128)} %get-tuple-element.276.start_ref, s32[5]{0:T(128)} %get-tuple-element.275.tiles_ref, s32[1,1280]{1,0:T(1,128)} %get-tuple-element.278.seg_ref, ...), custom_call_target="tpu_custom_call" | custom-call | flops 4000000000 | bytes 1000000 | tf_op jit(solution)/shard_map/mixer_forward/pallas_call | solution.py:338
  98.2 2.5 collective-permute-done.7.rest_0_.rest_10_
  100.7 3.1 broadcast_select_fusion.6
  108.1 14.4 %feed_forward.3 = (f32[1280,768]{1,0:T(8,128)}, bf16[1280,1536]{1,0:T(8,128)(2,1)}, bf16[1280,1536]{1,0:T(8,128)(2,1)}) custom-call(s32[2]{0:T(128)} %pad_add_fusion.place_ref, f32[1280,768]{1,0:T(8,128)} %get-tuple-element.146.middle_ref, f32[2,768]{1,0:T(2,128)} %pad_maximum_fusion.7.norm_ref, f32[4,1,768]{2,1,0:T(1,128)} %bitcast.156, ...), custom_call_target="tpu_custom_call" | custom-call | flops 4000000000 | bytes 1000000 | tf_op jit(solution)/shard_map/feed_forward/pallas_call | solution.py:417
  122.5 10.2 %collective-permute-done.11.rest_2_.rest_14_ = bf16[768,768]{1,0:T(8,128)(2,1)} collective-permute-done((bf16[768,768]{1,0:T(8,128)(2,1)}, bf16[768,768]{1,0:T(8,128)(2,1)}, u32[]{:S(2)}, u32[]{:S(2)}) %collective-permute-start.11) | collective-permute-done | bytes 1179680 | tf_op jit(solution)/shard_map/ppermute | solution.py:868
  136.4 14.7 %feed_forward.4 = (bf16[1280,768]{1,0:T(8,128)(2,1)}, bf16[1280,1536]{1,0:T(8,128)(2,1)}, bf16[1280,1536]{1,0:T(8,128)(2,1)}) custom-call(s32[2]{0:T(128)} %pad_add_fusion.place_ref, f32[1280,768]{1,0:T(8,128)} %get-tuple-element.146.middle_ref, f32[2,768]{1,0:T(2,128)} %pad_maximum_fusion.7.norm_ref, f32[4,1,768]{2,1,0:T(1,128)} %bitcast.157, ...), custom_call_target="tpu_custom_call" | custom-call | flops 4000000000 | bytes 1000000 | tf_op jit(solution)/shard_map/feed_forward/pallas_call | solution.py:417
  151.1 10.4 %collective-permute-done.14.rest_2_.rest_6_.rest_13_ = bf16[768,768]{1,0:T(8,128)(2,1)} collective-permute-done((bf16[768,768]{1,0:T(8,128)(2,1)}, bf16[768,768]{1,0:T(8,128)(2,1)}, u32[]{:S(2)}, u32[]{:S(2)}) %collective-permute-start.14) | collective-permute-done | bytes 1179680 | tf_op jit(solution)/shard_map/ppermute | solution.py:868
  167.1 36.4 %mixer_forward.5 = (bf16[4,576,1280]{2,1,0:T(8,128)(2,1)}, bf16[4,192,1280]{2,1,0:T(8,128)(2,1)}, f32[16,1,1280]{2,1,0:T(1,128)}, bf16[1280,768]{1,0:T(8,128)(2,1)}, f32[1280,768]{1,0:T(8,128)}) custom-call(s32[2]{0:T(128)} %pad_add_fusion.place_ref, s32[5]{0:T(128)} %get-tuple-element.276.start_ref, s32[5]{0:T(128)} %get-tuple-element.275.tiles_ref, ...), custom_call_target="tpu_custom_call" | custom-call | flops 4000000000 | bytes 1000000 | tf_op jit(solution)/shard_map/mixer_forward/pallas_call | solution.py:338
  203.6 11.7 %collective-permute-done.19.rest_6_.rest_14_ = bf16[768,768]{1,0:T(8,128)(2,1)} collective-permute-done((bf16[768,768]{1,0:T(8,128)(2,1)S(1)}, bf16[768,768]{1,0:T(8,128)(2,1)}, u32[]{:S(2)}, u32[]{:S(2)}) %collective-permute-start.19) | collective-permute-done | bytes 1179680 | tf_op jit(solution)/shard_map/ppermute | solution.py:868
  216.0 2.9 dynamic-slice_bitcast_fusion.5
  224.1 22.5 %feed_forward.5 = (bf16[1280,768]{1,0:T(8,128)(2,1)}, bf16[1280,3072]{1,0:T(8,128)(2,1)}, bf16[1280,3072]{1,0:T(8,128)(2,1)}) custom-call(s32[2]{0:T(128)} %pad_add_fusion.place_ref, f32[1280,768]{1,0:T(8,128)} %get-tuple-element.167.middle_ref, f32[2,768]{1,0:T(2,128)} %pad_maximum_fusion.9.norm_ref, f32[4,1,768]{2,1,0:T(1,128)} %bitcast.158, ...), custom_call_target="tpu_custom_call" | custom-call | flops 4000000000 | bytes 1000000 | tf_op jit(solution)/shard_map/feed_forward/pallas_call | solution.py:417
  251.2 2.4 collective-permute-start.26
  253.6 3.5 maximum_select_fusion.5.grad_ref
  257.1 40.0 %feed_backward.2 = (bf16[2,2,768,768]{3,2,1,0:T(8,128)(2,1)}, f32[4,1,768]{2,1,0:T(1,128)}, f32[1280,768]{1,0:T(8,128)}, f32[4,768]{1,0:T(4,128)}) custom-call(bf16[1280,768]{1,0:T(8,128)(2,1)} %maximum_select_fusion.5.grad_ref, f32[1280,768]{1,0:T(8,128)} %get-tuple-element.167.middle_ref, f32[2,768]{1,0:T(2,128)} %pad_maximum_fusion.9.norm_ref, ...), custom_call_target="tpu_custom_call" | custom-call | flops 16000000000 | bytes 1000000 | tf_op jit(solution)/shard_map/feed_backward/pallas_call | solution.py:603
  297.1 3.4 pad_maximum_fusion
  300.5 4.9 gather_fusion
  305.4 4.3 broadcast_select_fusion.1
  309.6 2.7 fusion.18
  317.8 4.9 gather_fusion.1
  324.4 42.8 %mixer_backward.2 = (bf16[4,576,1280]{2,1,0:T(8,128)(2,1)}, f32[4,576,1]{2,1,0:T(8,128)}) custom-call(s32[5]{0:T(128)} %get-tuple-element.276.start_ref, s32[5]{0:T(128)} %get-tuple-element.275.tiles_ref, s32[1,1280]{1,0:T(1,128)} %get-tuple-element.278.seg_ref, f32[1280,768]{1,0:T(8,128)} %get-tuple-element.187.middle_grad_ref, ...), custom_call_target="tpu_custom_call" | custom-call | flops 16000000000 | bytes 1000000 | tf_op jit(solution)/shard_map/mixer_backward/pallas_call | solution.py:699
  368.5 5.7 fusion
  374.2 21.4 %input_backward.2 = (bf16[2,768,768]{2,1,0:T(8,128)(2,1)}, bf16[1280,768]{1,0:T(8,128)(2,1)}, f32[2,768]{1,0:T(2,128)}) custom-call(bf16[1280,768]{1,0:T(8,128)(2,1)} %get-tuple-element.159.hidden_ref, f32[1280,768]{1,0:T(8,128)} %get-tuple-element.187.middle_grad_ref, f32[2,768]{1,0:T(2,128)} %pad_maximum_fusion.8.norm_ref, ...), custom_call_target="tpu_custom_call" | custom-call | flops 8000000000 | bytes 1000000 | tf_op jit(solution)/shard_map/input_backward/pallas_call | solution.py:795
  398.6 3.1 collective-permute-start.30
  401.7 5.7 collective-permute-start.31
  408.7 2.6 add_convert_fusion.1
  412.3 2.3 collective-permute-start.33
  429.6 39.2 %feed_backward.3 = (bf16[2,2,768,768]{3,2,1,0:T(8,128)(2,1)}, f32[4,1,768]{2,1,0:T(1,128)}, f32[1280,768]{1,0:T(8,128)}, f32[4,768]{1,0:T(4,128)}) custom-call(bf16[1280,768]{1,0:T(8,128)(2,1)} %get-tuple-element.196.grad_ref, f32[1280,768]{1,0:T(8,128)} %get-tuple-element.146.middle_ref, f32[2,768]{1,0:T(2,128)} %pad_maximum_fusion.7.norm_ref, ...), custom_call_target="tpu_custom_call" | custom-call | flops 16000000000 | bytes 1000000 | tf_op jit(solution)/shard_map/feed_backward/pallas_call | solution.py:603
  479.3 4.9 collective-permute-done.35
  485.0 2.7 fusion.17
  497.0 42.8 %mixer_backward.3 = (bf16[4,576,1280]{2,1,0:T(8,128)(2,1)}, f32[4,576,1]{2,1,0:T(8,128)}) custom-call(s32[5]{0:T(128)} %get-tuple-element.276.start_ref, s32[5]{0:T(128)} %get-tuple-element.275.tiles_ref, s32[1,1280]{1,0:T(1,128)} %get-tuple-element.278.seg_ref, f32[1280,768]{1,0:T(8,128)} %get-tuple-element.209.middle_grad_ref, ...), custom_call_target="tpu_custom_call" | custom-call | flops 16000000000 | bytes 1000000 | tf_op jit(solution)/shard_map/mixer_backward/pallas_call | solution.py:699
  542.0 9.5 %collective-permute-start.41 = (bf16[96,768]{1,0:T(8,128)(2,1)S(1)}, bf16[96,768]{1,0:T(8,128)(2,1)S(1)}, u32[]{:S(2)}, u32[]{:S(2)}) collective-permute-start(bf16[96,768]{1,0:T(8,128)(2,1)S(1)} %get-tuple-element.329), channel_id=1, source_target_pairs={{0,12},{1,13},{2,14},{3,15},{4,0},{5,1},{6,2},{7,3},{8,4},{9,5},{1... | collective-permute-start | bytes 442376 | tf_op jit(solution)/shard_map/ppermute | solution.py:868
  554.3 3.0 add_convert_fusion
  569.0 21.5 %input_backward.3 = (bf16[2,768,768]{2,1,0:T(8,128)(2,1)}, bf16[1280,768]{1,0:T(8,128)(2,1)}, f32[2,768]{1,0:T(2,128)}) custom-call(bf16[1280,768]{1,0:T(8,128)(2,1)} %maximum_select_fusion.4.hidden_ref, f32[1280,768]{1,0:T(8,128)} %get-tuple-element.209.middle_grad_ref, f32[2,768]{1,0:T(2,128)} %pad_maximum_fusion.6.norm_ref, ...), custom_call_target="tpu_custom_call" | custom-call | flops 8000000000 | bytes 1000000 | tf_op jit(solution)/shard_map/input_backward/pallas_call | solution.py:795
  590.7 2.6 broadcast_select_fusion.3
  599.2 3.0 collective-permute-start.62
  609.1 3.0 collective-permute-done.50
  615.4 14.3 %collective-permute-done.54 = f32[2,72,128]{2,1,0:T(8,128)S(1)} collective-permute-done((f32[2,72,128]{2,1,0:T(8,128)S(1)}, f32[2,72,128]{2,1,0:T(8,128)S(1)}, u32[]{:S(2)}, u32[]{:S(2)}) %collective-permute-start.54) | collective-permute-done | bytes 73760 | tf_op jit(solution)/shard_map/ppermute | solution.py:868
  629.7 2.6 collective-permute-start.52
  636.7 28.0 %collective-permute-done.55 = bf16[192,768]{1,0:T(8,128)(2,1)S(1)} collective-permute-done((bf16[192,768]{1,0:T(8,128)(2,1)S(1)}, bf16[192,768]{1,0:T(8,128)(2,1)S(1)}, u32[]{:S(2)}, u32[]{:S(2)}) %collective-permute-start.55) | collective-permute-done | bytes 294944 | tf_op jit(solution)/shard_map/ppermute | solution.py:868
  667.3 2.6 collective-permute-start.65
  672.5 10.4 %collective-permute-done.65 = bf16[96,768]{1,0:T(8,128)(2,1)S(1)} collective-permute-done((bf16[96,768]{1,0:T(8,128)(2,1)}, bf16[96,768]{1,0:T(8,128)(2,1)S(1)}, u32[]{:S(2)}, u32[]{:S(2)}) %collective-permute-start.65) | collective-permute-done | bytes 147488 | tf_op jit(solution)/shard_map/ppermute | solution.py:868
  683.4 9.7 %collective-permute-done.64 = bf16[96,768]{1,0:T(8,128)(2,1)} collective-permute-done((bf16[96,768]{1,0:T(8,128)(2,1)}, bf16[96,768]{1,0:T(8,128)(2,1)}, u32[]{:S(2)}, u32[]{:S(2)}) %collective-permute-start.64) | collective-permute-done | bytes 147488 | tf_op jit(solution)/shard_map/ppermute | solution.py:868
  698.0 36.6 %collective-permute-done.57 = bf16[2,192,768]{2,1,0:T(8,128)(2,1)S(1)} collective-permute-done((bf16[2,192,768]{2,1,0:T(8,128)(2,1)}, bf16[2,192,768]{2,1,0:T(8,128)(2,1)S(1)}, u32[]{:S(2)}, u32[]{:S(2)}) %collective-permute-start.57) | collective-permute-done | bytes 589856 | tf_op jit(solution)/shard_map/ppermute | solution.py:868
  735.2 2.8 pad_maximum_fusion.2
  738.0 3.9 gather_fusion.14
  741.9 3.2 copy.58
  748.3 3.3 pad_maximum_fusion.1
  751.6 5.0 gather_fusion.2
  756.7 15.8 %collective-permute-done.68 = bf16[2,96,768]{2,1,0:T(8,128)(2,1)S(1)} collective-permute-done((bf16[2,96,768]{2,1,0:T(8,128)(2,1)}, bf16[2,96,768]{2,1,0:T(8,128)(2,1)S(1)}, u32[]{:S(2)}, u32[]{:S(2)}) %collective-permute-start.68) | collective-permute-done | bytes 294944 | tf_op jit(solution)/shard_map/ppermute | solution.py:868
  773.7 3.0 gather_fusion.15
  776.7 2.4 copy.60
  779.7 4.2 broadcast_select_fusion
  783.9 5.1 gather_fusion.3
  788.9 6.3 fusion.2
  795.2 4.2 maximum_select_fusion.3.mixer_ref
  799.5 6.8 maximum_select_fusion.feed_ref
  806.3 9.4 %unpack.1 = (f32[3,768,384]{2,1,0:T(8,128)}, f32[384,768]{1,0:T(8,128)}, f32[768,1536]{1,0:T(8,128)}, f32[1536,768]{1,0:T(8,128)}) custom-call(bf16[2,2,768,768]{3,2,1,0:T(8,128)(2,1)} %maximum_select_fusion.feed_ref, bf16[2,768,768]{2,1,0:T(8,128)(2,1)} %maximum_select_fusion.3.mixer_ref), custom_call_target="tpu_custom_call" | custom-call | tf_op jit(solution)/shard_map/unpack/pallas_call | solution.py:842
  (398 shorter events, 147.5 us)
Async XLA Ops:
  3.7 30.4 %collective-permute-start = (bf16[640,768]{1,0:T(8,128)(2,1)}, bf16[640,768]{1,0:T(8,128)(2,1)}, u32[]{:S(2)}, u32[]{:S(2)}) collective-permute-start(bf16[640,768]{1,0:T(8,128)(2,1)} %get-tuple-element.290), channel_id=1, source_target_pairs={{0,1},{1,0},{2,3},{3,2},{4,5},{5,4},{6,7},{7,6},{8,9},{9,8},{10,11... | collective-permute-start | bytes 2949128 | tf_op jit(solution)/shard_map/ppermute | solution.py:868
  6.1 28.0 %collective-permute-start.1 = (bf16[768,768]{1,0:T(8,128)(2,1)}, bf16[768,768]{1,0:T(8,128)(2,1)}, u32[]{:S(2)}, u32[]{:S(2)}) collective-permute-start(bf16[768,768]{1,0:T(8,128)(2,1)} %pad_maximum_fusion.3), channel_id=1, source_target_pairs={{0,16},{1,17},{2,18},{3,19},{4,20},{5,21},{6,22},{7,23},{8,24},{9,... | collective-permute-start | bytes 3538952 | tf_op jit(solution)/shard_map/ppermute | solution.py:868
  7.8 26.3 %collective-permute-start.2 = (f32[9216]{0:T(1024)S(1)}, f32[9216]{0:T(1024)S(1)}, u32[]{:S(2)}, u32[]{:S(2)}) collective-permute-start(f32[9216]{0:T(1024)S(1)} %constant_dynamic-update-slice_fusion), channel_id=1, source_target_pairs={{0,16},{1,17},{2,18},{3,19},{4,20},{5,21},{6,22},{7,23},{8,24},{9,... | collective-permute-start | bytes 110600 | tf_op jit(solution)/shard_map/ppermute | solution.py:868
  10.3 57.6 %collective-permute-start.5 = (bf16[768,768]{1,0:T(8,128)(2,1)}, bf16[768,768]{1,0:T(8,128)(2,1)}, u32[]{:S(2)}, u32[]{:S(2)}) collective-permute-start(bf16[768,768]{1,0:T(8,128)(2,1)} %dynamic-slice_bitcast_fusion.1), channel_id=1, source_target_pairs={{0,16},{1,17},{2,18},{3,19},{4,20},{5,21},{6,22},{7,23},{8,24},{9,... | collective-permute-start | bytes 3538952 | tf_op jit(solution)/shard_map/ppermute | solution.py:868
  37.3 10.1 %collective-permute-start.3 = (bf16[768,768]{1,0:T(8,128)(2,1)}, bf16[768,768]{1,0:T(8,128)(2,1)S(1)}, u32[]{:S(2)}, u32[]{:S(2)}) collective-permute-start(bf16[768,768]{1,0:T(8,128)(2,1)} %get-tuple-element.304.rest_0_.rest_4_.rest_11_), channel_id=1, source_target_pairs={{0,2},{1,3},{2,0},{3,1},{4,6},{5,7},{6,4},{7,5},{8,10},{9,11},{10,... | collective-permute-start | bytes 3538952 | tf_op jit(solution)/shard_map/ppermute | solution.py:868
  39.9 28.4 %collective-permute-start.4 = (bf16[768,768]{1,0:T(8,128)(2,1)}, bf16[768,768]{1,0:T(8,128)(2,1)}, u32[]{:S(2)}, u32[]{:S(2)}) collective-permute-start(bf16[768,768]{1,0:T(8,128)(2,1)} %get-tuple-element.304.rest_0_.rest_4_.rest_11_), channel_id=1, source_target_pairs={{0,1},{1,0},{2,3},{3,2},{4,5},{5,4},{6,7},{7,6},{8,9},{9,8},{10,11... | collective-permute-start | bytes 3538952 | tf_op jit(solution)/shard_map/ppermute | solution.py:868
  68.3 7.3 collective-permute-start.6
  70.0 28.2 %collective-permute-start.9 = (bf16[768,768]{1,0:T(8,128)(2,1)}, bf16[768,768]{1,0:T(8,128)(2,1)S(1)}, u32[]{:S(2)}, u32[]{:S(2)}) collective-permute-start(bf16[768,768]{1,0:T(8,128)(2,1)} %dynamic-slice_bitcast_fusion), channel_id=1, source_target_pairs={{0,16},{1,17},{2,18},{3,19},{4,20},{5,21},{6,22},{7,23},{8,24},{9,... | collective-permute-start | bytes 3538952 | tf_op jit(solution)/shard_map/ppermute | solution.py:868
  73.2 27.5 %collective-permute-start.7 = (bf16[768,768]{1,0:T(8,128)(2,1)S(1)}, bf16[768,768]{1,0:T(8,128)(2,1)}, u32[]{:S(2)}, u32[]{:S(2)}) collective-permute-start(bf16[768,768]{1,0:T(8,128)(2,1)S(1)} %get-tuple-element.302.rest_0_.rest_8_), channel_id=1, source_target_pairs={{0,1},{1,0},{2,3},{3,2},{4,5},{5,4},{6,7},{7,6},{8,9},{9,8},{10,11... | collective-permute-start | bytes 3538952 | tf_op jit(solution)/shard_map/ppermute | solution.py:868
  74.5 26.2 %collective-permute-start.8 = (bf16[768,768]{1,0:T(8,128)(2,1)S(1)}, bf16[768,768]{1,0:T(8,128)(2,1)}, u32[]{:S(2)}, u32[]{:S(2)}) collective-permute-start(bf16[768,768]{1,0:T(8,128)(2,1)S(1)} %get-tuple-element.302.rest_0_.rest_8_), channel_id=1, source_target_pairs={{0,2},{1,3},{2,0},{3,1},{4,6},{5,7},{6,4},{7,5},{8,10},{9,11},{10,... | collective-permute-start | bytes 3538952 | tf_op jit(solution)/shard_map/ppermute | solution.py:868
  104.8 27.9 %collective-permute-start.11 = (bf16[768,768]{1,0:T(8,128)(2,1)}, bf16[768,768]{1,0:T(8,128)(2,1)}, u32[]{:S(2)}, u32[]{:S(2)}) collective-permute-start(bf16[768,768]{1,0:T(8,128)(2,1)} %get-tuple-element.300.rest_2_.rest_12_), channel_id=1, source_target_pairs={{0,1},{1,0},{2,3},{3,2},{4,5},{5,4},{6,7},{7,6},{8,9},{9,8},{10,11... | collective-permute-start | bytes 3538952 | tf_op jit(solution)/shard_map/ppermute | solution.py:868
  106.1 26.7 %collective-permute-start.12 = (bf16[768,768]{1,0:T(8,128)(2,1)}, bf16[768,768]{1,0:T(8,128)(2,1)}, u32[]{:S(2)}, u32[]{:S(2)}) collective-permute-start(bf16[768,768]{1,0:T(8,128)(2,1)} %collective-permute-done.7.rest_0_.rest_10_), channel_id=1, source_target_pairs={{0,2},{1,3},{2,0},{3,1},{4,6},{5,7},{6,4},{7,5},{8,10},{9,11},{10,... | collective-permute-start | bytes 3538952 | tf_op jit(solution)/shard_map/ppermute | solution.py:868
  133.5 27.9 %collective-permute-start.14 = (bf16[768,768]{1,0:T(8,128)(2,1)}, bf16[768,768]{1,0:T(8,128)(2,1)}, u32[]{:S(2)}, u32[]{:S(2)}) collective-permute-start(bf16[768,768]{1,0:T(8,128)(2,1)} %get-tuple-element.303.rest_0_.rest_4_.rest_11_), channel_id=1, source_target_pairs={{0,1},{1,0},{2,3},{3,2},{4,5},{5,4},{6,7},{7,6},{8,9},{9,8},{10,11... | collective-permute-start | bytes 3538952 | tf_op jit(solution)/shard_map/ppermute | solution.py:868
  134.8 26.7 %collective-permute-start.15 = (bf16[768,768]{1,0:T(8,128)(2,1)}, bf16[768,768]{1,0:T(8,128)(2,1)}, u32[]{:S(2)}, u32[]{:S(2)}) collective-permute-start(bf16[768,768]{1,0:T(8,128)(2,1)} %get-tuple-element.303.rest_0_.rest_4_.rest_11_), channel_id=1, source_target_pairs={{0,2},{1,3},{2,0},{3,1},{4,6},{5,7},{6,4},{7,5},{8,10},{9,11},{10,... | collective-permute-start | bytes 3538952 | tf_op jit(solution)/shard_map/ppermute | solution.py:868
  162.3 41.3 %collective-permute-start.17 = (bf16[768,768]{1,0:T(8,128)(2,1)S(1)}, bf16[768,768]{1,0:T(8,128)(2,1)}, u32[]{:S(2)}, u32[]{:S(2)}) collective-permute-start(bf16[768,768]{1,0:T(8,128)(2,1)S(1)} %get-tuple-element.301.rest_0_.rest_8_), channel_id=1, source_target_pairs={{0,1},{1,0},{2,3},{3,2},{4,5},{5,4},{6,7},{7,6},{8,9},{9,8},{10,11... | collective-permute-start | bytes 3538952 | tf_op jit(solution)/shard_map/ppermute | solution.py:868
  163.5 40.1 %collective-permute-start.18 = (bf16[768,768]{1,0:T(8,128)(2,1)S(1)}, bf16[768,768]{1,0:T(8,128)(2,1)}, u32[]{:S(2)}, u32[]{:S(2)}) collective-permute-start(bf16[768,768]{1,0:T(8,128)(2,1)S(1)} %get-tuple-element.301.rest_0_.rest_8_), channel_id=1, source_target_pairs={{0,2},{1,3},{2,0},{3,1},{4,6},{5,7},{6,4},{7,5},{8,10},{9,11},{10,... | collective-permute-start | bytes 3538952 | tf_op jit(solution)/shard_map/ppermute | solution.py:868
  163.8 51.5 %collective-permute-start.19 = (bf16[768,768]{1,0:T(8,128)(2,1)S(1)}, bf16[768,768]{1,0:T(8,128)(2,1)}, u32[]{:S(2)}, u32[]{:S(2)}) collective-permute-start(bf16[768,768]{1,0:T(8,128)(2,1)S(1)} %get-tuple-element.299.rest_4_.rest_12_), channel_id=1, source_target_pairs={{0,1},{1,0},{2,3},{3,2},{4,5},{5,4},{6,7},{7,6},{8,9},{9,8},{10,11... | collective-permute-start | bytes 3538952 | tf_op jit(solution)/shard_map/ppermute | solution.py:868
  164.0 51.2 %collective-permute-start.20 = (bf16[768,768]{1,0:T(8,128)(2,1)S(1)}, bf16[768,768]{1,0:T(8,128)(2,1)}, u32[]{:S(2)}, u32[]{:S(2)}) collective-permute-start(bf16[768,768]{1,0:T(8,128)(2,1)S(1)} %get-tuple-element.299.rest_4_.rest_12_), channel_id=1, source_target_pairs={{0,2},{1,3},{2,0},{3,1},{4,6},{5,7},{6,4},{7,5},{8,10},{9,11},{10,... | collective-permute-start | bytes 3538952 | tf_op jit(solution)/shard_map/ppermute | solution.py:868
  215.2 7.4 collective-permute-start.21
  218.9 27.7 %collective-permute-start.23 = (bf16[640,768]{1,0:T(8,128)(2,1)}, bf16[640,768]{1,0:T(8,128)(2,1)}, u32[]{:S(2)}, u32[]{:S(2)}) collective-permute-start(bf16[640,768]{1,0:T(8,128)(2,1)} %get-tuple-element.288), channel_id=1, source_target_pairs={{0,1},{1,0},{2,3},{3,2},{4,5},{5,4},{6,7},{7,6},{8,9},{9,8},{10,11... | collective-permute-start | bytes 2949128 | tf_op jit(solution)/shard_map/ppermute | solution.py:868
  249.5 47.6 %collective-permute-start.24 = (bf16[640,768]{1,0:T(8,128)(2,1)}, bf16[640,768]{1,0:T(8,128)(2,1)S(1)}, u32[]{:S(2)}, u32[]{:S(2)}) collective-permute-start(bf16[640,768]{1,0:T(8,128)(2,1)} %get-tuple-element.312), channel_id=1, source_target_pairs={{0,1},{1,0},{2,3},{3,2},{4,5},{5,4},{6,7},{7,6},{8,9},{9,8},{10,11... | collective-permute-start | bytes 2949128 | tf_op jit(solution)/shard_map/ppermute | solution.py:868
  251.2 46.0 %collective-permute-start.25 = (bf16[640,768]{1,0:T(8,128)(2,1)}, bf16[640,768]{1,0:T(8,128)(2,1)}, u32[]{:S(2)}, u32[]{:S(2)}) collective-permute-start(bf16[640,768]{1,0:T(8,128)(2,1)} %get-tuple-element.311), channel_id=1, source_target_pairs={{0,16},{1,17},{2,18},{3,19},{4,20},{5,21},{6,22},{7,23},{8,24},{9,... | collective-permute-start | bytes 2949128 | tf_op jit(solution)/shard_map/ppermute | solution.py:868
  251.2 46.0 %collective-permute-start.26 = (bf16[640,768]{1,0:T(8,128)(2,1)}, bf16[640,768]{1,0:T(8,128)(2,1)}, u32[]{:S(2)}, u32[]{:S(2)}) collective-permute-start(bf16[640,768]{1,0:T(8,128)(2,1)} %get-tuple-element.310), channel_id=1, source_target_pairs={{0,17},{1,16},{2,19},{3,18},{4,21},{5,20},{6,23},{7,22},{8,25},{9,... | collective-permute-start | bytes 2949128 | tf_op jit(solution)/shard_map/ppermute | solution.py:868
  314.0 60.2 %collective-permute-start.27 = (bf16[768,768]{1,0:T(8,128)(2,1)}, bf16[768,768]{1,0:T(8,128)(2,1)}, u32[]{:S(2)}, u32[]{:S(2)}) collective-permute-start(bf16[768,768]{1,0:T(8,128)(2,1)} %get-tuple-element.298), channel_id=1, source_target_pairs={{0,1},{1,0},{2,3},{3,2},{4,5},{5,4},{6,7},{7,6},{8,9},{9,8},{10,11... | collective-permute-start | bytes 3538952 | tf_op jit(solution)/shard_map/ppermute | solution.py:868
  315.6 58.6 %collective-permute-start.28 = (bf16[768,768]{1,0:T(8,128)(2,1)}, bf16[768,768]{1,0:T(8,128)(2,1)}, u32[]{:S(2)}, u32[]{:S(2)}) collective-permute-start(bf16[768,768]{1,0:T(8,128)(2,1)} %constant_dynamic-slice_fusion.19), channel_id=1, source_target_pairs={{0,16},{1,17},{2,18},{3,19},{4,20},{5,21},{6,22},{7,23},{8,24},{9,... | collective-permute-start | bytes 3538952 | tf_op jit(solution)/shard_map/ppermute | solution.py:868
  315.8 58.4 %collective-permute-start.29 = (bf16[768,768]{1,0:T(8,128)(2,1)}, bf16[768,768]{1,0:T(8,128)(2,1)}, u32[]{:S(2)}, u32[]{:S(2)}) collective-permute-start(bf16[768,768]{1,0:T(8,128)(2,1)} %get-tuple-element.297), channel_id=1, source_target_pairs={{0,17},{1,16},{2,19},{3,18},{4,21},{5,20},{6,23},{7,22},{8,25},{9,... | collective-permute-start | bytes 3538952 | tf_op jit(solution)/shard_map/ppermute | solution.py:868
  398.6 85.7 %collective-permute-start.30 = (bf16[384,768]{1,0:T(8,128)(2,1)}, bf16[384,768]{1,0:T(8,128)(2,1)S(1)}, u32[]{:S(2)}, u32[]{:S(2)}) collective-permute-start(bf16[384,768]{1,0:T(8,128)(2,1)} %get-tuple-element.323), channel_id=1, source_target_pairs={{0,1},{1,0},{2,3},{3,2},{4,5},{5,4},{6,7},{7,6},{8,9},{9,8},{10,11... | collective-permute-start | bytes 1769480 | tf_op jit(solution)/shard_map/ppermute | solution.py:868
  401.7 82.5 %collective-permute-start.31 = (bf16[384,768]{1,0:T(8,128)(2,1)S(1)}, bf16[384,768]{1,0:T(8,128)(2,1)}, u32[]{:S(2)}, u32[]{:S(2)}) collective-permute-start(bf16[384,768]{1,0:T(8,128)(2,1)S(1)} %dynamic-slice_bitcast_fusion.12), channel_id=1, source_target_pairs={{0,16},{1,17},{2,18},{3,19},{4,20},{5,21},{6,22},{7,23},{8,24},{9,... | collective-permute-start | bytes 1769480 | tf_op jit(solution)/shard_map/ppermute | solution.py:868
  407.4 76.8 %collective-permute-start.32 = (bf16[384,768]{1,0:T(8,128)(2,1)}, bf16[384,768]{1,0:T(8,128)(2,1)}, u32[]{:S(2)}, u32[]{:S(2)}) collective-permute-start(bf16[384,768]{1,0:T(8,128)(2,1)} %get-tuple-element.322), channel_id=1, source_target_pairs={{0,17},{1,16},{2,19},{3,18},{4,21},{5,20},{6,23},{7,22},{8,25},{9,... | collective-permute-start | bytes 1769480 | tf_op jit(solution)/shard_map/ppermute | solution.py:868
  412.3 63.1 %collective-permute-start.33 = (bf16[192,768]{1,0:T(8,128)(2,1)}, bf16[192,768]{1,0:T(8,128)(2,1)}, u32[]{:S(2)}, u32[]{:S(2)}) collective-permute-start(bf16[192,768]{1,0:T(8,128)(2,1)} %get-tuple-element.321), channel_id=1, source_target_pairs={{0,4},{1,5},{2,6},{3,7},{4,8},{5,9},{6,10},{7,11},{8,12},{9,13},{1... | collective-permute-start | bytes 884744 | tf_op jit(solution)/shard_map/ppermute | solution.py:868
  414.6 64.7 %collective-permute-start.34 = (bf16[192,768]{1,0:T(8,128)(2,1)}, bf16[192,768]{1,0:T(8,128)(2,1)}, u32[]{:S(2)}, u32[]{:S(2)}) collective-permute-start(bf16[192,768]{1,0:T(8,128)(2,1)} %get-tuple-element.320), channel_id=1, source_target_pairs={{0,8},{1,9},{2,10},{3,11},{4,12},{5,13},{6,14},{7,15},{8,0},{9,1},... | collective-permute-start | bytes 884744 | tf_op jit(solution)/shard_map/ppermute | solution.py:868
  475.4 8.8 %collective-permute-start.35 = (bf16[192,768]{1,0:T(8,128)(2,1)}, bf16[192,768]{1,0:T(8,128)(2,1)S(1)}, u32[]{:S(2)}, u32[]{:S(2)}) collective-permute-start(bf16[192,768]{1,0:T(8,128)(2,1)} %get-tuple-element.319), channel_id=1, source_target_pairs={{0,12},{1,13},{2,14},{3,15},{4,0},{5,1},{6,2},{7,3},{8,4},{9,5},{1... | collective-permute-start | bytes 884744 | tf_op jit(solution)/shard_map/ppermute | solution.py:868
  489.4 65.0 %collective-permute-start.36 = (bf16[768,768]{1,0:T(8,128)(2,1)}, bf16[768,768]{1,0:T(8,128)(2,1)}, u32[]{:S(2)}, u32[]{:S(2)}) collective-permute-start(bf16[768,768]{1,0:T(8,128)(2,1)} %get-tuple-element.294), channel_id=1, source_target_pairs={{0,1},{1,0},{2,3},{3,2},{4,5},{5,4},{6,7},{7,6},{8,9},{9,8},{10,11... | collective-permute-start | bytes 3538952 | tf_op jit(solution)/shard_map/ppermute | solution.py:868
  491.0 63.3 %collective-permute-start.37 = (bf16[768,768]{1,0:T(8,128)(2,1)}, bf16[768,768]{1,0:T(8,128)(2,1)}, u32[]{:S(2)}, u32[]{:S(2)}) collective-permute-start(bf16[768,768]{1,0:T(8,128)(2,1)} %constant_dynamic-slice_fusion.13), channel_id=1, source_target_pairs={{0,16},{1,17},{2,18},{3,19},{4,20},{5,21},{6,22},{7,23},{8,24},{9,... | collective-permute-start | bytes 3538952 | tf_op jit(solution)/shard_map/ppermute | solution.py:868
  491.0 63.3 %collective-permute-start.38 = (bf16[768,768]{1,0:T(8,128)(2,1)}, bf16[768,768]{1,0:T(8,128)(2,1)}, u32[]{:S(2)}, u32[]{:S(2)}) collective-permute-start(bf16[768,768]{1,0:T(8,128)(2,1)} %get-tuple-element.293), channel_id=1, source_target_pairs={{0,17},{1,16},{2,19},{3,18},{4,21},{5,20},{6,23},{7,22},{8,25},{9,... | collective-permute-start | bytes 3538952 | tf_op jit(solution)/shard_map/ppermute | solution.py:868
  494.8 47.2 %collective-permute-start.39 = (bf16[96,768]{1,0:T(8,128)(2,1)S(1)}, bf16[96,768]{1,0:T(8,128)(2,1)S(1)}, u32[]{:S(2)}, u32[]{:S(2)}) collective-permute-start(bf16[96,768]{1,0:T(8,128)(2,1)S(1)} %get-tuple-element.331), channel_id=1, source_target_pairs={{0,4},{1,5},{2,6},{3,7},{4,8},{5,9},{6,10},{7,11},{8,12},{9,13},{1... | collective-permute-start | bytes 442376 | tf_op jit(solution)/shard_map/ppermute | solution.py:868
  494.9 57.8 %collective-permute-start.40 = (bf16[96,768]{1,0:T(8,128)(2,1)S(1)}, bf16[96,768]{1,0:T(8,128)(2,1)S(1)}, u32[]{:S(2)}, u32[]{:S(2)}) collective-permute-start(bf16[96,768]{1,0:T(8,128)(2,1)S(1)} %get-tuple-element.330), channel_id=1, source_target_pairs={{0,8},{1,9},{2,10},{3,11},{4,12},{5,13},{6,14},{7,15},{8,0},{9,1},... | collective-permute-start | bytes 442376 | tf_op jit(solution)/shard_map/ppermute | solution.py:868
  542.0 12.3 %collective-permute-start.41 = (bf16[96,768]{1,0:T(8,128)(2,1)S(1)}, bf16[96,768]{1,0:T(8,128)(2,1)S(1)}, u32[]{:S(2)}, u32[]{:S(2)}) collective-permute-start(bf16[96,768]{1,0:T(8,128)(2,1)S(1)} %get-tuple-element.329), channel_id=1, source_target_pairs={{0,12},{1,13},{2,14},{3,15},{4,0},{5,1},{6,2},{7,3},{8,4},{9,5},{1... | collective-permute-start | bytes 442376 | tf_op jit(solution)/shard_map/ppermute | solution.py:868
  558.3 32.4 %collective-permute-start.42 = (bf16[192,768]{1,0:T(8,128)(2,1)}, bf16[192,768]{1,0:T(8,128)(2,1)S(1)}, u32[]{:S(2)}, u32[]{:S(2)}) collective-permute-start(bf16[192,768]{1,0:T(8,128)(2,1)} %get-tuple-element.318), channel_id=1, source_target_pairs={{0,4},{1,5},{2,6},{3,7},{4,8},{5,9},{6,10},{7,11},{8,12},{9,13},{1... | collective-permute-start | bytes 884744 | tf_op jit(solution)/shard_map/ppermute | solution.py:868
  559.7 30.9 %collective-permute-start.43 = (bf16[192,768]{1,0:T(8,128)(2,1)}, bf16[192,768]{1,0:T(8,128)(2,1)S(1)}, u32[]{:S(2)}, u32[]{:S(2)}) collective-permute-start(bf16[192,768]{1,0:T(8,128)(2,1)} %get-tuple-element.317), channel_id=1, source_target_pairs={{0,8},{1,9},{2,10},{3,11},{4,12},{5,13},{6,14},{7,15},{8,0},{9,1},... | collective-permute-start | bytes 884744 | tf_op jit(solution)/shard_map/ppermute | solution.py:868
  561.5 29.2 %collective-permute-start.44 = (bf16[192,768]{1,0:T(8,128)(2,1)}, bf16[192,768]{1,0:T(8,128)(2,1)}, u32[]{:S(2)}, u32[]{:S(2)}) collective-permute-start(bf16[192,768]{1,0:T(8,128)(2,1)} %get-tuple-element.316), channel_id=1, source_target_pairs={{0,12},{1,13},{2,14},{3,15},{4,0},{5,1},{6,2},{7,3},{8,4},{9,5},{1... | collective-permute-start | bytes 884744 | tf_op jit(solution)/shard_map/ppermute | solution.py:868
  599.2 66.9 %collective-permute-start.62 = (bf16[384,768]{1,0:T(8,128)(2,1)S(1)}, bf16[384,768]{1,0:T(8,128)(2,1)S(1)}, u32[]{:S(2)}, u32[]{:S(2)}) collective-permute-start(bf16[384,768]{1,0:T(8,128)(2,1)S(1)} %get-tuple-element.315), channel_id=1, source_target_pairs={{0,17},{1,16},{2,19},{3,18},{4,21},{5,20},{6,23},{7,22},{8,25},{9,... | collective-permute-start | bytes 1769480 | tf_op jit(solution)/shard_map/ppermute | solution.py:868
  604.8 7.3 collective-permute-start.50
  604.8 7.3 collective-permute-start.49
  605.8 60.3 %collective-permute-start.61 = (bf16[384,768]{1,0:T(8,128)(2,1)S(1)}, bf16[384,768]{1,0:T(8,128)(2,1)S(1)}, u32[]{:S(2)}, u32[]{:S(2)}) collective-permute-start(bf16[384,768]{1,0:T(8,128)(2,1)S(1)} %dynamic-slice_bitcast_fusion.9), channel_id=1, source_target_pairs={{0,16},{1,17},{2,18},{3,19},{4,20},{5,21},{6,22},{7,23},{8,24},{9,... | collective-permute-start | bytes 1769480 | tf_op jit(solution)/shard_map/ppermute | solution.py:868
  607.8 58.3 %collective-permute-start.60 = (bf16[384,768]{1,0:T(8,128)(2,1)S(1)}, bf16[384,768]{1,0:T(8,128)(2,1)S(1)}, u32[]{:S(2)}, u32[]{:S(2)}) collective-permute-start(bf16[384,768]{1,0:T(8,128)(2,1)S(1)} %get-tuple-element.314), channel_id=1, source_target_pairs={{0,1},{1,0},{2,3},{3,2},{4,5},{5,4},{6,7},{7,6},{8,9},{9,8},{10,11... | collective-permute-start | bytes 1769480 | tf_op jit(solution)/shard_map/ppermute | solution.py:868
  612.9 16.8 %collective-permute-start.54 = (f32[2,72,128]{2,1,0:T(8,128)S(1)}, f32[2,72,128]{2,1,0:T(8,128)S(1)}, u32[]{:S(2)}, u32[]{:S(2)}) collective-permute-start(f32[2,72,128]{2,1,0:T(8,128)S(1)} %add_add_fusion.1), channel_id=1, source_target_pairs={{0,17},{1,16},{2,19},{3,18},{4,21},{5,20},{6,23},{7,22},{8,25},{9,... | collective-permute-start | bytes 221192 | tf_op jit(solution)/shard_map/ppermute | solution.py:868
  613.4 20.4 %collective-permute-start.53 = (f32[2,72,128]{2,1,0:T(8,128)S(1)}, f32[2,72,128]{2,1,0:T(8,128)S(1)}, u32[]{:S(2)}, u32[]{:S(2)}) collective-permute-start(f32[2,72,128]{2,1,0:T(8,128)S(1)} %add_add_fusion.1), channel_id=1, source_target_pairs={{0,16},{1,17},{2,18},{3,19},{4,20},{5,21},{6,22},{7,23},{8,24},{9,... | collective-permute-start | bytes 221192 | tf_op jit(solution)/shard_map/ppermute | solution.py:868
  633.8 112.9 %collective-permute-start.47 = (bf16[640,768]{1,0:T(8,128)(2,1)}, bf16[640,768]{1,0:T(8,128)(2,1)S(1)}, u32[]{:S(2)}, u32[]{:S(2)}) collective-permute-start(bf16[640,768]{1,0:T(8,128)(2,1)} %get-tuple-element.309), channel_id=1, source_target_pairs={{0,17},{1,16},{2,19},{3,18},{4,21},{5,20},{6,23},{7,22},{8,25},{9,... | collective-permute-start | bytes 2949128 | tf_op jit(solution)/shard_map/ppermute | solution.py:868
  635.5 29.2 %collective-permute-start.55 = (bf16[192,768]{1,0:T(8,128)(2,1)S(1)}, bf16[192,768]{1,0:T(8,128)(2,1)S(1)}, u32[]{:S(2)}, u32[]{:S(2)}) collective-permute-start(bf16[192,768]{1,0:T(8,128)(2,1)S(1)} %get-tuple-element.328), channel_id=1, source_target_pairs={{0,16},{1,17},{2,18},{3,19},{4,20},{5,21},{6,22},{7,23},{8,24},{9,... | collective-permute-start | bytes 884744 | tf_op jit(solution)/shard_map/ppermute | solution.py:868
  665.7 29.6 %collective-permute-start.58 = (bf16[2,192,768]{2,1,0:T(8,128)(2,1)}, bf16[2,192,768]{2,1,0:T(8,128)(2,1)}, u32[]{:S(2)}, u32[]{:S(2)}) collective-permute-start(bf16[2,192,768]{2,1,0:T(8,128)(2,1)} %maximum_select_fusion.7), channel_id=1, source_target_pairs={{0,12},{1,13},{2,14},{3,15},{4,0},{5,1},{6,2},{7,3},{8,4},{9,5},{1... | collective-permute-start | bytes 1769480 | tf_op jit(solution)/shard_map/ppermute | solution.py:868
  667.3 15.6 %collective-permute-start.65 = (bf16[96,768]{1,0:T(8,128)(2,1)}, bf16[96,768]{1,0:T(8,128)(2,1)S(1)}, u32[]{:S(2)}, u32[]{:S(2)}) collective-permute-start(bf16[96,768]{1,0:T(8,128)(2,1)} %get-tuple-element.325), channel_id=1, source_target_pairs={{0,12},{1,13},{2,14},{3,15},{4,0},{5,1},{6,2},{7,3},{8,4},{9,5},{1... | collective-permute-start | bytes 442376 | tf_op jit(solution)/shard_map/ppermute | solution.py:868
  669.8 23.3 %collective-permute-start.64 = (bf16[96,768]{1,0:T(8,128)(2,1)}, bf16[96,768]{1,0:T(8,128)(2,1)}, u32[]{:S(2)}, u32[]{:S(2)}) collective-permute-start(bf16[96,768]{1,0:T(8,128)(2,1)} %get-tuple-element.326), channel_id=1, source_target_pairs={{0,8},{1,9},{2,10},{3,11},{4,12},{5,13},{6,14},{7,15},{8,0},{9,1},... | collective-permute-start | bytes 442376 | tf_op jit(solution)/shard_map/ppermute | solution.py:868
  669.8 24.6 %collective-permute-start.63 = (bf16[96,768]{1,0:T(8,128)(2,1)}, bf16[96,768]{1,0:T(8,128)(2,1)}, u32[]{:S(2)}, u32[]{:S(2)}) collective-permute-start(bf16[96,768]{1,0:T(8,128)(2,1)} %get-tuple-element.324), channel_id=1, source_target_pairs={{0,4},{1,5},{2,6},{3,7},{4,8},{5,9},{6,10},{7,11},{8,12},{9,13},{1... | collective-permute-start | bytes 442376 | tf_op jit(solution)/shard_map/ppermute | solution.py:868
  682.9 63.8 %collective-permute-start.46 = (bf16[640,768]{1,0:T(8,128)(2,1)}, bf16[640,768]{1,0:T(8,128)(2,1)}, u32[]{:S(2)}, u32[]{:S(2)}) collective-permute-start(bf16[640,768]{1,0:T(8,128)(2,1)} %get-tuple-element.308), channel_id=1, source_target_pairs={{0,16},{1,17},{2,18},{3,19},{4,20},{5,21},{6,22},{7,23},{8,24},{9,... | collective-permute-start | bytes 2949128 | tf_op jit(solution)/shard_map/ppermute | solution.py:868
  693.1 55.1 %collective-permute-start.45 = (bf16[640,768]{1,0:T(8,128)(2,1)}, bf16[640,768]{1,0:T(8,128)(2,1)}, u32[]{:S(2)}, u32[]{:S(2)}) collective-permute-start(bf16[640,768]{1,0:T(8,128)(2,1)} %get-tuple-element.306), channel_id=1, source_target_pairs={{0,1},{1,0},{2,3},{3,2},{4,5},{5,4},{6,7},{7,6},{8,9},{9,8},{10,11... | collective-permute-start | bytes 2949128 | tf_op jit(solution)/shard_map/ppermute | solution.py:868
  694.4 40.3 %collective-permute-start.57 = (bf16[2,192,768]{2,1,0:T(8,128)(2,1)}, bf16[2,192,768]{2,1,0:T(8,128)(2,1)S(1)}, u32[]{:S(2)}, u32[]{:S(2)}) collective-permute-start(bf16[2,192,768]{2,1,0:T(8,128)(2,1)} %maximum_select_fusion.7), channel_id=1, source_target_pairs={{0,8},{1,9},{2,10},{3,11},{4,12},{5,13},{6,14},{7,15},{8,0},{9,1},... | collective-permute-start | bytes 1769480 | tf_op jit(solution)/shard_map/ppermute | solution.py:868
  695.2 40.0 %collective-permute-start.56 = (bf16[2,192,768]{2,1,0:T(8,128)(2,1)}, bf16[2,192,768]{2,1,0:T(8,128)(2,1)S(1)}, u32[]{:S(2)}, u32[]{:S(2)}) collective-permute-start(bf16[2,192,768]{2,1,0:T(8,128)(2,1)} %maximum_select_fusion.7), channel_id=1, source_target_pairs={{0,4},{1,5},{2,6},{3,7},{4,8},{5,9},{6,10},{7,11},{8,12},{9,13},{1... | collective-permute-start | bytes 1769480 | tf_op jit(solution)/shard_map/ppermute | solution.py:868
  734.6 11.2 %collective-permute-start.66 = (bf16[96,768]{1,0:T(8,128)(2,1)S(1)}, bf16[96,768]{1,0:T(8,128)(2,1)S(1)}, u32[]{:S(2)}, u32[]{:S(2)}) collective-permute-start(bf16[96,768]{1,0:T(8,128)(2,1)S(1)} %get-tuple-element.333), channel_id=1, source_target_pairs={{0,16},{1,17},{2,18},{3,19},{4,20},{5,21},{6,22},{7,23},{8,24},{9,... | collective-permute-start | bytes 442376 | tf_op jit(solution)/shard_map/ppermute | solution.py:868
  745.1 54.4 %collective-permute-start.59 = (bf16[2,768,768]{2,1,0:T(8,128)(2,1)}, bf16[2,768,768]{2,1,0:T(8,128)(2,1)}, u32[]{:S(2)}, u32[]{:S(2)}) collective-permute-start(bf16[2,768,768]{2,1,0:T(8,128)(2,1)} %bitcast.57), channel_id=1, source_target_pairs={{0,2},{1,3},{2,0},{3,1},{4,6},{5,7},{6,4},{7,5},{8,10},{9,11},{10,... | collective-permute-start | bytes 7077896 | tf_op jit(solution)/shard_map/ppermute | solution.py:868
  746.6 10.1 %collective-permute-start.69 = (bf16[2,96,768]{2,1,0:T(8,128)(2,1)}, bf16[2,96,768]{2,1,0:T(8,128)(2,1)S(1)}, u32[]{:S(2)}, u32[]{:S(2)}) collective-permute-start(bf16[2,96,768]{2,1,0:T(8,128)(2,1)} %maximum_select_fusion.9), channel_id=1, source_target_pairs={{0,12},{1,13},{2,14},{3,15},{4,0},{5,1},{6,2},{7,3},{8,4},{9,5},{1... | collective-permute-start | bytes 884744 | tf_op jit(solution)/shard_map/ppermute | solution.py:868
  746.6 25.9 %collective-permute-start.68 = (bf16[2,96,768]{2,1,0:T(8,128)(2,1)}, bf16[2,96,768]{2,1,0:T(8,128)(2,1)S(1)}, u32[]{:S(2)}, u32[]{:S(2)}) collective-permute-start(bf16[2,96,768]{2,1,0:T(8,128)(2,1)} %maximum_select_fusion.9), channel_id=1, source_target_pairs={{0,8},{1,9},{2,10},{3,11},{4,12},{5,13},{6,14},{7,15},{8,0},{9,1},... | collective-permute-start | bytes 884744 | tf_op jit(solution)/shard_map/ppermute | solution.py:868
  746.7 25.8 %collective-permute-start.67 = (bf16[2,96,768]{2,1,0:T(8,128)(2,1)}, bf16[2,96,768]{2,1,0:T(8,128)(2,1)S(1)}, u32[]{:S(2)}, u32[]{:S(2)}) collective-permute-start(bf16[2,96,768]{2,1,0:T(8,128)(2,1)} %maximum_select_fusion.9), channel_id=1, source_target_pairs={{0,4},{1,5},{2,6},{3,7},{4,8},{5,9},{6,10},{7,11},{8,12},{9,13},{1... | collective-permute-start | bytes 884744 | tf_op jit(solution)/shard_map/ppermute | solution.py:868
  779.1 16.2 %collective-permute-start.70 = (bf16[2,384,768]{2,1,0:T(8,128)(2,1)}, bf16[2,384,768]{2,1,0:T(8,128)(2,1)}, u32[]{:S(2)}, u32[]{:S(2)}) collective-permute-start(bf16[2,384,768]{2,1,0:T(8,128)(2,1)} %bitcast.72), channel_id=1, source_target_pairs={{0,2},{1,3},{2,0},{3,1},{4,6},{5,7},{6,4},{7,5},{8,10},{9,11},{10,... | collective-permute-start | bytes 3538952 | tf_op jit(solution)/shard_map/ppermute | solution.py:868
  (71 other events, 1159.3 us)

commit v3 on v2

--- a/solution.py
+++ b/solution.py
@@ -455,52 +455,111 @@
 ORDER = (1, 3, 0, 2)
 
 
-def greet_core(step):
-    group = lax.axis_index("dp")
-    other = group + 1 - 2 * lax.rem(group, 2)
-
-    @pl.when(step == 0)
-    def _():
-        barrier = pltpu.get_barrier_semaphore()
-        pl.semaphore_signal(barrier, inc=1, device_id={"dp": other}, device_id_type=MESH)
-        pl.semaphore_wait(barrier, 1)
-
-    return other
-
-
-def sum_with_core(step, other, index, grad_of, sent, came, out_ref, send_sems, recv_sems):
-    def copy_of(slot):
+class Neighbours:
+    def __init__(self, count):
+        self.section, self.group, self.lane = [lax.axis_index(axis) for axis in AXES]
+        self.core = lax.rem(self.group, 2)
+        self.z_index = self.group // 2
+        self.count = count
+        self.twin = (self.section, self.group + 1 - 2 * self.core, self.lane)
+        self.beside = (self.section, self.group, 1 - self.lane)
+        self.across = (1 - self.section, self.group, self.lane)
+        self.far = (1 - self.section, self.group, 1 - self.lane)
+        self.line = [self.along(step) for step in range(1, count)]
+
+    def along(self, step):
+        return (self.section, lax.rem(self.z_index + step + self.count, self.count) * 2 + self.core, self.lane)
+
+    def slot_of(self, index):
+        return 2 * (self.lane + (index // 2) * (1 - 2 * self.lane)) + self.core + (index % 2) * (1 - 2 * self.core)
+
+
+def greet(devices):
+    barrier = pltpu.get_barrier_semaphore()
+    for device in devices:
+        pl.semaphore_signal(barrier, inc=1, device_id=device, device_id_type=MESH)
+    pl.semaphore_wait(barrier, len(devices))
+
+
+class Remote:
+    def __init__(self, sends, receives):
+        self.sends, self.receives, self.slot = sends, receives, 0
+
+    def reserve(self, number):
+        self.slot += number
+        return self.slot - number
+
+    def copy(self, source, target, device, slot=None):
+        slot = self.reserve(1) if slot is None else slot
         return pltpu.make_async_remote_copy(
-            src_ref=sent.at[slot],
-            dst_ref=came.at[slot],
-            send_sem=send_sems.at[slot],
-            recv_sem=recv_sems.at[slot],
-            device_id={"dp": other},
+            src_ref=source,
+            dst_ref=target,
+            send_sem=self.sends.at[slot],
+            recv_sem=self.receives.at[slot],
+            device_id=device,
             device_id_type=MESH,
         )
 
+
+def sum_with_core(index, copies, grad_of, sent, came, put):
     slot = index % 2
     if index < 2:
-        grad_of(lambda where, value: sent.__setitem__((slot,) + where, value.astype(BF16)))
-        copy_of(slot).start()
+
+        def keep(where, value):
+            sent[(slot,) + where] = value.astype(BF16)
+
+        grad_of(keep)
+        copies[slot].start()
     else:
-        copy_of(slot).wait_recv()
-        grad_of(
-            lambda where, value: out_ref.__setitem__(
-                (0,) + where, (value + came[(slot,) + where].astype(F32)).astype(BF16)
-            )
-        )
-        copy_of(slot).wait_send()
-
-
-def feed_backward_kernel(grad_ref, middle_ref, norm_ref, *rest, columns):
+        copies[slot].wait_recv()
+
+        def add(where, value):
+            put(slot, where, (value + came[(slot,) + where].astype(F32)).astype(BF16))
+
+        grad_of(add)
+        copies[slot].wait_send()
+
+
+def plane_copies(remote, near, sums, target, half, columns):
+    size = sums.shape[1] // 2
+    mine = pl.ds(pl.multiple_of(near.section * size, size), size)
+    theirs = pl.ds(pl.multiple_of((1 - near.section) * size, size), size)
+    return [
+        remote.copy(sums.at[1, mine, columns], target.at[0, :, columns], near.beside),
+        remote.copy(sums.at[0, theirs, columns], target.at[1, :, columns], near.across),
+        remote.copy(sums.at[1, theirs, columns], target.at[2, :, columns], near.far),
+    ]
+
+
+def line_copies(remote, near, part, target, columns):
+    size = part.shape[0] // near.count
+    copies = []
+    for i, device in enumerate(near.line):
+        to = lax.rem(near.z_index + i + 1, near.count)
+        rows = pl.ds(pl.multiple_of(to * size, size), size)
+        copies.append(remote.copy(part.at[rows, columns], target.at[i, :, columns], device))
+    return copies
+
+
+def line_total(near, part, came, columns):
+    size = came.shape[1]
+    total = part[pl.ds(pl.multiple_of(near.z_index * size, size), size), columns].astype(F32)
+    for i in range(near.count - 1):
+        total = total + came[i, :, columns].astype(F32)
+    return total
+
+
+def feed_backward_kernel(grad_ref, middle_ref, norm_ref, *rest, columns, rider, line):
     pieces = 4
     rest = list(rest)
     actives = [rest.pop(0) for _ in range(pieces)]
     slopes = [rest.pop(0) for _ in range(pieces)]
     ups = [rest.pop(0) for _ in range(pieces)]
     downs = [rest.pop(0) for _ in range(pieces)]
-    weight_grad_ref, up_shift_grad_ref, middle_grad_ref, small_ref = rest[:4]
+    rider_ref = rest.pop(0) if rider else None
+    keep_ref, beside_ref, across_ref, far_ref = [rest.pop(0) for _ in range(4)]
+    up_shift_grad_ref, middle_grad_ref, small_ref = [rest.pop(0) for _ in range(3)]
+    rider_out_ref = rest.pop(0) if rider else None
     (
         normed_t,
         grad_t,
@@ -513,14 +572,26 @@
         sent,
         came,
         sems,
-        send_sems,
-        recv_sems,
-    ) = rest[4:]
+        sends,
+        receives,
+    ) = rest[:13]
     step = pl.program_id(0)
     rows_all, width = grad_ref.shape
     size = up_weight.shape[2]
     blocks = blocks_of(grad_ref)
-    other = greet_core(step)
+    near = Neighbours(line)
+    remote = Remote(sends, receives)
+    core_copies = [remote.copy(sent.at[slot], came.at[slot], near.twin) for slot in range(2)]
+    devices = [near.twin]
+    rider_copies = []
+    if rider:
+        rider_own, rider_came, rider_sem = rest[13:]
+        devices += [near.beside, near.across, near.far]
+        half = rider_own.shape[0]
+        rider_copies = plane_copies(remote, near, rider_ref, rider_came, half, slice(None))
+        rider_keep = pltpu.make_async_copy(
+            rider_ref.at[0, pl.ds(pl.multiple_of(near.section * half, half), half)], rider_own, rider_sem.at[0]
+        )
     copies = []
     for slot, i in enumerate(ORDER):
         own = pl.ds(columns[i] * size, size)
@@ -537,6 +608,10 @@
     @pl.when(step == 0)
     def _():
         run_copies(copies[0])
+        greet(devices)
+        if rider:
+            run_copies(rider_copies)
+            rider_keep.start()
 
         def prepare(i, carry):
             rows = block_at(i)
@@ -564,14 +639,25 @@
                 shift_grad = shift_grad + jnp.sum(hidden_grad, axis=0, keepdims=True)
                 term = nt(low, up_weight[at])
                 normed_grad[rows, :] = term if index == 0 else normed_grad[rows, :] + term
-            up_shift_grad_ref[0] = shift_grad
+            up_shift_grad_ref[near.slot_of(ORDER[index])] = shift_grad
 
             def grad_of(put):
                 for rows in big_blocks(width):
                     put((0, rows, slice(None)), nn(normed_t[rows, :], low_grad[...]))
                     put((1, rows, slice(None)), nn(grad_t[rows, :], active[at]))
 
-            sum_with_core(step, other, index, grad_of, sent, came, weight_grad_ref, send_sems, recv_sems)
+            def put(slot, where, value):
+                inner, outer = ((keep_ref, across_ref), (beside_ref, far_ref))[slot]
+
+                @pl.when(near.section == where[0])
+                def _():
+                    inner[where[1:]] = value
+
+                @pl.when(near.section != where[0])
+                def _():
+                    outer[where[1:]] = value
+
+            sum_with_core(index, core_copies, grad_of, sent, came, put)
 
     @pl.when(step == pieces - 1)
     def _():
@@ -589,55 +675,64 @@
         sums = lax.fori_loop(0, blocks, finish, (zero, zero, zero, zero))
         for index, row in enumerate(sums):
             small_ref[index : index + 1, :] = row
-
-
-def tensor_slot(step):
-    return lax.max(step - 2, 0)
-
-
-def feed_backward(grad, middle, norm, actives, slopes, columns, ups, downs, collective):
+        if rider:
+            rider_keep.wait()
+            wait_copies(rider_copies)
+            total = rider_own[...].astype(F32)
+            for i in range(3):
+                total = total + rider_came[i].astype(F32)
+            rider_out_ref[...] = total.astype(BF16)
+
+
+def feed_backward(grad, middle, norm, actives, slopes, columns, ups, downs, collective, rider=None):
     rows, width = middle.shape
     pieces = len(ups)
     size = ups[0].shape[1]
-    operands = [*actives, *slopes, *ups, *downs]
+    operands = [*actives, *slopes, *ups, *downs] + ([] if rider is None else [rider])
+    outs = [jax.ShapeDtypeStruct((width, size), BF16)] * 4 + [
+        jax.ShapeDtypeStruct((pieces, 1, size), F32),
+        jax.ShapeDtypeStruct((rows, width), F32),
+        jax.ShapeDtypeStruct((4, width), F32),
+    ]
+    scratch = [
+        pltpu.VMEM((width, rows), BF16),
+        pltpu.VMEM((width, rows), BF16),
+        pltpu.VMEM((rows, width), F32),
+        pltpu.VMEM((2, width, size), BF16),
+        pltpu.VMEM((2, size, width), BF16),
+        pltpu.VMEM((2, rows, size), BF16),
+        pltpu.VMEM((2, rows, size), BF16),
+        pltpu.VMEM((rows, size), BF16),
+        pltpu.VMEM((2, 2, width, size), BF16),
+        pltpu.VMEM((2, 2, width, size), BF16),
+        pltpu.SemaphoreType.DMA((4, 2)),
+        pltpu.SemaphoreType.DMA((8,)),
+        pltpu.SemaphoreType.DMA((8,)),
+    ]
+    if rider is not None:
+        half = rider.shape[1] // 2
+        outs.append(jax.ShapeDtypeStruct((half, width), BF16))
+        scratch += [
+            pltpu.VMEM((half, width), BF16),
+            pltpu.VMEM((3, half, width), BF16),
+            pltpu.SemaphoreType.DMA((1,)),
+        ]
     return pl.pallas_call(
-        functools.partial(feed_backward_kernel, columns=columns),
+        functools.partial(
+            feed_backward_kernel, columns=columns, rider=rider is not None, line=lax.axis_size("dp") // 2
+        ),
         grid=(pieces,),
         in_specs=[once((rows, width)), once((rows, width)), once((2, width))] + anywhere(len(operands)),
-        out_specs=[
-            pl.BlockSpec((1, 2, width, size), lambda i: (tensor_slot(i), 0, 0, 0)),
-            pl.BlockSpec((1, 1, size), lambda i: (i, 0, 0)),
-            once((rows, width)),
-            once((4, width)),
-        ],
-        scratch_shapes=[
-            pltpu.VMEM((width, rows), BF16),
-            pltpu.VMEM((width, rows), BF16),
-            pltpu.VMEM((rows, width), F32),
-            pltpu.VMEM((2, width, size), BF16),
-            pltpu.VMEM((2, size, width), BF16),
-            pltpu.VMEM((2, rows, size), BF16),
-            pltpu.VMEM((2, rows, size), BF16),
-            pltpu.VMEM((rows, size), BF16),
-            pltpu.VMEM((2, 2, width, size), BF16),
-            pltpu.VMEM((2, 2, width, size), BF16),
-            pltpu.SemaphoreType.DMA((4, 2)),
-            pltpu.SemaphoreType.DMA((2,)),
-            pltpu.SemaphoreType.DMA((2,)),
-        ],
-        out_shape=[
-            jax.ShapeDtypeStruct((2, 2, width, size), BF16),
-            jax.ShapeDtypeStruct((pieces, 1, size), F32),
-            jax.ShapeDtypeStruct((rows, width), F32),
-            jax.ShapeDtypeStruct((4, width), F32),
-        ],
+        out_specs=[once(out.shape) for out in outs],
+        scratch_shapes=scratch,
+        out_shape=outs,
         name="feed_backward",
         **settings(16_000_000_000, collective),
     )(grad, middle, norm, *operands)
 
 
 def mixer_backward_kernel(
-    start_ref, tiles_ref, seg_ref, middle_grad_ref, qkv_ref_all, *rest, saved, heads
+    place_ref, start_ref, tiles_ref, seg_ref, middle_grad_ref, qkv_ref_all, *rest, saved, heads
 ):
     pieces = len(saved)
     rest = [qkv_ref_all] + list(rest)
@@ -686,7 +781,7 @@
     )
     gradient = sums[...]
     projected_ref[0] = gradient.astype(BF16)
-    qkv_shift_grad_ref[0] = jnp.sum(gradient, axis=1, keepdims=True)
+    qkv_shift_grad_ref[0] = jnp.sum(gradient, axis=1, keepdims=True).T
 
 
 def mixer_backward(images, middle_grad, qkvs, mixeds, log_totals, saved, weights):
@@ -699,12 +794,12 @@
     return pl.pallas_call(
         functools.partial(mixer_backward_kernel, saved=saved, heads=heads),
         grid_spec=pltpu.PrefetchScalarGridSpec(
-            num_scalar_prefetch=2,
+            num_scalar_prefetch=3,
             grid=(count,),
             in_specs=[once((1, rows)), once((rows, width))] + anywhere(len(operands)),
             out_specs=[
                 pl.BlockSpec((1, 3 * cols, rows), lambda i, *_: (i, 0, 0)),
-                pl.BlockSpec((1, 3 * cols, 1), lambda i, *_: (i, 0, 0)),
+                pl.BlockSpec((1, 1, 3 * cols), lambda i, place, *_: (slot_of(place, i), 0, 0)),
             ],
             scratch_shapes=[
                 pltpu.VMEM((count, 3 * cols, rows), BF16),
@@ -719,24 +814,68 @@
         ),
         out_shape=[
             jax.ShapeDtypeStruct((count, 3 * cols, rows), BF16),
-            jax.ShapeDtypeStruct((count, 3 * cols, 1), F32),
+            jax.ShapeDtypeStruct((count, 1, 3 * cols), F32),
         ],
         name="mixer_backward",
         **settings(16_000_000_000),
-    )(start, tiles, segment, middle_grad, *operands)
-
-
-def input_backward_kernel(hidden_ref, middle_grad_ref, norm_ref, projected, normed_in, *rest, saved):
+    )(place, start, tiles, segment, middle_grad, *operands)
+
+
+class Line:
+    def __init__(self, remote, near, ref, size, columns):
+        self.near = near
+        self.copies = []
+        for hop in range(near.count - 1):
+            pair = []
+            for sign in (1, -1):
+                origin = lax.rem(near.z_index - sign * hop + near.count, near.count)
+                chunk = ref.at[near.core, :, pl.ds(pl.multiple_of(origin * size, size), size), columns]
+                pair.append((sign, remote.copy(chunk, chunk, near.along(sign))))
+            self.copies.append(pair)
+
+    def each(self, hop, ahead, act):
+        for sign, copy in self.copies[hop]:
+            origin = self.near.z_index - sign * (hop + 1 - ahead)
+            target = self.near.z_index + sign * ahead
+
+            @pl.when((origin >= 0) & (origin < self.near.count) & (target >= 0) & (target < self.near.count))
+            def _():
+                act(copy)
+
+    def start(self, hop):
+        self.each(hop, 1, lambda copy: copy.start())
+
+    def receive(self, hop):
+        self.each(hop, 0, lambda copy: copy.wait_recv())
+
+    def finish(self):
+        for hop in range(self.near.count - 1):
+            self.each(hop, 1, lambda copy: copy.wait_send())
+
+
+def input_backward_kernel(hidden_ref, middle_grad_ref, norm_ref, projected, normed_in, *rest, saved, line, last):
     pieces = len(saved)
     rest = list(rest)
     mixeds = [rest.pop(0) for _ in range(pieces)]
     weights = [rest.pop(0) for _ in range(pieces)]
-    weight_grad_ref, in_grad_ref, small_ref = rest[:3]
-    projected_grad, mixed, normed, low_middle, weight, sent, came, sems, send_sems, recv_sems = rest[3:]
-    step = pl.program_id(0)
+    feed_terms = [rest.pop(0) for _ in range(4)]
+    if last:
+        mixer_part1, feed_total1, other_grad = [rest.pop(0) for _ in range(3)]
+        small_refs = [rest.pop(0) for _ in range(7)]
+        feed_result, mixer_result, parts_result, vector_out = [rest.pop(0) for _ in range(4)]
+    else:
+        sums_ref, in_grad_ref, small_ref, feed_total_ref = [rest.pop(0) for _ in range(4)]
+    projected_grad, mixed, normed, low_middle, weight, sent, came = [rest.pop(0) for _ in range(7)]
+    feed_part, feed_came, sems, sends, receives = [rest.pop(0) for _ in range(5)]
     rows_all, width = hidden_ref.shape
     count = projected.shape[1]
-    other = greet_core(step)
+    near = Neighbours(line)
+    remote = Remote(sends, receives)
+    everything = slice(None)
+    devices = [near.twin] + near.line
+    if last:
+        devices += [near.beside, near.across, near.far]
+        sums_ref, in_grad_ref = rest.pop(0), rest.pop(0)
     copies = []
     for i in range(pieces):
         copies.append(
@@ -751,76 +890,330 @@
             ]
         )
     norm_copy = pltpu.make_async_copy(normed_in, normed, sems.at[3, 0])
-
-    @pl.when(step == 0)
+    norm_copy.start()
+    for i in ORDER:
+        run_copies(copies[i])
+    greet(devices)
+
+    total = feed_terms[0][...].astype(F32)
+    for term in feed_terms[1:]:
+        total = total + term[...].astype(F32)
+    feed_part[...] = total.astype(BF16)
+    feed_line = line_copies(remote, near, feed_part, feed_came, everything)
+    run_copies(feed_line)
+    if last:
+        part1_came = rest.pop(0)
+        part1_line = line_copies(remote, near, mixer_part1, part1_came, everything)
+        run_copies(part1_line)
+
+    core_copies = [remote.copy(sent.at[slot], came.at[slot], near.twin) for slot in range(2)]
+    low_middle[...] = middle_grad_ref[...].astype(BF16)
+    norm_copy.wait()
+    for index, piece in enumerate(ORDER):
+        wait_copies(copies[piece])
+
+        def grad_of(put, piece=piece):
+            own = slice(piece * count, (piece + 1) * count)
+            put((slice(0, count), everything), nn(projected_grad[own, :], normed[...]))
+            put((slice(count, width), everything), nn(mixed[piece], low_middle[...]))
+
+        def put(slot, where, value):
+            sums_ref[(slot,) + where] = value
+
+        sum_with_core(index, core_copies, grad_of, sent, came, put)
+
+    if last:
+        (
+            mixer_came,
+            mixer_part,
+            line_came,
+            feed_own,
+            feed_other,
+            mixer_own,
+            mixer_other,
+            feed_out,
+            mixer_out,
+            parts_out,
+            vector,
+            vector_came,
+            locals_,
+        ) = rest
+        chunk_width = width // 2
+        chunks = [slice(i * chunk_width, (i + 1) * chunk_width) for i in range(2)]
+        plane = [plane_copies(remote, near, sums_ref, mixer_came, None, chunk) for chunk in chunks]
+        for group in plane:
+            run_copies(group)
+
+    gain = jnp.zeros((1, width), F32)
+    shift = jnp.zeros((1, width), F32)
+    for rows in big_blocks(rows_all):
+        scaled, inverse = normalise(hidden_ref[rows, :].astype(F32))
+        gradient = tn(projected_grad[:, rows], weight[...])
+        in_grad = middle_grad_ref[rows, :] + normalise_back(gradient, scaled, inverse, norm_ref[0:1, :])
+        in_grad_ref[rows, :] = in_grad.astype(BF16)
+        gain = gain + jnp.sum(gradient * scaled, axis=0, keepdims=True)
+        shift = shift + jnp.sum(gradient, axis=0, keepdims=True)
+
+    if not last:
+        small_ref[0:1, :] = gain
+        small_ref[1:2, :] = shift
+        wait_copies(feed_line)
+        feed_total_ref[...] = line_total(near, feed_part, feed_came, everything).astype(BF16)
+        return
+
+    first = near.section == 0
+
+    def local(source, target, slot):
+        return pltpu.make_async_copy(source, target, locals_.at[slot])
+
+    def place_total(total0, total1, own_ref, other_ref, out_ref, chunk, slot):
+        own_ref[:, chunk] = jnp.where(first, total0, total1).astype(BF16)
+        other_ref[:, chunk] = jnp.where(first, total1, total0).astype(BF16)
+        size = own_ref.shape[0]
+        rows = pl.ds(pl.multiple_of(near.z_index * size, size), size)
+        spot = out_ref.at[near.core, near.section, rows, chunk]
+        keep = local(own_ref.at[:, chunk], spot, slot)
+        keep.start()
+        send = remote.copy(other_ref.at[:, chunk], spot, near.across)
+        send.start()
+        return [keep, send]
+
+    small0, ups0, shifts0, small1, ups1, shifts1, in_small1 = small_refs
+    vector[...] = jnp.zeros_like(vector)
+    ins = ((gain, shift), (in_small1[0:1, :], in_small1[1:2, :]))
+    for layer, (small, ups, shifts) in enumerate(((small0, ups0, shifts0), (small1, ups1, shifts1))):
+        rows = [ins[layer][0], small[0:1, :], ins[layer][1], small[1:2, :], small[2:3, :], small[3:4, :]]
+        for i, row in enumerate(rows):
+            vector[layer, i : i + 1, :] = row
+        for i in range(pieces):
+            vector[layer, 8 + i : 9 + i, :] = ups[i]
+            vector[layer, 12 + i : 13 + i, 0:count] = shifts[i]
+
+    def vector_round(devices, at):
+        group = [remote.copy(vector, vector_came.at[at + i], device) for i, device in enumerate(devices)]
+        run_copies(group)
+        return group
+
+    def vector_sum(group, at):
+        wait_copies(group)
+        total = vector[...]
+        for i in range(len(group)):
+            total = total + vector_came[at + i]
+        vector[...] = total
+
+    pending = vector_round([near.twin], 0)
+    wait_copies(feed_line)
+    feed_total = line_total(near, feed_part, feed_came, everything)
+    feed_pair = place_total(
+        feed_total, feed_total1[...].astype(F32), feed_own, feed_other, feed_out, everything, 0
+    )
+    vector_sum(pending, 0)
+    pending = vector_round([near.beside], 1)
+    wait_copies(part1_line)
+    half = mixer_part.shape[0]
+    mine = pl.ds(pl.multiple_of(near.section * half, half), half)
+    spreads = []
+    for group, chunk in zip(plane, chunks):
+        wait_copies(group)
+        part = sums_ref[0, mine, chunk].astype(F32)
+        for i in range(3):
+            part = part + mixer_came[i, :, chunk].astype(F32)
+        mixer_part[:, chunk] = part.astype(BF16)
+        spreads.append(line_copies(remote, near, mixer_part, line_came, chunk))
+        run_copies(spreads[-1])
+    rows = rows_all // 2
+    inner = pl.ds(pl.multiple_of(near.lane * rows, rows), rows)
+    outer = pl.ds(pl.multiple_of((1 - near.lane) * rows, rows), rows)
+    spot = parts_out.at[2 * near.section + near.lane]
+    at = remote.reserve(3)
+
+    def grad_copies(own, other):
+        return [
+            remote.copy(own.at[outer], spot, near.beside, at),
+            remote.copy(other.at[inner], spot, near.across, at + 1),
+            remote.copy(other.at[outer], spot, near.far, at + 2),
+        ]
+
+    @pl.when(first)
     def _():
-        norm_copy.start()
-        for i in ORDER:
-            run_copies(copies[i])
-        low_middle[...] = middle_grad_ref[...].astype(BF16)
-        norm_copy.wait()
-
-    for index, piece in enumerate(ORDER):
-
-        @pl.when(step == index)
-        def _():
-            wait_copies(copies[piece])
-
-            def grad_of(put):
-                own = slice(piece * count, (piece + 1) * count)
-                put((slice(0, count), slice(None)), nn(projected_grad[own, :], normed[...]))
-                put((slice(count, width), slice(None)), nn(mixed[piece], low_middle[...]))
-
-            sum_with_core(step, other, index, grad_of, sent, came, weight_grad_ref, send_sems, recv_sems)
-
-    @pl.when(step == pieces - 1)
+        run_copies([local(in_grad_ref.at[inner], spot, 3)] + grad_copies(in_grad_ref, other_grad))
+
+    @pl.when(near.section == 1)
     def _():
-        total = jnp.zeros((1, width), F32)
-        shift = jnp.zeros((1, width), F32)
-        for rows in big_blocks(rows_all):
-            scaled, inverse = normalise(hidden_ref[rows, :].astype(F32))
-            gradient = tn(projected_grad[:, rows], weight[...])
-            in_grad = middle_grad_ref[rows, :] + normalise_back(gradient, scaled, inverse, norm_ref[0:1, :])
-            in_grad_ref[rows, :] = in_grad.astype(BF16)
-            total = total + jnp.sum(gradient * scaled, axis=0, keepdims=True)
-            shift = shift + jnp.sum(gradient, axis=0, keepdims=True)
-        small_ref[0:1, :] = total
-        small_ref[1:2, :] = shift
-
-
-def input_backward(hidden, middle_grad, norm, projected, normed, mixeds, saved, weights, collective):
+        run_copies([local(other_grad.at[inner], spot, 3)] + grad_copies(other_grad, in_grad_ref))
+
+    feed_size, mixer_size = feed_own.shape[0], mixer_own.shape[0]
+    feed_chain = Line(remote, near, feed_out, feed_size, everything)
+    mixer_chains = [Line(remote, near, mixer_out, mixer_size, chunk) for chunk in chunks]
+    wait_copies(feed_pair)
+    feed_chain.start(0)
+    vector_sum(pending, 1)
+    pending = vector_round([near.across], 2)
+    pairs = []
+    for i, chunk in enumerate(chunks):
+        wait_copies(spreads[i])
+        total0 = line_total(near, mixer_part, line_came, chunk)
+        total1 = line_total(near, mixer_part1, part1_came, chunk)
+        pairs.append(place_total(total0, total1, mixer_own, mixer_other, mixer_out, chunk, 1 + i))
+    vector_sum(pending, 2)
+    pending = vector_round(near.line, 3)
+    feed_chain.receive(0)
+    feed_chain.start(1)
+    for pair, chain in zip(pairs, mixer_chains):
+        wait_copies(pair)
+        chain.start(0)
+    vector_sum(pending, 3)
+    vector_out[...] = jnp.where(first, vector[0], vector[1])
+    for hop in range(1, line - 1):
+        feed_chain.receive(hop)
+        if hop + 1 < line - 1:
+            feed_chain.start(hop + 1)
+        for chain in mixer_chains:
+            chain.receive(hop - 1)
+            chain.start(hop)
+    feed_twin = remote.copy(feed_out.at[near.core], feed_out.at[near.core], near.twin)
+    feed_twin.start()
+    for chain in mixer_chains:
+        chain.receive(line - 2)
+    mixer_twin = remote.copy(mixer_out.at[near.core], mixer_out.at[near.core], near.twin)
+    mixer_twin.start()
+    feed_twin.wait()
+    feed_chain.finish()
+    results = [local(feed_out, feed_result, 4), local(parts_out, parts_result, 5), local(mixer_out, mixer_result, 6)]
+    results[0].start()
+    for copy in grad_copies(in_grad_ref, other_grad):
+        copy.wait()
+    local(in_grad_ref.at[inner], spot, 3).wait()
+    results[1].start()
+    mixer_twin.wait()
+    for chain in mixer_chains:
+        chain.finish()
+    results[2].start()
+    wait_copies(results)
+
+
+def input_backward(
+    hidden, middle_grad, norm, projected, normed, mixeds, saved, weights, feed_terms, collective, finish=None
+):
     rows, width = hidden.shape
     number, count, _ = projected.shape
-    operands = [projected, normed, *mixeds, *weights]
-    return pl.pallas_call(
-        functools.partial(input_backward_kernel, saved=saved),
-        grid=(number,),
-        in_specs=[once((rows, width)), once((rows, width)), once((2, width))] + anywhere(len(operands)),
-        out_specs=[
-            pl.BlockSpec((1, width, width), lambda i: (tensor_slot(i), 0, 0)),
-            once((rows, width)),
-            once((2, width)),
-        ],
-        scratch_shapes=[
-            pltpu.VMEM((number * count, rows), BF16),
-            pltpu.VMEM((number, width - count, rows), BF16),
-            pltpu.VMEM((rows, width), BF16),
-            pltpu.VMEM((rows, width), BF16),
-            pltpu.VMEM((number * count, width), BF16),
-            pltpu.VMEM((2, width, width), BF16),
-            pltpu.VMEM((2, width, width), BF16),
-            pltpu.SemaphoreType.DMA((4, number)),
-            pltpu.SemaphoreType.DMA((2,)),
-            pltpu.SemaphoreType.DMA((2,)),
-        ],
-        out_shape=[
+    line = lax.axis_size("dp") // 2
+    vmem = pl.BlockSpec(memory_space=pltpu.VMEM)
+    far = pl.BlockSpec(memory_space=pl.ANY)
+    operands = [hidden, middle_grad, norm, projected, normed, *mixeds, *weights, *feed_terms]
+    specs = [vmem] * 3 + [far] * (2 + 2 * number) + [vmem] * 4
+    feed_rows, half = width // line, width // 2
+    mixer_rows = half // line
+    scratch = [
+        pltpu.VMEM((number * count, rows), BF16),
+        pltpu.VMEM((number, width - count, rows), BF16),
+        pltpu.VMEM((rows, width), BF16),
+        pltpu.VMEM((rows, width), BF16),
+        pltpu.VMEM((number * count, width), BF16),
+        pltpu.VMEM((2, width, width), BF16),
+        pltpu.VMEM((2, width, width), BF16),
+        pltpu.VMEM((width, width), BF16),
+        pltpu.VMEM((line - 1, feed_rows, width), BF16),
+        pltpu.SemaphoreType.DMA((4, number)),
+        pltpu.SemaphoreType.DMA((64,)),
+        pltpu.SemaphoreType.DMA((64,)),
+    ]
+    if finish is None:
+        outs = [
             jax.ShapeDtypeStruct((2, width, width), BF16),
             jax.ShapeDtypeStruct((rows, width), BF16),
             jax.ShapeDtypeStruct((2, width), F32),
-        ],
+            jax.ShapeDtypeStruct((feed_rows, width), BF16),
+        ]
+        out_specs = [vmem] * 4
+    else:
+        operands += list(finish)
+        specs += [vmem, vmem, far] + [vmem] * (len(finish) - 3)
+        outs = [
+            jax.ShapeDtypeStruct((2, 2, width, width), BF16),
+            jax.ShapeDtypeStruct((2, 2, half, width), BF16),
+            jax.ShapeDtypeStruct((4, rows // 2, width), BF16),
+            jax.ShapeDtypeStruct((16, width), F32),
+        ]
+        out_specs = [far] * 3 + [vmem]
+        scratch += [
+            pltpu.VMEM((2, width, width), BF16),
+            pltpu.VMEM((rows, width), BF16),
+            pltpu.VMEM((line - 1, mixer_rows, width), BF16),
+            pltpu.VMEM((3, half, width), BF16),
+            pltpu.VMEM((half, width), BF16),
+            pltpu.VMEM((line - 1, mixer_rows, width), BF16),
+            pltpu.VMEM((feed_rows, width), BF16),
+            pltpu.VMEM((feed_rows, width), BF16),
+            pltpu.VMEM((mixer_rows, width), BF16),
+            pltpu.VMEM((mixer_rows, width), BF16),
+            pltpu.VMEM((2, 2, width, width), BF16),
+            pltpu.VMEM((2, 2, half, width), BF16),
+            pltpu.VMEM((4, rows // 2, width), BF16),
+            pltpu.VMEM((2, 16, width), F32),
+            pltpu.VMEM((2 + line, 2, 16, width), F32),
+            pltpu.SemaphoreType.DMA((8,)),
+        ]
+    return pl.pallas_call(
+        functools.partial(input_backward_kernel, saved=saved, line=line, last=finish is not None),
+        in_specs=specs,
+        out_specs=out_specs,
+        scratch_shapes=scratch,
+        out_shape=outs,
         name="input_backward",
         **settings(8_000_000_000, collective),
-    )(hidden, middle_grad, norm, *operands)
+    )(*operands)
+
+
+def place_states_kernel(place_ref, *rest):
+    parts, out_ref, held, sems = rest[:4], rest[4], rest[5], rest[6]
+    inward = [pltpu.make_async_copy(part, held.at[i], sems.at[0, i]) for i, part in enumerate(parts)]
+    outward = [
+        pltpu.make_async_copy(held.at[i], out_ref.at[place_ref[2] ^ i], sems.at[1, i]) for i in range(len(parts))
+    ]
+    run_copies(inward)
+    for first, second in zip(inward, outward):
+        first.wait()
+        second.start()
+    wait_copies(outward)
+
+
+def place_states(place, parts):
+    far = pl.BlockSpec(memory_space=pl.ANY)
+    return pl.pallas_call(
+        place_states_kernel,
+        grid_spec=pltpu.PrefetchScalarGridSpec(
+            num_scalar_prefetch=1,
+            grid=(1,),
+            in_specs=[far] * 4,
+            out_specs=far,
+            scratch_shapes=[
+                pltpu.VMEM((4,) + parts[0].shape, BF16),
+                pltpu.SemaphoreType.DMA((2, 4)),
+            ],
+        ),
+        out_shape=jax.ShapeDtypeStruct((4,) + parts[0].shape, BF16),
+        name="place_states",
+        **settings(1_000_000),
+    )(place, *parts)
+
+
+def widen_kernel(low_ref, out_ref):
+    out_ref[...] = low_ref[...].astype(F32)
+
+
+def widen(parts):
+    number, rows, width = parts.shape
+    spec = pl.BlockSpec((1, rows, width), lambda i: (i, 0, 0))
+    return pl.pallas_call(
+        widen_kernel,
+        grid=(number,),
+        in_specs=[spec],
+        out_specs=spec,
+        out_shape=jax.ShapeDtypeStruct(parts.shape, F32),
+        name="widen",
+        **settings(1_000_000),
+    )(parts)
 
 
 def unpack_kernel(feed_ref, mixer_ref, qkv_ref, out_ref, up_ref, down_ref):
@@ -903,19 +1296,6 @@
     for term in terms[1:]:
         total = total + term.astype(F32)
     return total.astype(terms[0].dtype)
-
-
-def send_plane(sums, section):
-    return [
-        moved(take_part(sums[1], section, 2), over_tensor),
-        moved(take_part(sums[0], 1 - section, 2), over_section),
-        moved(take_part(sums[1], 1 - section, 2), over_both),
-    ]
-
-
-def send_line(part, z_index):
-    count = lax.axis_size("dp") // 2
-    return [moved(take_part(part, (z_index + step) % count, count), along_z(step)) for step in range(1, count)]
 
 
 def reordered(pieces, lane, core):
@@ -978,7 +1358,7 @@
     begin = jnp.sum((segment < ids).astype(jnp.int32), axis=1)
     end = jnp.sum((segment <= ids).astype(jnp.int32), axis=1)
     start = begin // TILE
-    place = jnp.stack([lane, core]).astype(jnp.int32)
+    place = jnp.stack([lane, core, mine]).astype(jnp.int32)
     images = (place, start, (end - 1) // TILE - start + 1, segment)
 
     def params(vector):
@@ -1099,16 +1479,11 @@
             moved(take_part(other, 1 - lane, 2), over_both),
         ]
 
-    def ordered(relative):
-        relative = jnp.stack(relative)
-        relative = jnp.where(lane == 0, relative, relative[jnp.array([1, 0, 3, 2])])
-        return jnp.where(section == 0, relative, relative[jnp.array([2, 3, 0, 1])])
-
     out_parts = exchange(
         jnp.where(section == 0, first_out, second_out), jnp.where(section == 0, second_out, first_out)
     )
 
-    def feed_back(layer, grad):
+    def feed_back(layer, grad, rider=None):
         kept = saved[layer]
         return feed_backward(
             grad,
@@ -1120,6 +1495,7 @@
             up_pieces[layer],
             down_pieces[layer],
             layer,
+            rider,
         )
 
     def mixer_back(layer, middle_grad):
@@ -1128,7 +1504,7 @@
             images, middle_grad, kept["qkv"], kept["mixed"], kept["totals"], kept["at"], mixer_pieces[layer]
         )
 
-    def input_back(layer, middle_grad, projected):
+    def input_back(layer, middle_grad, projected, feed_terms, finish=None):
         kept = saved[layer]
         return input_backward(
             kept["state"],
@@ -1139,89 +1515,55 @@
             kept["mixed"],
             kept["at"],
             mixer_pieces[layer],
+            feed_terms,
             2 + layer,
-        )
-
-    def small_vector(feed, mixer, in_small):
-        shifts = reordered(mixer[1].reshape(4, 3, part), lane, core)
-        ups = reordered(feed[1].reshape(4, -1)[jnp.array([2, 0, 3, 1])], lane, core)
-        return jnp.concatenate(
-            [
-                in_small[0],
-                feed[3][0],
-                in_small[1],
-                feed[3][1],
-                shifts[:, 0].reshape(-1),
-                shifts[:, 2].reshape(-1),
-                ups.reshape(-1),
-                feed[3][2],
-                feed[3][3],
-            ]
-        ).reshape(-1, TILE)
-
-    def plane_sum(sums, came):
-        return added(take_part(sums[0], section, 2), *came)
-
-    def line_sum(block, came):
-        return added(take_part(block, z_index, z_count), *came)
+            finish,
+        )
+
+    def send_plane(blocks):
+        return [
+            moved(block, change) for block, change in zip(blocks, (over_tensor, over_section, over_both))
+        ]
 
     feed1, out_parts = tie(feed_back(1, grad), out_parts)
-    feed_sums1 = feed1[0].reshape(2, -1, width)
-    mixer1, came = tie(mixer_back(1, feed1[2]), send_plane(feed_sums1, section))
-    feed_part1 = plane_sum(feed_sums1, came)
-    input1 = input_back(1, feed1[2], mixer1[0])
-    in_grad1 = input1[1]
-    feed0, came, came_line = tie(
-        feed_back(0, in_grad1), send_plane(input1[0], section), send_line(feed_part1, z_index)
-    )
-    mixer_part1 = plane_sum(input1[0], came)
-    feed_total1 = line_sum(feed_part1, came_line)
-    feed_sums0 = feed0[0].reshape(2, -1, width)
-    mixer0, came, came_line = tie(
-        mixer_back(0, feed0[2]), send_plane(feed_sums0, section), send_line(mixer_part1, z_index)
-    )
-    feed_part0 = plane_sum(feed_sums0, came)
-    mixer_total1 = line_sum(mixer_part1, came_line)
-    input0, came_line = tie(input_back(0, feed0[2], mixer0[0]), send_line(feed_part0, z_index))
-    feed_total0 = line_sum(feed_part0, came_line)
-    mixer_part0 = plane_sum(input0[0], send_plane(input0[0], section))
-    mixer_total0 = line_sum(mixer_part0, send_line(mixer_part0, z_index))
-    in_parts = exchange(
-        jnp.where(section == 0, input0[1], in_grad1), jnp.where(section == 0, in_grad1, input0[1])
-    )
-    vector = jnp.stack([small_vector(feed0, mixer0, input0[2]), small_vector(feed1, mixer1, input1[2])])
-    vector = vector + moved(vector, over_core)
-    vector = added(vector, *[moved(vector, along_z(step)) for step in range(1, z_count)])
-    vector = added(vector, *[moved(vector, change) for change in (over_tensor, over_section, over_both)])
-    vector = jnp.where(section == 0, vector[0], vector[1]).reshape(-1)
-
-    def whole(total0, total1):
-        own = jnp.where(section == 0, total0, total1)
-        came = moved(jnp.where(section == 0, total1, total0), over_section)
-        both = jnp.where(section == 0, jnp.stack([own, came]), jnp.stack([came, own]))
-        parts = [both] + [moved(both, along_z(step)) for step in range(1, z_count)]
-        order = (z_index - jnp.arange(z_count)) % z_count
-        line = jnp.stack(parts)[order].transpose(1, 0, 2, 3).reshape(2, -1, width)
-        twin = moved(line, over_core)
-        return jnp.where(core == 0, jnp.stack([line, twin]), jnp.stack([twin, line]))
-
-    feed_sum = whole(feed_total0, feed_total1)
-    mixer_sum = whole(mixer_total0, mixer_total1).reshape(2, 4 * part, width)
-    qkv_grad, out_grad, up_grad, down_grad = unpack(feed_sum, mixer_sum)
-    states = ordered(out_parts)
-    grads = ordered(in_parts).astype(F32)
+    mixer1, came = tie(mixer_back(1, feed1[5]), send_plane(feed1[1:4]))
+    mixer_sums1, in_grad1, in_small1, feed_total1 = input_back(1, feed1[5], mixer1[0], [feed1[0], *came])
+    feed0 = feed_back(0, in_grad1, mixer_sums1)
+    mixer0, came = tie(mixer_back(0, feed0[5]), send_plane(feed0[1:4]))
+    feed_sum, mixer_sum, in_parts, vector = input_back(
+        0,
+        feed0[5],
+        mixer0[0],
+        [feed0[0], *came],
+        [
+            feed0[7],
+            feed_total1,
+            in_grad1,
+            feed0[6],
+            feed0[4],
+            mixer0[1],
+            feed1[6],
+            feed1[4],
+            mixer1[1],
+            in_small1,
+        ],
+    )
+    qkv_grad, out_grad, up_grad, down_grad = unpack(feed_sum, mixer_sum.reshape(2, 4 * part, width))
+    states = place_states(place, out_parts)
+    grads = widen(in_parts)
+    qv_grad = vector[12:16, : 3 * part].reshape(4, 3, part)
     return (
         states[None],
         grads[None],
-        vector[: 2 * width].reshape(1, 2, width),
-        vector[2 * width : 4 * width].reshape(1, 2, width),
+        vector[0:2][None],
+        vector[2:4][None],
         qkv_grad[None],
-        vector[4 * width : 6 * width].reshape(1, 2, width),
+        jnp.stack([qv_grad[:, 0].reshape(width), qv_grad[:, 2].reshape(width)])[None],
         out_grad[None],
         up_grad[None],
-        vector[6 * width : 6 * width + hidden].reshape(1, hidden),
+        vector[8:12].reshape(1, hidden),
         down_grad[None],
-        vector[6 * width + hidden :].reshape(1, 2, width),
+        vector[4:6][None],
     )
 
 

time: 826 us -> 673 us (0.81)
  Pallas kernels: 347 us -> 523 us
  waiting for transfers between devices: 181 us -> 60 us
  local copies, waits for them, and re-layouts: 112 us -> 32.7 us
  other arithmetic: 90.1 us -> 21.5 us
  starting transfers between devices: 84 us -> 29.4 us
    pallas_call x4 -> x6, Pallas kernels: 122 us -> 291 us  [the longest x2 190 us: input_backward(): pl.pallas_call(functools.partial(input_backward_kernel, saved=saved, line...]
    ppermute x71 -> x33, waiting for transfers between devices: 181 us -> 60 us  [moved(): return lax.ppermute(block, AXES, route(change))]
    ppermute x71 -> x33, starting transfers between devices: 84 us -> 29.4 us  [moved(): return lax.ppermute(block, AXES, route(change))]
    gather x16 -> x0, local copies, waits for them, and re-layouts: 35.6 us -> none  [the longest x2 9.92 us: ordered(): return jnp.where(section == 0, relative, relative[jnp.array([2, 3, 0, 1])])]
    select_n x20 -> x0, other arithmetic: 33.1 us -> none  [the longest x2 11.1 us: whole(): jnp.where(core == 0, jnp.stack([line, twin]), jnp.stack([twin, line]))]
    another operation x10 -> x1, other arithmetic: 15.7 us -> 0.66 us  [one_sequence_each(): place = jnp.stack([lane, core, mine]).astype(jnp.int32)]
    convert_element_type x5 -> x0, other arithmetic: 13.7 us -> none  [the longest x4 7.42 us: added(): return total.astype(terms[0].dtype)]
    dynamic_slice x19 -> x6, local copies, waits for them, and re-layouts: 17.6 us -> 7.1 us  [take_part(): return lax.dynamic_slice_in_dim(block, which * size, size, axis)]
  transfers between devices with their start and end apart: 71 -> 33, of which waited for: 17 -> 8; matrix products, arithmetic and copies ran while one was open for 18% -> 5% of each run, Pallas kernels for 39% -> 40%
where the time goes in v3:
time: 673 us; the launch traced here: 668 us
  Pallas kernels  523 us (78%)
  waiting for transfers between devices  60 us (9%)
  local copies, waits for them, and re-layouts  32.7 us (5%)
  starting transfers between devices  29.4 us (4%)
  other arithmetic  21.5 us (3%)
    pallas_call x2, Pallas kernels, input_backward(): pl.pallas_call(functools.partial(input_backward_kernel, saved=saved, line...  190 us
    pallas_call x2, Pallas kernels, mixer_backward(): pl.pallas_call(functools.partial(mixer_backward_kernel, saved=saved, head...  94.9 us
    pallas_call x2, Pallas kernels, feed_backward(): pl.pallas_call(functools.partial(feed_backward_kernel, columns=columns, r...  91.2 us
    pallas_call x3, Pallas kernels, mixer_forward(): pl.pallas_call(functools.partial(mixer_forward_kernel, pieces=count, out_...  75.4 us
    ppermute x33, waiting for transfers between devices, moved(): return lax.ppermute(block, AXES, route(change))  60 us
    pallas_call x3, Pallas kernels, feed_forward(): pl.pallas_call(functools.partial(feed_forward_kernel, pieces=pieces, offs...  51.8 us
    ppermute x33, starting transfers between devices, moved(): return lax.ppermute(block, AXES, route(change))  29.4 us
  transfers between devices with their start and end apart: 33, of which 8 were waited for; matrix products, arithmetic and copies ran while one was open for 5% of the time, Pallas kernels for 40%

profile of v3, /device:TPU:3, one launch (start us, length us, event | category | flops | bytes accessed | tf_op | source)
XLA Modules:
  0.0 667.9 jit_solution(3458798427325158544)
XLA Ops:
  0.7 3.0 dynamic-slice_bitcast_fusion.4
  5.1 1.6 collective-permute-start.1
  7.0 2.4 dynamic-slice_bitcast_fusion.1
  9.3 1.4 collective-permute-start.5
  10.7 1.3 fusion
  13.5 19.4 %collective-permute-done.2 = f32[9216]{0:T(1024)S(1)} collective-permute-done((f32[9216]{0:T(1024)S(1)}, f32[9216]{0:T(1024)S(1)}, u32[]{:S(2)}, u32[]{:S(2)}) %collective-permute-start.2) | collective-permute-done | bytes 36896 | tf_op jit(solution)/shard_map/ppermute | solution.py:1261
  33.0 2.7 broadcast_select_fusion.4
  35.7 2.6 collective-permute-start.3
  38.3 1.7 collective-permute-start.4
  40.4 1.4 copy.33.qkv_shift_ref
  42.5 3.3 maximum_select_fusion.hidden_ref
  45.8 18.6 %mixer_forward.3 = (bf16[2,576,1280]{2,1,0:T(8,128)(2,1)}, bf16[2,192,1280]{2,1,0:T(8,128)(2,1)}, f32[8,1,1280]{2,1,0:T(1,128)}, bf16[1280,768]{1,0:T(8,128)(2,1)}) custom-call(s32[3]{0:T(128)} %pad_add_fusion.place_ref, s32[5]{0:T(128)} %get-tuple-element.242.start_ref, s32[5]{0:T(128)} %get-tuple-element.241.tiles_ref, ...), custom_call_target="tpu_custom_call" | custom-call | flops 4000000000 | bytes 1000000 | tf_op jit(solution)/shard_map/mixer_forward/pallas_call | solution.py:338
  64.5 1.9 collective-permute-done.4.rest_0_.rest_6_.rest_13_
  67.1 1.3 dynamic-slice_bitcast_fusion
  68.4 1.6 collective-permute-start.9
  70.0 2.8 broadcast_select_fusion.3
  72.8 1.2 collective-permute-start.7
  75.1 1.0 copy-done.9
  76.1 21.8 %mixer_forward.4 = (bf16[2,576,1280]{2,1,0:T(8,128)(2,1)}, bf16[2,192,1280]{2,1,0:T(8,128)(2,1)}, f32[8,1,1280]{2,1,0:T(1,128)}, f32[1280,768]{1,0:T(8,128)}) custom-call(s32[3]{0:T(128)} %pad_add_fusion.place_ref, s32[5]{0:T(128)} %get-tuple-element.242.start_ref, s32[5]{0:T(128)} %get-tuple-element.241.tiles_ref, s32[1,1280]{1,0:T(1,128)} %get-tuple-element.244.seg_ref, ...), custom_call_target="tpu_custom_call" | custom-call | flops 4000000000 | bytes 1000000 | tf_op jit(solution)/shard_map/mixer_forward/pallas_call | solution.py:338
  98.0 2.4 collective-permute-done.7.rest_0_.rest_10_
  100.4 3.1 broadcast_select_fusion.2
  103.5 1.1 collective-permute-start.10
  104.5 1.2 collective-permute-start.11
  107.8 1.1 copy-done.25
  108.9 14.5 %feed_forward.3 = (f32[1280,768]{1,0:T(8,128)}, bf16[1280,1536]{1,0:T(8,128)(2,1)}, bf16[1280,1536]{1,0:T(8,128)(2,1)}) custom-call(s32[3]{0:T(128)} %pad_add_fusion.place_ref, f32[1280,768]{1,0:T(8,128)} %get-tuple-element.139.middle_ref, f32[2,768]{1,0:T(2,128)} %pad_maximum_fusion.2.norm_ref, f32[4,1,768]{2,1,0:T(1,128)} %bitcast.58, ...), custom_call_target="tpu_custom_call" | custom-call | flops 4000000000 | bytes 1000000 | tf_op jit(solution)/shard_map/feed_forward/pallas_call | solution.py:417
  123.4 9.0 %collective-permute-done.11.rest_2_.rest_14_ = bf16[768,768]{1,0:T(8,128)(2,1)} collective-permute-done((bf16[768,768]{1,0:T(8,128)(2,1)}, bf16[768,768]{1,0:T(8,128)(2,1)}, u32[]{:S(2)}, u32[]{:S(2)}) %collective-permute-start.11) | collective-permute-done | bytes 1179680 | tf_op jit(solution)/shard_map/ppermute | solution.py:1261
  132.5 0.8 collective-permute-start.13
  133.2 1.2 collective-permute-start.14
  134.8 1.3 collective-permute-done.13.rest_3_.rest_15_
  136.1 14.7 %feed_forward.4 = (bf16[1280,768]{1,0:T(8,128)(2,1)}, bf16[1280,1536]{1,0:T(8,128)(2,1)}, bf16[1280,1536]{1,0:T(8,128)(2,1)}) custom-call(s32[3]{0:T(128)} %pad_add_fusion.place_ref, f32[1280,768]{1,0:T(8,128)} %get-tuple-element.139.middle_ref, f32[2,768]{1,0:T(2,128)} %pad_maximum_fusion.2.norm_ref, f32[4,1,768]{2,1,0:T(1,128)} %bitcast.59, ...), custom_call_target="tpu_custom_call" | custom-call | flops 4000000000 | bytes 1000000 | tf_op jit(solution)/shard_map/feed_forward/pallas_call | solution.py:417
  150.8 10.1 %collective-permute-done.14.rest_2_.rest_6_.rest_13_ = bf16[768,768]{1,0:T(8,128)(2,1)} collective-permute-done((bf16[768,768]{1,0:T(8,128)(2,1)S(1)}, bf16[768,768]{1,0:T(8,128)(2,1)}, u32[]{:S(2)}, u32[]{:S(2)}) %collective-permute-start.14) | collective-permute-done | bytes 1179680 | tf_op jit(solution)/shard_map/ppermute | solution.py:1261
  160.9 0.9 collective-permute-start.16
  161.7 1.2 collective-permute-start.17
  164.0 1.4 copy.34.qkv_shift_ref
  166.6 35.0 %mixer_forward.5 = (bf16[4,576,1280]{2,1,0:T(8,128)(2,1)}, bf16[4,192,1280]{2,1,0:T(8,128)(2,1)}, f32[16,1,1280]{2,1,0:T(1,128)}, bf16[1280,768]{1,0:T(8,128)(2,1)}, f32[1280,768]{1,0:T(8,128)}) custom-call(s32[3]{0:T(128)} %pad_add_fusion.place_ref, s32[5]{0:T(128)} %get-tuple-element.242.start_ref, s32[5]{0:T(128)} %get-tuple-element.241.tiles_ref, ...), custom_call_target="tpu_custom_call" | custom-call | flops 4000000000 | bytes 1000000 | tf_op jit(solution)/shard_map/mixer_forward/pallas_call | solution.py:338
  201.6 13.1 %collective-permute-done.19.rest_6_.rest_14_ = bf16[768,768]{1,0:T(8,128)(2,1)} collective-permute-done((bf16[768,768]{1,0:T(8,128)(2,1)S(1)}, bf16[768,768]{1,0:T(8,128)(2,1)}, u32[]{:S(2)}, u32[]{:S(2)}) %collective-permute-start.19) | collective-permute-done | bytes 1179680 | tf_op jit(solution)/shard_map/ppermute | solution.py:1261
  214.7 0.8 collective-permute-start.21
  215.5 2.6 dynamic-slice_bitcast_fusion.5
  218.1 1.2 collective-permute-start.23
  221.2 1.0 copy-done.16
  222.2 22.5 %feed_forward.5 = (bf16[1280,768]{1,0:T(8,128)(2,1)}, bf16[1280,3072]{1,0:T(8,128)(2,1)}, bf16[1280,3072]{1,0:T(8,128)(2,1)}) custom-call(s32[3]{0:T(128)} %pad_add_fusion.place_ref, f32[1280,768]{1,0:T(8,128)} %get-tuple-element.160.middle_ref, f32[2,768]{1,0:T(2,128)} %pad_maximum_fusion.4.norm_ref, f32[4,1,768]{2,1,0:T(1,128)} %bitcast.61, ...), custom_call_target="tpu_custom_call" | custom-call | flops 4000000000 | bytes 1000000 | tf_op jit(solution)/shard_map/feed_forward/pallas_call | solution.py:417
  244.8 1.8 broadcast_select_fusion
  246.6 1.5 constant_dynamic-slice_fusion.2
  248.3 1.4 constant_dynamic-slice_fusion
  249.7 2.4 collective-permute-start.26
  252.1 3.3 maximum_select_fusion.1.grad_ref
  255.4 43.9 %feed_backward.2 = (bf16[768,768]{1,0:T(8,128)(2,1)}, bf16[768,768]{1,0:T(8,128)(2,1)}, bf16[768,768]{1,0:T(8,128)(2,1)}, bf16[768,768]{1,0:T(8,128)(2,1)}, f32[...) custom-call(bf16[1280,768]{1,0:T(8,128)(2,1)} %maximum_select_fusion.1.grad_ref, ...), custom_call_target="tpu_custom_call" | custom-call | flops 16000000000 | bytes 1000000 | tf_op jit(solution)/shard_map/feed_backward/pallas_call | solution.py:720
  299.3 0.9 copy-done.17
  300.8 2.4 collective-permute-start.29
  303.2 3.8 place_states.1
  307.1 47.4 %mixer_backward.2 = (bf16[4,576,1280]{2,1,0:T(8,128)(2,1)}, f32[4,1,576]{2,1,0:T(1,128)}) custom-call(s32[3]{0:T(128)} %pad_add_fusion.place_ref, s32[5]{0:T(128)} %get-tuple-element.242.start_ref, s32[5]{0:T(128)} %get-tuple-element.241.tiles_ref, s32[1,1280]{1,0:T(1,128)} %get-tuple-element.244.seg_ref, f32[1280,768]{1,0:T(8,128)} %get-tuple-element.183.middle_grad_ref, ...), custom_call_target="tpu_custom_call" | custom-call | flops 16000000000 | bytes 1000000 | tf_op jit(solution)/shard_map/mixer_backward/pallas_call | solution.py:794
  354.6 1.0 copy-done.13
  356.3 31.7 %input_backward.2 = (bf16[2,768,768]{2,1,0:T(8,128)(2,1)}, bf16[1280,768]{1,0:T(8,128)(2,1)}, f32[2,768]{1,0:T(2,128)}, bf16[192,768]{1,0:T(8,128)(2,1)}) custom-call(bf16[1280,768]{1,0:T(8,128)(2,1)} %get-tuple-element.152.hidden_ref, f32[1280,768]{1,0:T(8,128)} %get-tuple-element.183.middle_grad_ref, f32[2,768]{1,0:T(2,128)} %pad_maximum_fusion.3.norm_ref, ...), custom_call_target="tpu_custom_call" | custom-call | flops 8000000000 | bytes 1000000 | tf_op jit(solution)/shard_map/input_backward/pallas_call | solution.py:1157
  388.0 47.4 %feed_backward.3 = (bf16[768,768]{1,0:T(8,128)(2,1)}, bf16[768,768]{1,0:T(8,128)(2,1)}, bf16[768,768]{1,0:T(8,128)(2,1)}, bf16[768,768]{1,0:T(8,128)(2,1)}, f32[...) custom-call(bf16[1280,768]{1,0:T(8,128)(2,1)} %get-tuple-element.198.grad_ref.rest_14_, ...), custom_call_target="tpu_custom_call" | custom-call | flops 16000000000 | bytes 1000000 | tf_op jit(solution)/shard_map/feed_backward/pallas_call | solution.py:720
  435.4 1.2 collective-permute-start.30
  436.9 1.2 collective-permute-start.32
  438.1 47.5 %mixer_backward.3 = (bf16[4,576,1280]{2,1,0:T(8,128)(2,1)}, f32[4,1,576]{2,1,0:T(1,128)}) custom-call(s32[3]{0:T(128)} %pad_add_fusion.place_ref, s32[5]{0:T(128)} %get-tuple-element.242.start_ref, s32[5]{0:T(128)} %get-tuple-element.241.tiles_ref, s32[1,1280]{1,0:T(1,128)} %get-tuple-element.244.seg_ref, f32[1280,768]{1,0:T(8,128)} %get-tuple-element.204.middle_grad_ref, ...), custom_call_target="tpu_custom_call" | custom-call | flops 16000000000 | bytes 1000000 | tf_op jit(solution)/shard_map/mixer_backward/pallas_call | solution.py:794
  485.6 2.7 collective-permute-done.32.rest_11_
  488.3 1.0 copy-done.12
  489.3 158.6 %input_backward.3 = (bf16[2,2,768,768]{3,2,1,0:T(8,128)(2,1)}, bf16[2,2,384,768]{3,2,1,0:T(8,128)(2,1)}, bf16[4,640,768]{2,1,0:T(8,128)(2,1)}, f32[16,768]{1,0:T(8,128)}) custom-call(bf16[1280,768]{1,0:T(8,128)(2,1)} %maximum_select_fusion.hidden_ref, f32[1280,768]{1,0:T(8,128)} %get-tuple-element.204.middle_grad_ref, f32[2,768]{1,0:T(2,128)} %pad_maximum_fusion.1.norm_ref, ...), custom_call_target="tpu_custom_call" | custom-call | flops 8000000000 | bytes 1000000 | tf_op jit(solution)/shard_map/input_backward/pallas_call | solution.py:1157
  647.9 1.5 slice_bitcast_fusion.1
  650.1 0.7 slice_bitcast_fusion
  650.8 5.7 widen.1
  657.4 9.5 %unpack.1 = (f32[3,768,384]{2,1,0:T(8,128)}, f32[384,768]{1,0:T(8,128)}, f32[768,1536]{1,0:T(8,128)}, f32[1536,768]{1,0:T(8,128)}) custom-call(bf16[2,2,768,768]{3,2,1,0:T(8,128)(2,1)} %get-tuple-element.231.feed_ref, bf16[2,768,768]{2,1,0:T(8,128)(2,1)} %bitcast.56), custom_call_target="tpu_custom_call" | custom-call | tf_op jit(solution)/shard_map/unpack/pallas_call | solution.py:1235
  (137 shorter events, 16.4 us)
Async XLA Ops:
  0.6 3.1 copy-start
  0.7 3.1 copy-start.19
  3.7 29.2 %collective-permute-start = (bf16[640,768]{1,0:T(8,128)(2,1)}, bf16[640,768]{1,0:T(8,128)(2,1)}, u32[]{:S(2)}, u32[]{:S(2)}) collective-permute-start(bf16[640,768]{1,0:T(8,128)(2,1)} %get-tuple-element.250), channel_id=1, source_target_pairs={{0,1},{1,0},{2,3},{3,2},{4,5},{5,4},{6,7},{7,6},{8,9},{9,8},{10,11... | collective-permute-start | bytes 2949128 | tf_op jit(solution)/shard_map/ppermute | solution.py:1261
  4.3 2.4 copy-start.21
  4.3 2.4 copy-start.22
  4.3 2.4 copy-start.23
  4.3 2.5 copy-start.24
  4.3 2.5 copy-start.20
  5.1 27.8 %collective-permute-start.1 = (bf16[768,768]{1,0:T(8,128)(2,1)S(1)}, bf16[768,768]{1,0:T(8,128)(2,1)}, u32[]{:S(2)}, u32[]{:S(2)}) collective-permute-start(bf16[768,768]{1,0:T(8,128)(2,1)S(1)} %pad_maximum_fusion), channel_id=1, source_target_pairs={{0,16},{1,17},{2,18},{3,19},{4,20},{5,21},{6,22},{7,23},{8,24},{9,... | collective-permute-start | bytes 3538952 | tf_op jit(solution)/shard_map/ppermute | solution.py:1261
  6.9 26.1 %collective-permute-start.2 = (f32[9216]{0:T(1024)S(1)}, f32[9216]{0:T(1024)S(1)}, u32[]{:S(2)}, u32[]{:S(2)}) collective-permute-start(f32[9216]{0:T(1024)S(1)} %constant_dynamic-update-slice_fusion), channel_id=1, source_target_pairs={{0,16},{1,17},{2,18},{3,19},{4,20},{5,21},{6,22},{7,23},{8,24},{9,... | collective-permute-start | bytes 110600 | tf_op jit(solution)/shard_map/ppermute | solution.py:1261
  9.3 55.2 %collective-permute-start.5 = (bf16[768,768]{1,0:T(8,128)(2,1)}, bf16[768,768]{1,0:T(8,128)(2,1)}, u32[]{:S(2)}, u32[]{:S(2)}) collective-permute-start(bf16[768,768]{1,0:T(8,128)(2,1)} %dynamic-slice_bitcast_fusion.1), channel_id=1, source_target_pairs={{0,16},{1,17},{2,18},{3,19},{4,20},{5,21},{6,22},{7,23},{8,24},{9,... | collective-permute-start | bytes 3538952 | tf_op jit(solution)/shard_map/ppermute | solution.py:1261
  35.7 10.1 %copy-start.3 = (bf16[768,768]{1,0:T(8,128)(2,1)}, bf16[768,768]{1,0:T(8,128)(2,1)S(1)}, u32[]{:S(2)}) copy-start(bf16[768,768]{1,0:T(8,128)(2,1)S(1)} %get-tuple-element.256.rest_0_.rest_4_.rest_11_) | copy-start | bytes 3538948
  35.7 6.7 %copy-start.7 = (bf16[640,768]{1,0:T(8,128)(2,1)S(1)}, bf16[640,768]{1,0:T(8,128)(2,1)}, u32[]{:S(2)}) copy-start(bf16[640,768]{1,0:T(8,128)(2,1)} %get-tuple-element.249) | copy-start | bytes 2949124
  35.7 10.1 %collective-permute-start.3 = (bf16[768,768]{1,0:T(8,128)(2,1)S(1)}, bf16[768,768]{1,0:T(8,128)(2,1)}, u32[]{:S(2)}, u32[]{:S(2)}) collective-permute-start(bf16[768,768]{1,0:T(8,128)(2,1)S(1)} %get-tuple-element.256.rest_0_.rest_4_.rest_11_), channel_id=1, source_target_pairs={{0,2},{1,3},{2,0},{3,1},{4,6},{5,7},{6,4},{7,5},{8,10},{9,11},{10,... | collective-permute-start | bytes 3538952 | tf_op jit(solution)/shard_map/ppermute | solution.py:1261
  38.3 28.1 %collective-permute-start.4 = (bf16[768,768]{1,0:T(8,128)(2,1)S(1)}, bf16[768,768]{1,0:T(8,128)(2,1)}, u32[]{:S(2)}, u32[]{:S(2)}) collective-permute-start(bf16[768,768]{1,0:T(8,128)(2,1)S(1)} %get-tuple-element.256.rest_0_.rest_4_.rest_11_), channel_id=1, source_target_pairs={{0,1},{1,0},{2,3},{3,2},{4,5},{5,4},{6,7},{7,6},{8,9},{9,8},{10,11... | collective-permute-start | bytes 3538952 | tf_op jit(solution)/shard_map/ppermute | solution.py:1261
  64.5 5.5 copy-start.8
  66.4 8.7 %collective-permute-start.6 = (bf16[768,768]{1,0:T(8,128)(2,1)}, bf16[768,768]{1,0:T(8,128)(2,1)S(1)}, u32[]{:S(2)}, u32[]{:S(2)}) collective-permute-start(bf16[768,768]{1,0:T(8,128)(2,1)} %collective-permute-done.4.rest_0_.rest_6_.rest_13_), channel_id=1, source_target_pairs={{0,2},{1,3},{2,0},{3,1},{4,6},{5,7},{6,4},{7,5},{8,10},{9,11},{10,... | collective-permute-start | bytes 3538952 | tf_op jit(solution)/shard_map/ppermute | solution.py:1261
  68.4 29.5 %collective-permute-start.9 = (bf16[768,768]{1,0:T(8,128)(2,1)S(1)}, bf16[768,768]{1,0:T(8,128)(2,1)}, u32[]{:S(2)}, u32[]{:S(2)}) collective-permute-start(bf16[768,768]{1,0:T(8,128)(2,1)S(1)} %dynamic-slice_bitcast_fusion), channel_id=1, source_target_pairs={{0,16},{1,17},{2,18},{3,19},{4,20},{5,21},{6,22},{7,23},{8,24},{9,... | collective-permute-start | bytes 3538952 | tf_op jit(solution)/shard_map/ppermute | solution.py:1261
  72.8 90.2 %copy-start.5 = (bf16[768,768]{1,0:T(8,128)(2,1)}, bf16[768,768]{1,0:T(8,128)(2,1)S(1)}, u32[]{:S(2)}) copy-start(bf16[768,768]{1,0:T(8,128)(2,1)S(1)} %get-tuple-element.253.rest_0_.rest_8_) | copy-start | bytes 3538948
  72.8 27.6 %collective-permute-start.7 = (bf16[768,768]{1,0:T(8,128)(2,1)}, bf16[768,768]{1,0:T(8,128)(2,1)}, u32[]{:S(2)}, u32[]{:S(2)}) collective-permute-start(bf16[768,768]{1,0:T(8,128)(2,1)} %get-tuple-element.254.rest_0_.rest_8_), channel_id=1, source_target_pairs={{0,1},{1,0},{2,3},{3,2},{4,5},{5,4},{6,7},{7,6},{8,9},{9,8},{10,11... | collective-permute-start | bytes 3538952 | tf_op jit(solution)/shard_map/ppermute | solution.py:1261
  74.0 26.4 %collective-permute-start.8 = (bf16[768,768]{1,0:T(8,128)(2,1)}, bf16[768,768]{1,0:T(8,128)(2,1)}, u32[]{:S(2)}, u32[]{:S(2)}) collective-permute-start(bf16[768,768]{1,0:T(8,128)(2,1)} %get-tuple-element.254.rest_0_.rest_8_), channel_id=1, source_target_pairs={{0,2},{1,3},{2,0},{3,1},{4,6},{5,7},{6,4},{7,5},{8,10},{9,11},{10,... | collective-permute-start | bytes 3538952 | tf_op jit(solution)/shard_map/ppermute | solution.py:1261
  75.1 1.1 copy-start.9
  103.5 60.0 %copy-start.6 = (bf16[768,768]{1,0:T(8,128)(2,1)}, bf16[768,768]{1,0:T(8,128)(2,1)S(1)}, u32[]{:S(2)}) copy-start(bf16[768,768]{1,0:T(8,128)(2,1)S(1)} %get-tuple-element.251.rest_4_.rest_12_) | copy-start | bytes 3538948
  103.5 4.4 collective-permute-start.10
  104.5 27.9 %collective-permute-start.11 = (bf16[768,768]{1,0:T(8,128)(2,1)}, bf16[768,768]{1,0:T(8,128)(2,1)}, u32[]{:S(2)}, u32[]{:S(2)}) collective-permute-start(bf16[768,768]{1,0:T(8,128)(2,1)} %get-tuple-element.252.rest_2_.rest_12_), channel_id=1, source_target_pairs={{0,1},{1,0},{2,3},{3,2},{4,5},{5,4},{6,7},{7,6},{8,9},{9,8},{10,11... | collective-permute-start | bytes 3538952 | tf_op jit(solution)/shard_map/ppermute | solution.py:1261
  105.7 26.7 %collective-permute-start.12 = (bf16[768,768]{1,0:T(8,128)(2,1)}, bf16[768,768]{1,0:T(8,128)(2,1)}, u32[]{:S(2)}, u32[]{:S(2)}) collective-permute-start(bf16[768,768]{1,0:T(8,128)(2,1)} %collective-permute-done.7.rest_0_.rest_10_), channel_id=1, source_target_pairs={{0,2},{1,3},{2,0},{3,1},{4,6},{5,7},{6,4},{7,5},{8,10},{9,11},{10,... | collective-permute-start | bytes 3538952 | tf_op jit(solution)/shard_map/ppermute | solution.py:1261
  107.8 1.1 copy-start.25
  108.9 24.3 %copy-start.4 = (bf16[768,768]{1,0:T(8,128)(2,1)S(1)}, bf16[768,768]{1,0:T(8,128)(2,1)}, u32[]{:S(2)}) copy-start(bf16[768,768]{1,0:T(8,128)(2,1)} %get-tuple-element.255.rest_0_.rest_4_.rest_11_) | copy-start | bytes 3538948
  132.5 3.6 collective-permute-start.13
  133.2 27.6 %collective-permute-start.14 = (bf16[768,768]{1,0:T(8,128)(2,1)S(1)}, bf16[768,768]{1,0:T(8,128)(2,1)}, u32[]{:S(2)}, u32[]{:S(2)}) collective-permute-start(bf16[768,768]{1,0:T(8,128)(2,1)S(1)} %copy-done.4), channel_id=1, source_target_pairs={{0,1},{1,0},{2,3},{3,2},{4,5},{5,4},{6,7},{7,6},{8,9},{9,8},{10,11... | collective-permute-start | bytes 3538952 | tf_op jit(solution)/shard_map/ppermute | solution.py:1261
  134.5 26.4 %collective-permute-start.15 = (bf16[768,768]{1,0:T(8,128)(2,1)S(1)}, bf16[768,768]{1,0:T(8,128)(2,1)}, u32[]{:S(2)}, u32[]{:S(2)}) collective-permute-start(bf16[768,768]{1,0:T(8,128)(2,1)S(1)} %copy-done.4), channel_id=1, source_target_pairs={{0,2},{1,3},{2,0},{3,1},{4,6},{5,7},{6,4},{7,5},{8,10},{9,11},{10,... | collective-permute-start | bytes 3538952 | tf_op jit(solution)/shard_map/ppermute | solution.py:1261
  160.9 5.7 collective-permute-start.16
  161.7 39.9 %collective-permute-start.17 = (bf16[768,768]{1,0:T(8,128)(2,1)S(1)}, bf16[768,768]{1,0:T(8,128)(2,1)}, u32[]{:S(2)}, u32[]{:S(2)}) collective-permute-start(bf16[768,768]{1,0:T(8,128)(2,1)S(1)} %get-tuple-element.253.rest_0_.rest_8_), channel_id=1, source_target_pairs={{0,1},{1,0},{2,3},{3,2},{4,5},{5,4},{6,7},{7,6},{8,9},{9,8},{10,11... | collective-permute-start | bytes 3538952 | tf_op jit(solution)/shard_map/ppermute | solution.py:1261
  162.9 38.7 %collective-permute-start.18 = (bf16[768,768]{1,0:T(8,128)(2,1)S(1)}, bf16[768,768]{1,0:T(8,128)(2,1)}, u32[]{:S(2)}, u32[]{:S(2)}) collective-permute-start(bf16[768,768]{1,0:T(8,128)(2,1)S(1)} %get-tuple-element.253.rest_0_.rest_8_), channel_id=1, source_target_pairs={{0,2},{1,3},{2,0},{3,1},{4,6},{5,7},{6,4},{7,5},{8,10},{9,11},{10,... | collective-permute-start | bytes 3538952 | tf_op jit(solution)/shard_map/ppermute | solution.py:1261
  163.2 51.5 %collective-permute-start.19 = (bf16[768,768]{1,0:T(8,128)(2,1)S(1)}, bf16[768,768]{1,0:T(8,128)(2,1)}, u32[]{:S(2)}, u32[]{:S(2)}) collective-permute-start(bf16[768,768]{1,0:T(8,128)(2,1)S(1)} %get-tuple-element.251.rest_4_.rest_12_), channel_id=1, source_target_pairs={{0,1},{1,0},{2,3},{3,2},{4,5},{5,4},{6,7},{7,6},{8,9},{9,8},{10,11... | collective-permute-start | bytes 3538952 | tf_op jit(solution)/shard_map/ppermute | solution.py:1261
  163.5 51.2 %collective-permute-start.20 = (bf16[768,768]{1,0:T(8,128)(2,1)S(1)}, bf16[768,768]{1,0:T(8,128)(2,1)}, u32[]{:S(2)}, u32[]{:S(2)}) collective-permute-start(bf16[768,768]{1,0:T(8,128)(2,1)S(1)} %get-tuple-element.251.rest_4_.rest_12_), channel_id=1, source_target_pairs={{0,2},{1,3},{2,0},{3,1},{4,6},{5,7},{6,4},{7,5},{8,10},{9,11},{10,... | collective-permute-start | bytes 3538952 | tf_op jit(solution)/shard_map/ppermute | solution.py:1261
  214.7 6.4 collective-permute-start.21
  215.5 5.6 collective-permute-start.22
  218.1 26.6 %collective-permute-start.23 = (bf16[640,768]{1,0:T(8,128)(2,1)}, bf16[640,768]{1,0:T(8,128)(2,1)}, u32[]{:S(2)}, u32[]{:S(2)}) collective-permute-start(bf16[640,768]{1,0:T(8,128)(2,1)} %get-tuple-element.248), channel_id=1, source_target_pairs={{0,1},{1,0},{2,3},{3,2},{4,5},{5,4},{6,7},{7,6},{8,9},{9,8},{10,11... | collective-permute-start | bytes 2949128 | tf_op jit(solution)/shard_map/ppermute | solution.py:1261
  221.1 1.0 copy-start.16
  222.2 22.6 %copy-start.2 = (bf16[1280,768]{1,0:T(8,128)(2,1)S(1)}, bf16[1280,768]{1,0:T(8,128)(2,1)}, u32[]{:S(2)}) copy-start(bf16[1280,768]{1,0:T(8,128)(2,1)} %get-tuple-element.152.hidden_ref) | copy-start | bytes 5898244
  248.0 51.2 %collective-permute-start.24 = (bf16[640,768]{1,0:T(8,128)(2,1)}, bf16[640,768]{1,0:T(8,128)(2,1)S(1)}, u32[]{:S(2)}, u32[]{:S(2)}) collective-permute-start(bf16[640,768]{1,0:T(8,128)(2,1)} %get-tuple-element.259), channel_id=1, source_target_pairs={{0,1},{1,0},{2,3},{3,2},{4,5},{5,4},{6,7},{7,6},{8,9},{9,8},{10,11... | collective-permute-start | bytes 2949128 | tf_op jit(solution)/shard_map/ppermute | solution.py:1261
  249.6 49.6 %collective-permute-start.25 = (bf16[640,768]{1,0:T(8,128)(2,1)}, bf16[640,768]{1,0:T(8,128)(2,1)S(1)}, u32[]{:S(2)}, u32[]{:S(2)}) collective-permute-start(bf16[640,768]{1,0:T(8,128)(2,1)} %get-tuple-element.258), channel_id=1, source_target_pairs={{0,16},{1,17},{2,18},{3,19},{4,20},{5,21},{6,22},{7,23},{8,24},{9,... | collective-permute-start | bytes 2949128 | tf_op jit(solution)/shard_map/ppermute | solution.py:1261
  249.7 49.6 %collective-permute-start.26 = (bf16[640,768]{1,0:T(8,128)(2,1)}, bf16[640,768]{1,0:T(8,128)(2,1)}, u32[]{:S(2)}, u32[]{:S(2)}) collective-permute-start(bf16[640,768]{1,0:T(8,128)(2,1)} %get-tuple-element.257), channel_id=1, source_target_pairs={{0,17},{1,16},{2,19},{3,18},{4,21},{5,20},{6,23},{7,22},{8,25},{9,... | collective-permute-start | bytes 2949128 | tf_op jit(solution)/shard_map/ppermute | solution.py:1261
  299.3 0.9 copy-start.17
  299.3 1.3 copy-start.18
  300.6 53.9 %collective-permute-start.27 = (bf16[768,768]{1,0:T(8,128)(2,1)}, bf16[768,768]{1,0:T(8,128)(2,1)S(1)}, u32[]{:S(2)}, u32[]{:S(2)}) collective-permute-start(bf16[768,768]{1,0:T(8,128)(2,1)} %get-tuple-element.189), channel_id=1, source_target_pairs={{0,1},{1,0},{2,3},{3,2},{4,5},{5,4},{6,7},{7,6},{8,9},{9,8},{10,11... | collective-permute-start | bytes 3538952 | tf_op jit(solution)/shard_map/ppermute | solution.py:1261
  300.8 53.7 %collective-permute-start.28 = (bf16[768,768]{1,0:T(8,128)(2,1)}, bf16[768,768]{1,0:T(8,128)(2,1)S(1)}, u32[]{:S(2)}, u32[]{:S(2)}) collective-permute-start(bf16[768,768]{1,0:T(8,128)(2,1)} %get-tuple-element.190), channel_id=1, source_target_pairs={{0,16},{1,17},{2,18},{3,19},{4,20},{5,21},{6,22},{7,23},{8,24},{9,... | collective-permute-start | bytes 3538952 | tf_op jit(solution)/shard_map/ppermute | solution.py:1261
  300.8 53.7 %collective-permute-start.29 = (bf16[768,768]{1,0:T(8,128)(2,1)}, bf16[768,768]{1,0:T(8,128)(2,1)S(1)}, u32[]{:S(2)}, u32[]{:S(2)}) collective-permute-start(bf16[768,768]{1,0:T(8,128)(2,1)} %get-tuple-element.191), channel_id=1, source_target_pairs={{0,17},{1,16},{2,19},{3,18},{4,21},{5,20},{6,23},{7,22},{8,25},{9,... | collective-permute-start | bytes 3538952 | tf_op jit(solution)/shard_map/ppermute | solution.py:1261
  354.5 1.0 copy-start.13
  354.5 1.4 copy-start.14
  354.5 1.7 copy-start.15
  435.4 50.2 %collective-permute-start.30 = (bf16[768,768]{1,0:T(8,128)(2,1)}, bf16[768,768]{1,0:T(8,128)(2,1)S(1)}, u32[]{:S(2)}, u32[]{:S(2)}) collective-permute-start(bf16[768,768]{1,0:T(8,128)(2,1)} %get-tuple-element.212), channel_id=1, source_target_pairs={{0,1},{1,0},{2,3},{3,2},{4,5},{5,4},{6,7},{7,6},{8,9},{9,8},{10,11... | collective-permute-start | bytes 3538952 | tf_op jit(solution)/shard_map/ppermute | solution.py:1261
  436.6 48.9 %collective-permute-start.31 = (bf16[768,768]{1,0:T(8,128)(2,1)}, bf16[768,768]{1,0:T(8,128)(2,1)S(1)}, u32[]{:S(2)}, u32[]{:S(2)}) collective-permute-start(bf16[768,768]{1,0:T(8,128)(2,1)} %get-tuple-element.213), channel_id=1, source_target_pairs={{0,16},{1,17},{2,18},{3,19},{4,20},{5,21},{6,22},{7,23},{8,24},{9,... | collective-permute-start | bytes 3538952 | tf_op jit(solution)/shard_map/ppermute | solution.py:1261
  436.9 51.4 %collective-permute-start.32 = (bf16[768,768]{1,0:T(8,128)(2,1)}, bf16[768,768]{1,0:T(8,128)(2,1)S(1)}, u32[]{:S(2)}, u32[]{:S(2)}) collective-permute-start(bf16[768,768]{1,0:T(8,128)(2,1)} %get-tuple-element.214), channel_id=1, source_target_pairs={{0,17},{1,16},{2,19},{3,18},{4,21},{5,20},{6,23},{7,22},{8,25},{9,... | collective-permute-start | bytes 3538952 | tf_op jit(solution)/shard_map/ppermute | solution.py:1261
  485.6 2.7 copy-start.10
  485.6 2.7 copy-start.11
  488.3 1.0 copy-start.12
  657.4 10.2 %copy-start.1 = (bf16[1,3,768,384]{3,2,1,0:T(8,128)(2,1)S(1)}, bf16[1,3,768,384]{3,2,1,0:T(8,128)(2,1)}, u32[]{:S(2)}) copy-start(bf16[1,3,768,384]{3,2,1,0:T(8,128)(2,1)} %param.17) | copy-start | bytes 5308420
